TPU v7x, 32 devices: a whole 2x2x4 slice. The times are simulated.
32 devices in a mesh: dp: 8 (over z, y), mp: 4 (over x, core).
Axes of the slice: x: 2, y: 2, z: 4, core: 2. Of those that a mesh axis runs over, the one named last changes fastest.
Arguments:
- patches: bfloat16 [15360, 128], P(('dp', 'mp')), may hold values from -6 to 6
- row_count: int32 [32], P(('dp', 'mp')), may hold values from 0 to 480, as said below
- target_group: int32 [15360], P(('dp', 'mp')), may hold values from 0 to 7, as said below
- target_offset: int32 [15360], P(('dp', 'mp')), may hold values from 0 to 639, as said below
- embed: bfloat16 [128, 6144], replicated, may hold values from -0.5 to 0.5
- norm_gain: bfloat16 [6144], replicated, may hold values from 0.099609375 to 1.8984375
- readout: bfloat16 [6144, 128], P('mp'), may hold values from -0.078125 to 0.078125
- target: bfloat16 [5120, 128], P('dp'), may hold values from -12 to 12
- master: float32 [6144, 6144], P('dp', 'mp'), may hold values from -6 to 6
- moment1: float32 [6144, 6144], P('dp', 'mp'), may hold values from -2 to 2
- moment2: float32 [6144, 6144], P('dp', 'mp'), may hold values from 0.00086805556 to 0.034722224
Outputs:
- prediction: float32 [5120, 128], P('dp')
- master_new: float32 [6144, 6144], P('dp', 'mp')
- moment1_new: float32 [6144, 6144], P('dp', 'mp')
- moment2_new: float32 [6144, 6144], P('dp', 'mp')
- weight_copy: bfloat16 [6144, 6144], P('dp', 'mp')
Inputs may be any that keep to these rules, and one draw needn't show every extreme that they name: Device i holds its live patch rows in its first row_count[i] slots; some device holds 480 of them in every draw. Over the live slots of all devices, each pair (target_group, target_offset) of the 5120 positions occurs exactly once; values in slots past row_count are arbitrary within the range. Call target_offset // 160 the block of a row. Each (batch, block) receives exactly 160 live rows; one device sends at most 15 live rows to one (batch, block), and every (batch, block) gets 15 rows from some device.
All inputs are finite; a program needn't handle non-finite values.
Results may differ from a plain program's by a relative error of at most 0.03.
Values may be sent and summed in bfloat16 or wider, within the bound.
No kernel may reach another device: no remote copies, remote signals or barrier semaphores. Data moves between devices by JAX's collectives and lax.ppermute only.
A program may use at most 128 MiB of HBM per device.

v0:
```python
import jax
import jax.numpy as jnp
from jax import lax
from jax.sharding import PartitionSpec as P

gelu_const = 0.7978845608028654
beta_one = 0.9
beta_two = 0.95
learn_rate = 0.01
decay_rate = 0.1
adam_epsilon = 1e-08
step_count = 20


def gelu_tanh(value):
    inner = gelu_const * (value + 0.044715 * value * value * value)
    return 0.5 * value * (1.0 + jnp.tanh(inner))


def gelu_slope(value):
    tangent = jnp.tanh(gelu_const * (value + 0.044715 * value * value * value))
    return 0.5 * (1.0 + tangent) + 0.5 * value * (1.0 - tangent * tangent) * gelu_const * (
        1.0 + 3.0 * 0.044715 * value * value
    )


def shards(
    patches,
    row_count,
    target_group,
    target_offset,
    embed,
    norm_gain,
    readout,
    target,
    master,
    moment1,
    moment2,
):
    model_count = lax.axis_size("mp")
    batch_count = lax.axis_size("dp")
    devices_all = batch_count * model_count
    slot_total = patches.shape[0]
    capacity = slot_total // devices_all
    batch_rows = target.shape[0]
    block_rows = batch_rows // model_count
    width = embed.shape[1]
    patch_width = patches.shape[1]
    occupied = jnp.arange(slot_total, dtype=jnp.int32) < row_count[0]
    owner_index = jnp.where(
        occupied, target_group * model_count + target_offset // block_rows, devices_all
    )
    onehot = (owner_index[:, None] == jnp.arange(devices_all, dtype=jnp.int32)[None, :]).astype(
        jnp.int32
    )
    running = jnp.cumsum(onehot, axis=0)
    placing = jnp.sum(onehot * running, axis=1) - 1
    send_slot = jnp.where(occupied, owner_index * capacity + placing, devices_all * capacity)
    outgoing = (
        jnp.zeros((devices_all * capacity, patch_width), jnp.bfloat16)
        .at[send_slot]
        .set(patches, mode="drop")
    )
    slot_marks = (
        jnp.full((devices_all * capacity,), block_rows, jnp.int32)
        .at[send_slot]
        .set(target_offset % block_rows, mode="drop")
    )
    arrived, arrived_marks = (
        lax.all_to_all(outgoing, ("dp", "mp"), split_axis=0, concat_axis=0, tiled=True),
        lax.all_to_all(slot_marks, ("dp", "mp"), split_axis=0, concat_axis=0, tiled=True),
    )
    block_patches = (
        jnp.zeros((block_rows, patch_width), jnp.bfloat16)
        .at[arrived_marks]
        .set(arrived, mode="drop")
    )
    gain_wide = norm_gain.astype(jnp.float32)
    hidden = gelu_tanh(
        jnp.dot(
            lax.all_gather(block_patches, "mp", axis=0, tiled=True),
            embed,
            preferred_element_type=jnp.float32,
        )
    )
    normed = (
        hidden * lax.rsqrt(jnp.mean(hidden * hidden, axis=-1, keepdims=True) + 1e-05) * gain_wide
    ).astype(jnp.bfloat16)
    weight = master.astype(jnp.bfloat16)
    width_scale = 1.0 / width**0.5
    columns = normed
    preact = (
        jnp.dot(
            columns,
            lax.all_gather(weight, "dp", axis=0, tiled=True),
            preferred_element_type=jnp.float32,
        )
        * width_scale
    )
    activation = gelu_tanh(preact).astype(jnp.bfloat16)
    prediction = lax.psum(
        jnp.dot(activation, readout, preferred_element_type=jnp.float32).astype(jnp.bfloat16), "mp"
    ).astype(jnp.float32)
    errors = (prediction - target.astype(jnp.float32)).astype(jnp.bfloat16)
    backward = lax.dot_general(
        errors, readout, (((1,), (1,)), ((), ())), preferred_element_type=jnp.float32
    )
    delta_rows = (backward * gelu_slope(preact)).astype(jnp.bfloat16)
    columns = normed
    gradient = lax.psum_scatter(
        (
            lax.dot_general(
                columns, delta_rows, (((0,), (0,)), ((), ())), preferred_element_type=jnp.float32
            )
            * width_scale
        ).astype(jnp.bfloat16),
        "dp",
        scatter_dimension=0,
        tiled=True,
    ).astype(jnp.float32)
    moment1_new = beta_one * moment1 + (1.0 - beta_one) * gradient
    moment2_new = beta_two * moment2 + (1.0 - beta_two) * gradient * gradient
    first_fix = moment1_new / (1.0 - beta_one**step_count)
    second_fix = moment2_new / (1.0 - beta_two**step_count)
    master_new = master - learn_rate * (
        first_fix / (jnp.sqrt(second_fix) + adam_epsilon) + decay_rate * master
    )
    return (prediction, master_new, moment1_new, moment2_new, master_new.astype(jnp.bfloat16))


def solution(mesh):
    placed = (
        P(("dp", "mp"), None),
        P(("dp", "mp")),
        P(("dp", "mp")),
        P(("dp", "mp")),
        P(),
        P(),
        P("mp", None),
        P("dp", None),
        P("dp", "mp"),
        P("dp", "mp"),
        P("dp", "mp"),
    )
    return jax.shard_map(
        shards,
        mesh=mesh,
        in_specs=placed,
        out_specs=(P("dp", None), P("dp", "mp"), P("dp", "mp"), P("dp", "mp"), P("dp", "mp")),
        check_vma=False,
    )
```

profile of v0, /device:TPU:0, one launch (start us, length us, event | category | flops | bytes accessed | tf_op | source)
XLA Modules:
  0.0 792.7 jit_solution(16259718120482048095)
XLA Ops:
  7.2 0.0 copy-start
  7.2 0.0 copy-start.4
  7.2 0.0 copy-start.5
  7.2 0.0 copy-start.3
  7.2 0.0 all-gather.2.cloned.1.call-start
  7.3 4.1 convert_element_type.40
  11.4 0.0 all-gather.2.cloned.1.call-update
  12.1 0.0 copy-done.4
  12.1 0.0 copy-done.5
  12.1 1.2 reduce-window.6
  13.3 0.2 slice_reduce_fusion
  13.6 0.1 bitcast_bitcast_fusion
  13.7 2.9 scatter_custom_fusion
  16.6 0.7 all_to_all.16
  17.3 7.3 all-to-all-start
  24.6 2.0 scatter_custom_fusion.1
  26.7 0.7 all_to_all.19
  27.4 24.1 %all-to-all-done = s32[32,15,1]{1,2,0:T(1,128)S(1)} async-done(((s32[32,15,1]{1,2,0:T(1,128)}), s32[32,15,1]{1,2,0:T(1,128)S(1)}, u32[]{:S(2)}, u32[]{:S(2)}) %all-to-all-start) | async-done | bytes 1952 | tf_op jit(solution)/shard_map/all_to_all | solution.py:71
  51.5 2.6 all-to-all-start.1
  54.1 0.0 all-reduce.3.cloned.1.call-start
  54.1 0.0 copy-done.3
  54.1 0.5 broadcast.110
  54.7 0.7 reduce.5
  55.4 0.1 all_to_all.18
  55.5 12.7 %all-to-all-done.1 = bf16[32,15,128]{2,1,0:T(8,128)(2,1)S(1)} async-done(((bf16[32,15,128]{2,1,0:T(8,128)(2,1)}), bf16[32,15,128]{2,1,0:T(8,128)(2,1)S(1)}, u32[]{:S(2)}, u32[]{:S(2)}) %all-to-all-start.1) | async-done | bytes 122912 | tf_op jit(solution)/shard_map/all_to_all | solution.py:70
  68.2 0.1 reshape.86
  68.3 1.6 scatter_custom_fusion.2
  69.9 5.7 all_gather.6
  75.6 0.0 copy-done
  75.6 9.0 %multiply_reduce_fusion = (f32[640]{0:T(1024)S(1)}, f32[640,6144]{1,0:T(8,128)}) fusion(bf16[640,128]{1,0:T(8,128)(2,1)S(1)} %all_gather.6, bf16[128,6144]{1,0:T(8,128)(2,1)S(1)} %copy-done), kind=kOutput, calls=%fused_computation.10 | convolution fusion | flops 1045953920 | bytes 17467904 | tf_op jit(solution)/shard_map/dot_general | solution.py:80
  84.6 293.7 %all-gather.2.cloned.1.call-done = bf16[6144,1536]{1,0:T(8,128)(2,1)} async-done(((bf16[768,1536]{1,0:T(8,128)(2,1)}), bf16[6144,1536]{1,0:T(8,128)(2,1)}) %all-gather.2.cloned.1.call-update) | async-done | bytes 18874384 | tf_op jit(solution)/shard_map/all_gather | solution.py:95
  378.3 18.6 %fusion.36 = f32[640,1536]{1,0:T(8,128)S(1)} fusion(bf16[6144,1536]{1,0:T(8,128)(2,1)} %all-gather.2.cloned.1.call-done, f32[640,6144]{1,0:T(8,128)} %get-tuple-element.12, f32[6144]{0:T(1024)S(1)} %convert_element_type.38, f32[640]{0:T(1024)S(1)} %add_rsqrt_fusion), kind=kOutput, calls=%fused_computation.66 | convolution fusion | flops 12091392000 | bytes 38562304 | tf_op jit(solution)/shard_map/dot_general | solution.py:93
  396.9 0.0 copy-start.8
  396.9 1.9 copy-done.8
  398.8 0.0 copy-done.6
  398.8 2.2 fusion.13
  401.0 0.0 all-reduce.3.cloned.1.call-update
  401.0 0.3 reduce-scatter.2.cloned.1.call-start
  401.3 31.4 %all-reduce.3.cloned.1.call-done = bf16[640,128]{1,0:T(8,128)(2,1)} async-done(((bf16[640,128]{1,0:T(8,128)(2,1)}), bf16[640,128]{1,0:T(8,128)(2,1)}) %all-reduce.3.cloned.1.call-update) | async-done | bytes 163856 | tf_op jit(solution)/shard_map/psum | solution.py:101
  432.7 0.9 convert_element_type.43
  433.7 0.0 copy-done.7
  433.7 0.0 copy-start.2
  433.7 27.2 %multiply_convert_fusion = bf16[6144,1536]{1,0:T(8,128)(2,1)} fusion(f32[640,1536]{1,0:T(8,128)} %copy-done.8, bf16[1536,128]{1,0:T(8,128)(2,1)S(1)} %copy-done.6, f32[640,128]{1,0:T(8,128)S(1)} %convert_element_type.43, bf16[640,128]{1,0:T(8,128)(2,1)S(1)} %copy-done.7, f32[640,6144]{1,0:T(8,128)} %get-tuple-element.12, f32[6144]{0:T(1024)S(1)} %convert_element_type.38, ...), kind=kOutput, calls=%fused_computation.3 | convolution fusion | flops 12381831168 | bytes 39447040 | tf_op jit(solution)/shard_map/dot_general | solution.py:112
  460.9 0.0 copy-done.2
  460.9 0.0 reduce-scatter.2.cloned.1.call-update
  460.9 313.5 %reduce-scatter.2.cloned.1.call-done = bf16[768,1536]{1,0:T(8,128)(2,1)} async-done(((bf16[6144,1536]{1,0:T(8,128)(2,1)}), bf16[768,1536]{1,0:T(8,128)(2,1)}) %reduce-scatter.2.cloned.1.call-update) | async-done | bytes 2359312 | tf_op jit(solution)/shard_map/reduce_scatter | solution.py:110
  774.5 11.7 %fusion.37 = (bf16[768,1536]{1,0:T(8,128)(2,1)}, f32[768,1536]{1,0:T(8,128)}, f32[768,1536]{1,0:T(8,128)}, f32[768,1536]{1,0:T(8,128)}) fusion(f32[768,1536]{1,0:T(8,128)} %param.19, bf16[768,1536]{1,0:T(8,128)(2,1)} %reduce-scatter.2.cloned.1.call-done, f32[768,1536]{1,0:T(8,128)} %param.20, f32[768,1536]{1,0:T(8,128)} %param.21), kind=kLoop, calls=%fused_computation.67 | loop fusion | flops 20054016 | bytes 33030144 | tf_op jit(solution)/shard_map/convert_element_type | solution.py:128
  786.2 0.0 copy-done.1
  (13 shorter events, 0.1 us)
Async XLA Ops:
  7.2 68.5 %copy-start = (bf16[128,6144]{1,0:T(8,128)(2,1)S(1)}, bf16[128,6144]{1,0:T(8,128)(2,1)}, u32[]{:S(2)}) copy-start(bf16[128,6144]{1,0:T(8,128)(2,1)} %param.15) | copy-start | bytes 4718596
  7.2 4.9 copy-start.4
  7.2 4.9 copy-start.5
  7.2 46.9 %copy-start.3 = (bf16[6144]{0:T(1024)(128)(2,1)S(1)}, bf16[6144]{0:T(1024)(128)(2,1)}, u32[]{:S(2)}) copy-start(bf16[6144]{0:T(1024)(128)(2,1)} %param.16) | copy-start | bytes 36868
  7.2 371.1 %all-gather.2.cloned.1.call-start = ((), (), s32[]{:S(2)}) async-start(), calls=%async_computation.3 | async-start | bytes 21233664 | tf_op jit(solution)/shard_map/all_gather | solution.py:95
  17.3 34.2 %all-to-all-start = ((s32[32,15,1]{1,2,0:T(1,128)}), s32[32,15,1]{1,2,0:T(1,128)S(1)}, u32[]{:S(2)}, u32[]{:S(2)}) async-start(s32[32,15,1]{1,2,0:T(1,128)} %bitcast.2), calls=%async_computation | async-start | bytes 32768 | tf_op jit(solution)/shard_map/all_to_all | solution.py:71
  51.5 16.7 %all-to-all-start.1 = ((bf16[32,15,128]{2,1,0:T(8,128)(2,1)}), bf16[32,15,128]{2,1,0:T(8,128)(2,1)S(1)}, u32[]{:S(2)}, u32[]{:S(2)}) async-start(bf16[32,15,128]{2,1,0:T(8,128)(2,1)} %all_to_all.19), calls=%async_computation.1 | async-start | bytes 262144 | tf_op jit(solution)/shard_map/all_to_all | solution.py:70
  54.1 378.7 %all-reduce.3.cloned.1.call-start = ((), (), s32[]{:S(2)}) async-start(), calls=%async_computation.4 | async-start | bytes 327680 | tf_op jit(solution)/shard_map/psum | solution.py:101
  378.3 20.5 %copy-start.6 = (bf16[1536,128]{1,0:T(8,128)(2,1)S(1)}, bf16[1536,128]{1,0:T(8,128)(2,1)}, u32[]{:S(2)}) copy-start(bf16[1536,128]{1,0:T(8,128)(2,1)} %param.17) | copy-start | bytes 1179652
  396.9 1.9 copy-start.8
  398.8 34.8 %copy-start.7 = (bf16[640,128]{1,0:T(8,128)(2,1)S(1)}, bf16[640,128]{1,0:T(8,128)(2,1)}, u32[]{:S(2)}) copy-start(bf16[640,128]{1,0:T(8,128)(2,1)} %param.18) | copy-start | bytes 491524
  401.0 373.4 %reduce-scatter.2.cloned.1.call-start = ((), (), s32[]{:S(2)}) async-start(), calls=%async_computation.5 | async-start | bytes 21233664 | tf_op jit(solution)/shard_map/reduce_scatter | solution.py:110
  433.7 27.2 %copy-start.2 = (f32[640,128]{1,0:T(8,128)}, f32[640,128]{1,0:T(8,128)S(1)}, u32[]{:S(2)}) copy-start(f32[640,128]{1,0:T(8,128)S(1)} %convert_element_type.43) | copy-start | bytes 983044
  774.5 11.7 %copy-start.1 = (bf16[128,6144]{1,0:T(8,128)(2,1)S(1)}, bf16[128,6144]{1,0:T(8,128)(2,1)}, u32[]{:S(2)}) copy-start(bf16[128,6144]{1,0:T(8,128)(2,1)} %param.15) | copy-start | bytes 4718596
Sparse Core Ops, SparseCore 0:
  11.5 366.7 all-gather.1
  401.1 31.5 all-reduce.2
  461.1 313.3 reduce-scatter.1
where the time goes:
time: 793 us
  waiting for transfers between devices  676 us (85%)
  matrix products  57 us (7%)
  other arithmetic  18.8 us (2%)
  between operations  14.6 us (2%)
  local copies, waits for them, and re-layouts  10.9 us (1%)
  starting transfers between devices  10.2 us (1%)
    reduce_scatter x1, waiting for transfers between devices, shards(): lax.psum_scatter((lax.dot_general(columns, delta_rows, (((0,), (0,)), (()...  314 us
    all_gather x1, waiting for transfers between devices, shards(): lax.all_gather(weight, 'dp', axis=0, tiled=True)  294 us
    psum x1, waiting for transfers between devices, shards(): lax.psum(jnp.dot(activation, readout, preferred_element_type=jnp.float32)...  31.4 us
    dot_general x1, matrix products, shards(): lax.dot_general(columns, delta_rows, (((0,), (0,)), ((), ())), preferred_...  27.2 us
    all_to_all x1, waiting for transfers between devices, shards(): lax.all_to_all(slot_marks, ('dp', 'mp'), split_axis=0, concat_axis=0, til...  24.1 us
    dot_general x1, matrix products, shards(): jnp.dot(columns, lax.all_gather(weight, 'dp', axis=0, tiled=True), prefer...  18.6 us
  transfers between devices with their start and end apart: 5, of which 5 were waited for; matrix products, arithmetic and copies ran while one was open for 2% of the time, Pallas kernels for 0%

commit v1 on v0

v1 whole, which is shorter than its diff:
```python
import jax
import jax.numpy as jnp
from jax import lax
from jax.experimental import pallas as pl
from jax.experimental.pallas import tpu as pltpu
from jax.sharding import PartitionSpec as P

gelu_const = 0.7978845608028654
beta_one = 0.9
beta_two = 0.95
learn_rate = 0.01
decay_rate = 0.1
adam_epsilon = 1e-08
step_count = 20

line = 4
groups = 2
pieces = 4
streams = 2


def gelu_tanh(value):
    inner = value * (gelu_const + (gelu_const * 0.044715) * (value * value))
    half = 0.5 * value
    return half + half * jnp.tanh(inner)


def gelu_slope(value):
    square = value * value
    tangent = jnp.tanh(value * (gelu_const + (gelu_const * 0.044715) * square))
    return 0.5 * (1.0 + tangent) + value * (1.0 - tangent * tangent) * (
        0.5 * gelu_const + (1.5 * gelu_const * 0.044715) * square
    )


def dot32(left, right):
    return jnp.dot(left, right, preferred_element_type=jnp.float32)


def route(patches, row_count, target_group, target_offset, block_rows):
    model_count, batch_count = lax.axis_size("mp"), lax.axis_size("dp")
    inner = batch_count // line
    devices_all = batch_count * model_count
    columns_all = inner * model_count
    slot_total, patch_width = patches.shape
    capacity = slot_total // devices_all
    lot = capacity + 1
    occupied = jnp.arange(slot_total, dtype=jnp.int32) < row_count[0]
    column = target_group % inner * model_count + target_offset // block_rows
    owner = jnp.where(occupied, column * line + target_group // inner, devices_all)
    onehot = (owner[:, None] == jnp.arange(devices_all, dtype=jnp.int32)[None, :]).astype(
        jnp.int32
    )
    placing = jnp.sum(onehot * jnp.cumsum(onehot, axis=0), axis=1) - 1
    slot = jnp.where(occupied, owner * lot + placing, devices_all * lot)
    spread = (jnp.arange(devices_all * lot, dtype=jnp.int32)[:, None] == slot[None, :]).astype(
        jnp.bfloat16
    )
    rows = dot32(spread, patches).astype(jnp.bfloat16).reshape(devices_all, lot, patch_width)
    lanes = (placing[:, None] == jnp.arange(patch_width, dtype=jnp.int32)[None, :]).astype(
        jnp.bfloat16
    )
    shifted = onehot * (target_offset % block_rows - block_rows)[:, None]
    marks = block_rows + lax.dot_general(
        shifted.astype(jnp.bfloat16),
        lanes,
        (((0,), (0,)), ((), ())),
        preferred_element_type=jnp.float32,
    )
    last = lax.broadcasted_iota(jnp.int32, rows.shape, 1) == capacity
    outgoing = jnp.where(last, marks.astype(jnp.bfloat16)[:, None, :], rows)
    outgoing = outgoing.reshape(1, columns_all, line * lot, patch_width)
    outgoing = jnp.broadcast_to(outgoing, (line,) + outgoing.shape[1:])
    arrived = lax.all_to_all(
        outgoing.reshape(devices_all, line * lot, patch_width),
        ("dp", "mp"),
        split_axis=0,
        concat_axis=0,
        tiled=True,
    )
    places = arrived.reshape(devices_all, line, lot, patch_width)[:, :, capacity, :lot]
    places = places.astype(jnp.int32)
    offsets = jnp.arange(line, dtype=jnp.int32)[None, :, None] * block_rows
    places = jnp.where(places < block_rows, places + offsets, line * block_rows)
    gather = (
        places.reshape(1, devices_all * line * lot)
        == jnp.arange(line * block_rows, dtype=jnp.int32)[:, None]
    ).astype(jnp.bfloat16)
    return dot32(gather, arrived.reshape(devices_all * line * lot, patch_width)).astype(
        jnp.bfloat16
    )


def adam_kernel(own_ref, came_ref, master_ref, moment1_ref, moment2_ref, *refs):
    master_out, moment1_out, moment2_out, copy_out = refs[-4:]
    gradient = own_ref[...] + came_ref[...].astype(jnp.float32)
    moment1_new = beta_one * moment1_ref[...] + (1.0 - beta_one) * gradient
    moment2_new = beta_two * moment2_ref[...] + (1.0 - beta_two) * gradient * gradient
    first_fix = moment1_new / (1.0 - beta_one**step_count)
    second_fix = moment2_new / (1.0 - beta_two**step_count)
    master = master_ref[...]
    master_new = master - learn_rate * (
        first_fix / (jnp.sqrt(second_fix) + adam_epsilon) + decay_rate * master
    )
    master_out[...] = master_new
    moment1_out[...] = moment1_new
    moment2_out[...] = moment2_new
    copy_out[...] = master_new.astype(jnp.bfloat16)


def adam_piece(own, came, state, outs, which):
    depth, cut = own.shape
    tile = depth // 3
    piece = pl.BlockSpec((tile, cut), lambda i: (i, 0))
    column = pl.BlockSpec((tile, cut), lambda i: (i, which))
    whole = [jax.ShapeDtypeStruct(state[0].shape, jnp.float32)] * 3
    whole.append(jax.ShapeDtypeStruct(state[0].shape, jnp.bfloat16))
    outs = outs or []
    return pl.pallas_call(
        adam_kernel,
        grid=(3,),
        in_specs=[piece, piece, column, column, column]
        + [pl.BlockSpec(memory_space=pl.ANY)] * len(outs),
        out_specs=[column] * 4,
        out_shape=whole,
        input_output_aliases={5 + i: i for i in range(len(outs))},
        compiler_params=pltpu.CompilerParams(vmem_limit_bytes=24 * 1024 * 1024),
        cost_estimate=pl.CostEstimate(
            flops=20 * depth * cut, bytes_accessed=32 * depth * cut, transcendentals=depth * cut
        ),
        name="adam_piece",
    )(own, came, *state, *outs)


def shards(
    patches,
    row_count,
    target_group,
    target_offset,
    embed,
    norm_gain,
    readout,
    target,
    master,
    moment1,
    moment2,
):
    model_count, batch_count = lax.axis_size("mp"), lax.axis_size("dp")
    inner = batch_count // line
    place = lax.axis_index("dp") // inner
    inside = lax.axis_index("dp") % inner
    last = line - 1
    at_end = (place == 0) | (place == last)
    far_side = place >= line // 2
    batch_rows = target.shape[0]
    block_rows = batch_rows // model_count
    width = embed.shape[1]
    patch_width = embed.shape[0]
    depth, columns = master.shape
    width_scale = 1.0 / width**0.5

    def swap(value, partners):
        pairs = [
            (p * inner + q, r * inner + q)
            for one, two in partners
            for p, r in ((one, two), (two, one))
            for q in range(inner)
        ]
        return lax.ppermute(value, "dp", pairs)

    def swap_end(value):
        return swap(value, ((0, 1), (last - 1, last)))

    def swap_middle(value):
        return swap(value, ((1, 2),))

    def turn(value, step):
        pairs = [
            (p * inner + q, p * inner + (q + step) % inner)
            for p in range(line)
            for q in range(inner)
        ]
        return lax.ppermute(value, "dp", pairs)

    def mp_sum(value, kind):
        step = 1
        while step < model_count:
            value = value.astype(kind)
            other = lax.ppermute(value, "mp", [(m, m ^ step) for m in range(model_count)])
            value = value.astype(jnp.float32) + other.astype(jnp.float32)
            step *= 2
        return value

    cut = columns // pieces
    lot = pieces // 2
    slices = [slice(piece * cut, (piece + 1) * cut) for piece in range(pieces)]
    weight_own = [
        master[:, first * cut : (first + lot) * cut].astype(jnp.bfloat16)
        for first in range(0, pieces, lot)
    ]
    weight_own[0], patches, target_offset = lax.optimization_barrier(
        (weight_own[0], patches, target_offset)
    )
    weight = []

    def gather_weight():
        rows = weight_own[len(weight)]
        if weight:
            rows, weight[-1] = lax.optimization_barrier((rows, weight[-1]))
        weight.append([rows] + [turn(rows, -step) for step in range(1, inner)])

    def weight_piece(piece):
        cols = slices[piece % lot]
        return jnp.concatenate([rows[:, cols] for rows in weight[piece // lot]], axis=0)

    gather_weight()
    target_other = swap_end(target)

    blocks = route(patches, row_count, target_group, target_offset, block_rows)
    batches = lax.all_gather(blocks.reshape(line, block_rows, -1), "mp", axis=1, tiled=True)
    outbound = [jnp.where(far_side, batches[g], batches[last - g]) for g in range(groups)]
    inbound = [jnp.where(far_side, batches[last - g], batches[g]) for g in range(groups)]

    starts = [(place * inner + (inside + step) % inner) * depth for step in range(inner)]
    embed_here = jnp.concatenate(
        [lax.dynamic_slice_in_dim(embed, start, depth, axis=1) for start in starts], axis=1
    )
    gain_here = jnp.concatenate(
        [lax.dynamic_slice_in_dim(norm_gain, start, depth, axis=0) for start in starts], axis=0
    ).astype(jnp.float32)

    def make_features(tokens):
        return (gelu_tanh(dot32(tokens, embed_here)) * gain_here).astype(jnp.bfloat16)

    def local_scales():
        share = lax.axis_index("mp") * block_rows
        mine = jnp.concatenate(
            [lax.dynamic_slice_in_dim(tokens, share, block_rows, axis=0) for tokens in inbound],
            axis=0,
        )
        hidden = gelu_tanh(dot32(mine, embed))
        return lax.rsqrt(jnp.mean(hidden * hidden, axis=-1) + 1e-05) * width_scale

    def all_scales(scale):
        placed = jnp.zeros((groups, model_count, block_rows), jnp.float32)
        placed = lax.dynamic_update_slice_in_dim(
            placed, scale.reshape(groups, 1, block_rows), lax.axis_index("mp"), axis=1
        )
        placed = mp_sum(placed.reshape(groups, batch_rows), jnp.float32)
        return [placed[g][:, None] for g in range(groups)]

    units = groups * pieces
    goals = [target, target_other]
    rows_each = batch_rows // streams
    parts = [slice(part * rows_each, (part + 1) * rows_each) for part in range(streams)]
    features, scales, predicted, errors = [], [], [], []
    sums, preact, partial, delta = {}, {}, {}, {}
    ends, middles = {}, {}
    whole_parts = {}
    early, pending, outs = {}, {}, None

    def wide(value):
        return value.astype(jnp.float32)

    def group_features(group):
        return make_features(jnp.concatenate([outbound[group], inbound[group]], axis=0))

    def partial_sums(unit):
        group, piece = divmod(unit, pieces)
        right = weight_piece(piece)
        return [
            dot32(features[group][side * batch_rows :][:batch_rows], right).astype(jnp.bfloat16)
            for side in range(2)
        ]

    def finished(part, unit, before):
        group, piece = divmod(unit, pieces)
        value = (wide(sums[unit][1][parts[part]]) + wide(before)) * scales[group][parts[part]]
        active = gelu_tanh(value).astype(jnp.bfloat16)
        return value, dot32(active, readout[slices[piece]])

    def new_delta(part, unit, before):
        group, piece = divmod(unit, pieces)
        back = lax.dot_general(
            lax.optimization_barrier((errors[group][parts[part]], before))[0],
            readout[slices[piece]],
            (((1,), (1,)), ((), ())),
            preferred_element_type=jnp.float32,
        )
        slope = gelu_slope(preact[part, unit])
        return (back * slope * scales[group][parts[part]]).astype(jnp.bfloat16)

    def gradient_term(unit, rows):
        first = units + unit
        arrived = [
            jnp.where(at_end, ends[part, first + 2], middles[part, first + 1])
            for part in range(streams)
        ] + [jnp.where(at_end, delta[part, unit], ends[part, first]) for part in range(streams)]
        return lax.dot_general(
            features[unit // pieces][:, rows],
            jnp.concatenate(arrived, axis=0),
            (((0,), (0,)), ((), ())),
            preferred_element_type=jnp.float32,
        )

    features.append(group_features(0))
    sums[0] = partial_sums(0)
    gather_weight()
    side_work = {
        (0, 0): [1, "scales"],
        (0, streams - 1): ["features"],
        (1, 0): [4, 5],
        (1, streams - 1): [2],
        (2, 0): [3],
        (2, streams - 1): [6, 7],
    }
    for tick, part in [(t, p) for t in range(2 * units + line) for p in range(streams)]:
        back_tick = tick - units
        was_end = was_middle = None
        if tick:
            was_end, was_middle, pending = lax.optimization_barrier(
                (ends.get((part, tick - 1)), middles.get((part, tick - 1)), pending)
            )
            ends[part, tick - 1], middles[part, tick - 1] = was_end, was_middle
            for box, key in list(pending):
                value = pending.pop((box, key))
                if box == "sums":
                    sums[key] = value
                elif box == "preact":
                    preact[key], partial[key] = value
                elif box == "delta":
                    delta[key] = value
                elif box == "early":
                    early[key] = value
                elif box == "features":
                    features.append(value)
                else:
                    scales = all_scales(value)

        from_end = from_middle = None
        if tick < units:
            from_end = sums[tick][0][parts[part]]
        elif back_tick < units:
            from_end = delta[part, back_tick]
        elif back_tick == units:
            narrow = predicted[1][parts[part]].astype(jnp.bfloat16)
            from_end = jnp.pad(narrow, ((0, 0), (0, cut - patch_width)))
        if 2 <= tick < units + 2:
            from_middle = (wide(sums[tick - 2][1][parts[part]]) + wide(was_middle)).astype(jnp.bfloat16)
        elif 2 <= back_tick < units + 2:
            from_middle = was_middle
        if from_end is None or from_middle is None:
            payload = from_middle if from_end is None else from_end
        else:
            payload = jnp.where(at_end, from_end, from_middle)
        if payload is not None:
            ends[part, tick] = swap_end(payload)
        if 1 <= tick < units + 1:
            payload = (wide(sums[tick - 1][0][parts[part]]) + wide(was_end)).astype(jnp.bfloat16)
            middles[part, tick] = swap_middle(payload)
        elif 1 <= back_tick < units + 1:
            middles[part, tick] = swap_middle(was_end)

        for work in side_work.get((tick, part), ()):
            if work == "scales":
                pending["scales", None] = local_scales()
            elif work == "features":
                pending["features", None] = group_features(1)
            else:
                pending["sums", work] = partial_sums(work)

        unit = tick - line + 1
        if 0 <= unit < units:
            group, piece = divmod(unit, pieces)
            value = finished(part, unit, was_end)
            pending["preact", (part, unit)] = value
            if piece == pieces - 1:
                whole = sum(partial[part, unit - back] for back in range(1, pieces)) + value[1]
                whole_parts[part] = whole
                if part == streams - 1:
                    whole = [whole_parts[other] for other in range(streams)]
                    predicted.append(mp_sum(jnp.concatenate(whole, axis=0), jnp.bfloat16))
                    errors.append((predicted[-1] - wide(goals[group])).astype(jnp.bfloat16))

        unit = back_tick + 1
        if 0 <= unit < units:
            pending["delta", (part, unit)] = new_delta(part, unit, was_end)

        unit = back_tick - line + 1
        if 0 <= unit < units and part == streams - 1:
            group, piece = divmod(unit, pieces)
            if group < groups - 1:
                pending["early", (group, piece)] = gradient_term(unit, slice(None))
            else:
                total = None
                for step in [*range(1, inner), 0]:
                    rows = slice(step * depth, (step + 1) * depth)
                    value = gradient_term(unit, rows)
                    for other in range(groups - 1):
                        value += early[other, piece][rows]
                    if step == 0:
                        outs = adam_piece(value, total, (master, moment1, moment2), outs, piece)
                    else:
                        value = turn(value.astype(jnp.bfloat16), step)
                        total = value if total is None else (wide(total) + wide(value)).astype(
                            jnp.bfloat16
                        )

    from_ends = [ends[part, 2 * units][:, :patch_width] for part in range(streams)]
    prediction = jnp.where(at_end, predicted[0], wide(jnp.concatenate(from_ends, axis=0)))
    return (prediction, *outs)


def solution(mesh):
    placed = (
        P(("dp", "mp"), None),
        P(("dp", "mp")),
        P(("dp", "mp")),
        P(("dp", "mp")),
        P(),
        P(),
        P("mp", None),
        P("dp", None),
        P("dp", "mp"),
        P("dp", "mp"),
        P("dp", "mp"),
    )
    return jax.shard_map(
        shards,
        mesh=mesh,
        in_specs=placed,
        out_specs=(P("dp", None), P("dp", "mp"), P("dp", "mp"), P("dp", "mp"), P("dp", "mp")),
        check_vma=False,
    )
```

time: 793 us -> 348 us (0.44)
  waiting for transfers between devices: 676 us -> 91.7 us
  starting transfers between devices: 10.2 us -> 141 us
  Pallas kernels: 0 us -> 11.7 us
  between operations: 14.6 us -> 3.69 us
    reduce_scatter x1 -> x0, waiting for transfers between devices: 314 us -> none  [shards(): lax.psum_scatter((lax.dot_general(columns, delta_rows, (((0,), (0,)), (()...]
    all_gather x1 -> x0, waiting for transfers between devices: 294 us -> none  [shards(): lax.all_gather(weight, 'dp', axis=0, tiled=True)]
    ppermute x0 -> x81, starting transfers between devices: none -> 134 us  [the longest x69 123 us: swap(): return lax.ppermute(value, 'dp', pairs)]
    ppermute x0 -> x81, waiting for transfers between devices: none -> 81 us  [the longest x69 64.1 us: swap(): return lax.ppermute(value, 'dp', pairs)]
    psum x1 -> x0, waiting for transfers between devices: 31.4 us -> none  [shards(): lax.psum(jnp.dot(activation, readout, preferred_element_type=jnp.float32)...]
    all_to_all x2 -> x1, waiting for transfers between devices: 36.8 us -> 10.7 us  [route(): lax.all_to_all(outgoing.reshape(devices_all, line * lot, patch_width), ('...]
    convert_element_type x4 -> x13, other arithmetic: 16.8 us -> 2.91 us  [the longest x8 2.47 us: shards(): (wide(sums[tick - 1][0][parts[part]]) + wide(was_end)).astype(jnp.bfloat16)]
    pallas_call x0 -> x4, Pallas kernels: none -> 11.7 us  [adam_piece(): pl.pallas_call(adam_kernel, grid=(3,), in_specs=[piece, piece, column, co...]
  transfers between devices with their start and end apart: 5 -> 82, of which waited for: 5 -> 26; matrix products, arithmetic and copies ran while one was open for 2% -> 22% of each run, Pallas kernels for 0% -> 3%
where the time goes in v1:
time: 348 us; the launch traced here: 344 us
  starting transfers between devices  141 us (41%)
  waiting for transfers between devices  91.7 us (26%)
  matrix products  62.8 us (18%)
  local copies, waits for them, and re-layouts  13 us (4%)
  other arithmetic  12.4 us (4%)
  Pallas kernels  11.7 us (3%)
  blocking collectives  7.78 us (2%)
  between operations  3.69 us (1%)
    ppermute x69, starting transfers between devices, swap(): return lax.ppermute(value, 'dp', pairs)  123 us
    ppermute x69, waiting for transfers between devices, swap(): return lax.ppermute(value, 'dp', pairs)  64.1 us
    dot_general x37, matrix products, dot32(): return jnp.dot(left, right, preferred_element_type=jnp.float32)  38 us
    dot_general x12, matrix products, gradient_term(): lax.dot_general(features[unit // pieces][:, rows], jnp.concatenate(arrive...  18.9 us
    pallas_call x4, Pallas kernels, adam_piece(): pl.pallas_call(adam_kernel, grid=(3,), in_specs=[piece, piece, column, co...  11.7 us
    ppermute x6, waiting for transfers between devices, turn(): return lax.ppermute(value, 'dp', pairs)  11.5 us
    all_to_all x1, waiting for transfers between devices, route(): lax.all_to_all(outgoing.reshape(devices_all, line * lot, patch_width), ('...  10.7 us
    all_gather x1, blocking collectives, shards(): lax.all_gather(blocks.reshape(line, block_rows, -1), 'mp', axis=1, tiled=...  7.78 us
  transfers between devices with their start and end apart: 82, of which 26 were waited for; matrix products, arithmetic and copies ran while one was open for 22% of the time, Pallas kernels for 3%

profile of v1, /device:TPU:0, one launch (start us, length us, event | category | flops | bytes accessed | tf_op | source)
XLA Modules:
  0.0 344.2 jit_solution(1854399460490719416)
XLA Ops:
  1.4 2.6 convert.26
  8.0 7.3 %all-to-all-start = ((bf16[32,64,128]{2,1,0:T(8,128)(2,1)}), bf16[32,64,128]{2,1,0:T(8,128)(2,1)S(1)}, u32[]{:S(2)}, u32[]{:S(2)}) async-start(bf16[32,64,128]{2,1,0:T(8,128)(2,1)} %bitcast.4), calls=%async_computation | async-start | bytes 1048576 | tf_op jit(solution)/shard_map/all_to_all | solution.py:74
  20.1 10.7 %all-to-all-done = bf16[32,64,128]{2,1,0:T(8,128)(2,1)S(1)} async-done(((bf16[32,64,128]{2,1,0:T(8,128)(2,1)}), bf16[32,64,128]{2,1,0:T(8,128)(2,1)S(1)}, u32[]{:S(2)}, u32[]{:S(2)}) %all-to-all-start) | async-done | bytes 524320 | tf_op jit(solution)/shard_map/all_to_all | solution.py:74
  32.2 7.8 %all_gather.3 = bf16[4,640,128]{2,1,0:T(8,128)(2,1)S(1)} all-gather(bf16[4,160,128]{2,1,0:T(8,128)(2,1)S(1)} %bitcast.67), channel_id=1, replica_groups=mesh['dp'=8,'mp'=4] {'mp'}, dimensions={1}, use_global_device_ids=true | all-gather | bytes 819200 | tf_op jit(solution)/shard_map/all_gather | solution.py:220
  40.0 3.5 %fusion.5 = f32[320]{0:T(512)S(1)} fusion(bf16[128,6144]{1,0:T(8,128)(2,1)S(1)} %copy-done.16, bf16[160,128]{1,0:T(8,128)(2,1)S(1)} %get-tuple-element.441, bf16[160,128]{1,0:T(8,128)(2,1)S(1)} %get-tuple-element.442), kind=kOutput, calls=%fused_computation.8 | convolution fusion | flops 521174720 | bytes 1656064 | tf_op jit(solution)/shard_map/dot_general | solution.py:37
  43.5 2.9 fusion.3
  46.5 2.9 fusion.1
  64.9 8.2 %collective-permute-done.2 = bf16[320,384]{1,0:T(8,128)(2,1)S(1)} collective-permute-done((bf16[320,384]{1,0:T(8,128)(2,1)S(1)}, bf16[320,384]{1,0:T(8,128)(2,1)S(1)}, u32[]{:S(2)}, u32[]{:S(2)}) %collective-permute-start.2) | collective-permute-done | bytes 245792 | tf_op jit(solution)/shard_map/ppermute | solution.py:169
  76.6 3.0 convolution_convert_fusion.11
  85.3 5.3 %collective-permute-start.3 = (bf16[320,384]{1,0:T(8,128)(2,1)S(1)}, bf16[320,384]{1,0:T(8,128)(2,1)S(1)}, u32[]{:S(2)}, u32[]{:S(2)}) collective-permute-start(bf16[320,384]{1,0:T(8,128)(2,1)S(1)} %get-tuple-element.393), channel_id=1, source_target_pairs={{0,8},{4,12},{8,0},{12,4},{16,24},{20,28},{24,16},{28,20},{1,9},{5... | collective-permute-start | bytes 737288 | tf_op jit(solution)/shard_map/ppermute | solution.py:169
  107.9 4.0 %collective-permute-done.10 = bf16[320,384]{1,0:T(8,128)(2,1)S(1)} collective-permute-done((bf16[320,384]{1,0:T(8,128)(2,1)S(1)}, bf16[320,384]{1,0:T(8,128)(2,1)S(1)}, u32[]{:S(2)}, u32[]{:S(2)}) %collective-permute-start.10) | collective-permute-done | bytes 245792 | tf_op jit(solution)/shard_map/ppermute | solution.py:169
  112.3 2.6 collective-permute-done.8
  115.1 4.2 %collective-permute-start.16 = (bf16[320,384]{1,0:T(8,128)(2,1)S(1)}, bf16[320,384]{1,0:T(8,128)(2,1)S(1)}, u32[]{:S(2)}, u32[]{:S(2)}) collective-permute-start(bf16[320,384]{1,0:T(8,128)(2,1)S(1)} %get-tuple-element.365), channel_id=1, source_target_pairs={{0,8},{4,12},{8,0},{12,4},{16,24},{20,28},{24,16},{28,20},{1,9},{5... | collective-permute-start | bytes 737288 | tf_op jit(solution)/shard_map/ppermute | solution.py:169
  120.2 2.3 collective-permute-start.14
  123.5 2.5 collective-permute-done.16
  129.0 3.7 %collective-permute-start.20 = (bf16[320,384]{1,0:T(8,128)(2,1)S(1)}, bf16[320,384]{1,0:T(8,128)(2,1)S(1)}, u32[]{:S(2)}, u32[]{:S(2)}) collective-permute-start(bf16[320,384]{1,0:T(8,128)(2,1)S(1)} %get-tuple-element.363), channel_id=1, source_target_pairs={{0,8},{4,12},{8,0},{12,4},{16,24},{20,28},{24,16},{28,20},{1,9},{5... | collective-permute-start | bytes 737288 | tf_op jit(solution)/shard_map/ppermute | solution.py:169
  141.4 3.7 %collective-permute-start.22 = (bf16[320,384]{1,0:T(8,128)(2,1)S(1)}, bf16[320,384]{1,0:T(8,128)(2,1)S(1)}, u32[]{:S(2)}, u32[]{:S(2)}) collective-permute-start(bf16[320,384]{1,0:T(8,128)(2,1)S(1)} %get-tuple-element.361), channel_id=1, source_target_pairs={{0,8},{4,12},{8,0},{12,4},{16,24},{20,28},{24,16},{28,20},{1,9},{5... | collective-permute-start | bytes 737288 | tf_op jit(solution)/shard_map/ppermute | solution.py:169
  145.8 2.4 collective-permute-start.24
  153.8 3.7 %collective-permute-start.28 = (bf16[320,384]{1,0:T(8,128)(2,1)S(1)}, bf16[320,384]{1,0:T(8,128)(2,1)S(1)}, u32[]{:S(2)}, u32[]{:S(2)}) collective-permute-start(bf16[320,384]{1,0:T(8,128)(2,1)S(1)} %get-tuple-element.359), channel_id=1, source_target_pairs={{0,8},{4,12},{8,0},{12,4},{16,24},{20,28},{24,16},{28,20},{1,9},{5... | collective-permute-start | bytes 737288 | tf_op jit(solution)/shard_map/ppermute | solution.py:169
  161.4 2.9 collective-permute-done.28
  165.7 4.4 %collective-permute-done.27 = bf16[640,128]{1,0:T(8,128)(2,1)S(1)} collective-permute-done((bf16[640,128]{1,0:T(8,128)(2,1)S(1)}, bf16[640,128]{1,0:T(8,128)(2,1)S(1)}, u32[]{:S(2)}, u32[]{:S(2)}) %collective-permute-start.27) | collective-permute-done | bytes 163872 | tf_op jit(solution)/shard_map/ppermute | solution.py:189
  170.6 2.3 collective-permute-done.32
  177.4 9.3 %collective-permute-done.30 = bf16[320,384]{1,0:T(8,128)(2,1)S(1)} collective-permute-done((bf16[320,384]{1,0:T(8,128)(2,1)S(1)}, bf16[320,384]{1,0:T(8,128)(2,1)S(1)}, u32[]{:S(2)}, u32[]{:S(2)}) %collective-permute-start.30) | collective-permute-done | bytes 245792 | tf_op jit(solution)/shard_map/ppermute | solution.py:169
  188.1 4.9 %collective-permute-start.36 = (bf16[320,384]{1,0:T(8,128)(2,1)S(1)}, bf16[320,384]{1,0:T(8,128)(2,1)S(1)}, u32[]{:S(2)}, u32[]{:S(2)}) collective-permute-start(bf16[320,384]{1,0:T(8,128)(2,1)S(1)} %get-tuple-element.377), channel_id=1, source_target_pairs={{0,8},{4,12},{8,0},{12,4},{16,24},{20,28},{24,16},{28,20},{1,9},{5... | collective-permute-start | bytes 737288 | tf_op jit(solution)/shard_map/ppermute | solution.py:169
  194.9 7.8 %collective-permute-done.38 = bf16[320,384]{1,0:T(8,128)(2,1)S(1)} collective-permute-done((bf16[320,384]{1,0:T(8,128)(2,1)S(1)}, bf16[320,384]{1,0:T(8,128)(2,1)S(1)}, u32[]{:S(2)}, u32[]{:S(2)}) %collective-permute-start.38) | collective-permute-done | bytes 245792 | tf_op jit(solution)/shard_map/ppermute | solution.py:169
  205.5 9.6 %collective-permute-start.40 = (bf16[320,384]{1,0:T(8,128)(2,1)S(1)}, bf16[320,384]{1,0:T(8,128)(2,1)S(1)}, u32[]{:S(2)}, u32[]{:S(2)}) collective-permute-start(bf16[320,384]{1,0:T(8,128)(2,1)S(1)} %get-tuple-element.373), channel_id=1, source_target_pairs={{0,8},{4,12},{8,0},{12,4},{16,24},{20,28},{24,16},{28,20},{1,9},{5... | collective-permute-start | bytes 737288 | tf_op jit(solution)/shard_map/ppermute | solution.py:169
  215.6 4.5 %collective-permute-done.40 = bf16[320,384]{1,0:T(8,128)(2,1)S(1)} collective-permute-done((bf16[320,384]{1,0:T(8,128)(2,1)S(1)}, bf16[320,384]{1,0:T(8,128)(2,1)S(1)}, u32[]{:S(2)}, u32[]{:S(2)}) %collective-permute-start.40) | collective-permute-done | bytes 245792 | tf_op jit(solution)/shard_map/ppermute | solution.py:169
  223.6 5.2 %collective-permute-start.49 = (bf16[320,384]{1,0:T(8,128)(2,1)S(1)}, bf16[320,384]{1,0:T(8,128)(2,1)S(1)}, u32[]{:S(2)}, u32[]{:S(2)}) collective-permute-start(bf16[320,384]{1,0:T(8,128)(2,1)S(1)} %broadcast_select_fusion.42), channel_id=1, source_target_pairs={{0,8},{4,12},{8,0},{12,4},{16,24},{20,28},{24,16},{28,20},{1,9},{5... | collective-permute-start | bytes 737288 | tf_op jit(solution)/shard_map/ppermute | solution.py:169
  230.7 3.1 collective-permute-done.49
  235.8 4.6 %collective-permute-start.51 = (bf16[320,384]{1,0:T(8,128)(2,1)S(1)}, bf16[320,384]{1,0:T(8,128)(2,1)S(1)}, u32[]{:S(2)}, u32[]{:S(2)}) collective-permute-start(bf16[320,384]{1,0:T(8,128)(2,1)S(1)} %broadcast_select_fusion.41), channel_id=1, source_target_pairs={{0,8},{4,12},{8,0},{12,4},{16,24},{20,28},{24,16},{28,20},{1,9},{5... | collective-permute-start | bytes 737288 | tf_op jit(solution)/shard_map/ppermute | solution.py:169
  241.7 3.7 %collective-permute-start.55 = (bf16[320,384]{1,0:T(8,128)(2,1)S(1)}, bf16[320,384]{1,0:T(8,128)(2,1)S(1)}, u32[]{:S(2)}, u32[]{:S(2)}) collective-permute-start(bf16[320,384]{1,0:T(8,128)(2,1)S(1)} %broadcast_select_fusion.35), channel_id=1, source_target_pairs={{0,8},{4,12},{8,0},{12,4},{16,24},{20,28},{24,16},{28,20},{1,9},{5... | collective-permute-start | bytes 737288 | tf_op jit(solution)/shard_map/ppermute | solution.py:169
  245.5 2.3 fusion.70
  249.1 3.3 collective-permute-start.53
  253.6 3.1 collective-permute-start.57
  260.1 3.2 collective-permute-start.61
  264.9 3.2 collective-permute-start.59
  268.1 2.3 fusion.86
  271.6 3.2 collective-permute-start.63
  275.9 4.8 %collective-permute-start.69 = (bf16[320,384]{1,0:T(8,128)(2,1)S(1)}, bf16[320,384]{1,0:T(8,128)(2,1)S(1)}, u32[]{:S(2)}, u32[]{:S(2)}) collective-permute-start(bf16[320,384]{1,0:T(8,128)(2,1)S(1)} %broadcast_select_fusion.17), channel_id=1, source_target_pairs={{0,8},{4,12},{8,0},{12,4},{16,24},{20,28},{24,16},{28,20},{1,9},{5... | collective-permute-start | bytes 737288 | tf_op jit(solution)/shard_map/ppermute | solution.py:169
  280.8 2.3 fusion.94
  286.7 5.1 %collective-permute-start.71 = (bf16[320,384]{1,0:T(8,128)(2,1)S(1)}, bf16[320,384]{1,0:T(8,128)(2,1)S(1)}, u32[]{:S(2)}, u32[]{:S(2)}) collective-permute-start(bf16[320,384]{1,0:T(8,128)(2,1)S(1)} %broadcast_select_fusion.16), channel_id=1, source_target_pairs={{0,8},{4,12},{8,0},{12,4},{16,24},{20,28},{24,16},{28,20},{1,9},{5... | collective-permute-start | bytes 737288 | tf_op jit(solution)/shard_map/ppermute | solution.py:169
  298.0 5.7 %collective-permute-start.73 = (bf16[320,384]{1,0:T(8,128)(2,1)S(1)}, bf16[320,384]{1,0:T(8,128)(2,1)S(1)}, u32[]{:S(2)}, u32[]{:S(2)}) collective-permute-start(bf16[320,384]{1,0:T(8,128)(2,1)S(1)} %pad_select_fusion), channel_id=1, source_target_pairs={{0,8},{4,12},{8,0},{12,4},{16,24},{20,28},{24,16},{28,20},{1,9},{5... | collective-permute-start | bytes 737288 | tf_op jit(solution)/shard_map/ppermute | solution.py:169
  319.4 2.9 adam_piece.4
  323.6 2.9 adam_piece.5
  326.5 8.0 %collective-permute-done.78.came_ref = bf16[768,384]{1,0:T(8,128)(2,1)S(1)} collective-permute-done((bf16[768,384]{1,0:T(8,128)(2,1)S(1)}, bf16[768,384]{1,0:T(8,128)(2,1)S(1)}, u32[]{:S(2)}, u32[]{:S(2)}) %collective-permute-start.78) | collective-permute-done | bytes 589856 | tf_op jit(solution)/shard_map/ppermute | solution.py:183
  334.6 2.9 adam_piece.6
  337.5 3.4 collective-permute-done.77.came_ref
  340.9 2.9 adam_piece.7
  (372 shorter events, 133.1 us)
Async XLA Ops:
  8.0 22.9 %all-to-all-start = ((bf16[32,64,128]{2,1,0:T(8,128)(2,1)}), bf16[32,64,128]{2,1,0:T(8,128)(2,1)S(1)}, u32[]{:S(2)}, u32[]{:S(2)}) async-start(bf16[32,64,128]{2,1,0:T(8,128)(2,1)} %bitcast.4), calls=%async_computation | async-start | bytes 1048576 | tf_op jit(solution)/shard_map/all_to_all | solution.py:74
  15.3 34.1 %collective-permute-start = (bf16[768,768]{1,0:T(8,128)(2,1)S(1)}, bf16[768,768]{1,0:T(8,128)(2,1)}, u32[]{:S(2)}, u32[]{:S(2)}) collective-permute-start(bf16[768,768]{1,0:T(8,128)(2,1)S(1)} %get-tuple-element.176), channel_id=1, source_target_pairs={{0,4},{4,0},{8,12},{12,8},{16,20},{20,16},{24,28},{28,24},{1,5},{5... | collective-permute-start | bytes 3538952 | tf_op jit(solution)/shard_map/ppermute | solution.py:183
  54.1 38.8 %collective-permute-start.5 = (bf16[768,768]{1,0:T(8,128)(2,1)S(1)}, bf16[768,768]{1,0:T(8,128)(2,1)}, u32[]{:S(2)}, u32[]{:S(2)}) collective-permute-start(bf16[768,768]{1,0:T(8,128)(2,1)S(1)} %get-tuple-element.182), channel_id=1, source_target_pairs={{0,4},{4,0},{8,12},{12,8},{16,20},{20,16},{24,28},{28,24},{1,5},{5... | collective-permute-start | bytes 3538952 | tf_op jit(solution)/shard_map/ppermute | solution.py:183
  59.7 21.3 %collective-permute-start.1 = (bf16[320,384]{1,0:T(8,128)(2,1)}, bf16[320,384]{1,0:T(8,128)(2,1)}, u32[]{:S(2)}, u32[]{:S(2)}) collective-permute-start(bf16[320,384]{1,0:T(8,128)(2,1)} %get-tuple-element.395), channel_id=1, source_target_pairs={{0,8},{4,12},{8,0},{12,4},{16,24},{20,28},{24,16},{28,20},{1,9},{5... | collective-permute-start | bytes 737288 | tf_op jit(solution)/shard_map/ppermute | solution.py:169
  60.4 12.7 %collective-permute-start.2 = (bf16[320,384]{1,0:T(8,128)(2,1)S(1)}, bf16[320,384]{1,0:T(8,128)(2,1)S(1)}, u32[]{:S(2)}, u32[]{:S(2)}) collective-permute-start(bf16[320,384]{1,0:T(8,128)(2,1)S(1)} %get-tuple-element.396), channel_id=1, source_target_pairs={{0,8},{4,12},{8,0},{12,4},{16,24},{20,28},{24,16},{28,20},{1,9},{5... | collective-permute-start | bytes 737288 | tf_op jit(solution)/shard_map/ppermute | solution.py:169
  82.3 19.2 %collective-permute-start.4 = (bf16[320,384]{1,0:T(8,128)(2,1)S(1)}, bf16[320,384]{1,0:T(8,128)(2,1)S(1)}, u32[]{:S(2)}, u32[]{:S(2)}) collective-permute-start(bf16[320,384]{1,0:T(8,128)(2,1)S(1)} %get-tuple-element.391), channel_id=1, source_target_pairs={{8,16},{12,20},{16,8},{20,12},{9,17},{13,21},{17,9},{21,13},{10,18... | collective-permute-start | bytes 737288 | tf_op jit(solution)/shard_map/ppermute | solution.py:169
  83.1 19.6 %collective-permute-start.7 = (bf16[320,384]{1,0:T(8,128)(2,1)S(1)}, bf16[320,384]{1,0:T(8,128)(2,1)S(1)}, u32[]{:S(2)}, u32[]{:S(2)}) collective-permute-start(bf16[320,384]{1,0:T(8,128)(2,1)S(1)} %get-tuple-element.392), channel_id=1, source_target_pairs={{8,16},{12,20},{16,8},{20,12},{9,17},{13,21},{17,9},{21,13},{10,18... | collective-permute-start | bytes 737288 | tf_op jit(solution)/shard_map/ppermute | solution.py:169
  85.3 16.2 %collective-permute-start.3 = (bf16[320,384]{1,0:T(8,128)(2,1)S(1)}, bf16[320,384]{1,0:T(8,128)(2,1)S(1)}, u32[]{:S(2)}, u32[]{:S(2)}) collective-permute-start(bf16[320,384]{1,0:T(8,128)(2,1)S(1)} %get-tuple-element.393), channel_id=1, source_target_pairs={{0,8},{4,12},{8,0},{12,4},{16,24},{20,28},{24,16},{28,20},{1,9},{5... | collective-permute-start | bytes 737288 | tf_op jit(solution)/shard_map/ppermute | solution.py:169
  90.6 12.1 %collective-permute-start.6 = (bf16[320,384]{1,0:T(8,128)(2,1)S(1)}, bf16[320,384]{1,0:T(8,128)(2,1)S(1)}, u32[]{:S(2)}, u32[]{:S(2)}) collective-permute-start(bf16[320,384]{1,0:T(8,128)(2,1)S(1)} %get-tuple-element.394), channel_id=1, source_target_pairs={{0,8},{4,12},{8,0},{12,4},{16,24},{20,28},{24,16},{28,20},{1,9},{5... | collective-permute-start | bytes 737288 | tf_op jit(solution)/shard_map/ppermute | solution.py:169
  103.7 11.2 %collective-permute-start.8 = (bf16[320,384]{1,0:T(8,128)(2,1)S(1)}, bf16[320,384]{1,0:T(8,128)(2,1)S(1)}, u32[]{:S(2)}, u32[]{:S(2)}) collective-permute-start(bf16[320,384]{1,0:T(8,128)(2,1)S(1)} %get-tuple-element.368), channel_id=1, source_target_pairs={{0,8},{4,12},{8,0},{12,4},{16,24},{20,28},{24,16},{28,20},{1,9},{5... | collective-permute-start | bytes 737288 | tf_op jit(solution)/shard_map/ppermute | solution.py:169
  115.1 10.9 %collective-permute-start.16 = (bf16[320,384]{1,0:T(8,128)(2,1)S(1)}, bf16[320,384]{1,0:T(8,128)(2,1)S(1)}, u32[]{:S(2)}, u32[]{:S(2)}) collective-permute-start(bf16[320,384]{1,0:T(8,128)(2,1)S(1)} %get-tuple-element.365), channel_id=1, source_target_pairs={{0,8},{4,12},{8,0},{12,4},{16,24},{20,28},{24,16},{28,20},{1,9},{5... | collective-permute-start | bytes 737288 | tf_op jit(solution)/shard_map/ppermute | solution.py:169
  158.2 77.7 %collective-permute-start.48 = (bf16[640,128]{1,0:T(8,128)(2,1)S(1)}, bf16[640,128]{1,0:T(8,128)(2,1)S(1)}, u32[]{:S(2)}, u32[]{:S(2)}) collective-permute-start(bf16[640,128]{1,0:T(8,128)(2,1)S(1)} %copy-done.15), channel_id=1, source_target_pairs={{0,8},{4,12},{8,0},{12,4},{16,24},{20,28},{24,16},{28,20},{1,9},{5... | collective-permute-start | bytes 491528 | tf_op jit(solution)/shard_map/ppermute | solution.py:169
  160.4 12.5 %collective-permute-start.32 = (bf16[320,384]{1,0:T(8,128)(2,1)S(1)}, bf16[320,384]{1,0:T(8,128)(2,1)S(1)}, u32[]{:S(2)}, u32[]{:S(2)}) collective-permute-start(bf16[320,384]{1,0:T(8,128)(2,1)S(1)} %get-tuple-element.360), channel_id=1, source_target_pairs={{0,8},{4,12},{8,0},{12,4},{16,24},{20,28},{24,16},{28,20},{1,9},{5... | collective-permute-start | bytes 737288 | tf_op jit(solution)/shard_map/ppermute | solution.py:169
  160.5 12.4 %collective-permute-start.33 = (bf16[320,384]{1,0:T(8,128)(2,1)S(1)}, bf16[320,384]{1,0:T(8,128)(2,1)S(1)}, u32[]{:S(2)}, u32[]{:S(2)}) collective-permute-start(bf16[320,384]{1,0:T(8,128)(2,1)S(1)} %get-tuple-element.382), channel_id=1, source_target_pairs={{8,16},{12,20},{16,8},{20,12},{9,17},{13,21},{17,9},{21,13},{10,18... | collective-permute-start | bytes 737288 | tf_op jit(solution)/shard_map/ppermute | solution.py:169
  173.6 13.9 %collective-permute-start.34 = (bf16[320,384]{1,0:T(8,128)(2,1)S(1)}, bf16[320,384]{1,0:T(8,128)(2,1)S(1)}, u32[]{:S(2)}, u32[]{:S(2)}) collective-permute-start(bf16[320,384]{1,0:T(8,128)(2,1)S(1)} %get-tuple-element.357), channel_id=1, source_target_pairs={{0,8},{4,12},{8,0},{12,4},{16,24},{20,28},{24,16},{28,20},{1,9},{5... | collective-permute-start | bytes 737288 | tf_op jit(solution)/shard_map/ppermute | solution.py:169
  175.4 11.3 %collective-permute-start.30 = (bf16[320,384]{1,0:T(8,128)(2,1)S(1)}, bf16[320,384]{1,0:T(8,128)(2,1)S(1)}, u32[]{:S(2)}, u32[]{:S(2)}) collective-permute-start(bf16[320,384]{1,0:T(8,128)(2,1)S(1)} %get-tuple-element.358), channel_id=1, source_target_pairs={{0,8},{4,12},{8,0},{12,4},{16,24},{20,28},{24,16},{28,20},{1,9},{5... | collective-permute-start | bytes 737288 | tf_op jit(solution)/shard_map/ppermute | solution.py:169
  175.6 11.8 %collective-permute-start.35 = (bf16[320,384]{1,0:T(8,128)(2,1)S(1)}, bf16[320,384]{1,0:T(8,128)(2,1)S(1)}, u32[]{:S(2)}, u32[]{:S(2)}) collective-permute-start(bf16[320,384]{1,0:T(8,128)(2,1)S(1)} %get-tuple-element.379), channel_id=1, source_target_pairs={{8,16},{12,20},{16,8},{20,12},{9,17},{13,21},{17,9},{21,13},{10,18... | collective-permute-start | bytes 737288 | tf_op jit(solution)/shard_map/ppermute | solution.py:169
  188.1 16.1 %collective-permute-start.36 = (bf16[320,384]{1,0:T(8,128)(2,1)S(1)}, bf16[320,384]{1,0:T(8,128)(2,1)S(1)}, u32[]{:S(2)}, u32[]{:S(2)}) collective-permute-start(bf16[320,384]{1,0:T(8,128)(2,1)S(1)} %get-tuple-element.377), channel_id=1, source_target_pairs={{0,8},{4,12},{8,0},{12,4},{16,24},{20,28},{24,16},{28,20},{1,9},{5... | collective-permute-start | bytes 737288 | tf_op jit(solution)/shard_map/ppermute | solution.py:169
  193.1 11.0 %collective-permute-start.37 = (bf16[320,384]{1,0:T(8,128)(2,1)S(1)}, bf16[320,384]{1,0:T(8,128)(2,1)S(1)}, u32[]{:S(2)}, u32[]{:S(2)}) collective-permute-start(bf16[320,384]{1,0:T(8,128)(2,1)S(1)} %get-tuple-element.375), channel_id=1, source_target_pairs={{8,16},{12,20},{16,8},{20,12},{9,17},{13,21},{17,9},{21,13},{10,18... | collective-permute-start | bytes 737288 | tf_op jit(solution)/shard_map/ppermute | solution.py:169
  202.7 12.9 %collective-permute-start.41 = (bf16[320,384]{1,0:T(8,128)(2,1)S(1)}, bf16[320,384]{1,0:T(8,128)(2,1)S(1)}, u32[]{:S(2)}, u32[]{:S(2)}) collective-permute-start(bf16[320,384]{1,0:T(8,128)(2,1)S(1)} %collective-permute-done.38), channel_id=1, source_target_pairs={{8,16},{12,20},{16,8},{20,12},{9,17},{13,21},{17,9},{21,13},{10,18... | collective-permute-start | bytes 737288 | tf_op jit(solution)/shard_map/ppermute | solution.py:169
  204.4 18.4 %collective-permute-start.43 = (bf16[320,384]{1,0:T(8,128)(2,1)S(1)}, bf16[320,384]{1,0:T(8,128)(2,1)S(1)}, u32[]{:S(2)}, u32[]{:S(2)}) collective-permute-start(bf16[320,384]{1,0:T(8,128)(2,1)S(1)} %collective-permute-done.36), channel_id=1, source_target_pairs={{8,16},{12,20},{16,8},{20,12},{9,17},{13,21},{17,9},{21,13},{10,18... | collective-permute-start | bytes 737288 | tf_op jit(solution)/shard_map/ppermute | solution.py:169
  205.5 14.6 %collective-permute-start.40 = (bf16[320,384]{1,0:T(8,128)(2,1)S(1)}, bf16[320,384]{1,0:T(8,128)(2,1)S(1)}, u32[]{:S(2)}, u32[]{:S(2)}) collective-permute-start(bf16[320,384]{1,0:T(8,128)(2,1)S(1)} %get-tuple-element.373), channel_id=1, source_target_pairs={{0,8},{4,12},{8,0},{12,4},{16,24},{20,28},{24,16},{28,20},{1,9},{5... | collective-permute-start | bytes 737288 | tf_op jit(solution)/shard_map/ppermute | solution.py:169
  220.1 14.9 %collective-permute-start.50 = (bf16[320,384]{1,0:T(8,128)(2,1)S(1)}, bf16[320,384]{1,0:T(8,128)(2,1)S(1)}, u32[]{:S(2)}, u32[]{:S(2)}) collective-permute-start(bf16[320,384]{1,0:T(8,128)(2,1)S(1)} %collective-permute-done.40), channel_id=1, source_target_pairs={{8,16},{12,20},{16,8},{20,12},{9,17},{13,21},{17,9},{21,13},{10,18... | collective-permute-start | bytes 737288 | tf_op jit(solution)/shard_map/ppermute | solution.py:169
  222.9 18.0 %collective-permute-start.47 = (bf16[320,384]{1,0:T(8,128)(2,1)S(1)}, bf16[320,384]{1,0:T(8,128)(2,1)S(1)}, u32[]{:S(2)}, u32[]{:S(2)}) collective-permute-start(bf16[320,384]{1,0:T(8,128)(2,1)S(1)} %collective-permute-done.42), channel_id=1, source_target_pairs={{8,16},{12,20},{16,8},{20,12},{9,17},{13,21},{17,9},{21,13},{10,18... | collective-permute-start | bytes 737288 | tf_op jit(solution)/shard_map/ppermute | solution.py:169
  235.1 13.0 %collective-permute-start.52 = (bf16[320,384]{1,0:T(8,128)(2,1)S(1)}, bf16[320,384]{1,0:T(8,128)(2,1)S(1)}, u32[]{:S(2)}, u32[]{:S(2)}) collective-permute-start(bf16[320,384]{1,0:T(8,128)(2,1)S(1)} %collective-permute-done.49), channel_id=1, source_target_pairs={{8,16},{12,20},{16,8},{20,12},{9,17},{13,21},{17,9},{21,13},{10,18... | collective-permute-start | bytes 737288 | tf_op jit(solution)/shard_map/ppermute | solution.py:169
  235.8 12.3 %collective-permute-start.51 = (bf16[320,384]{1,0:T(8,128)(2,1)S(1)}, bf16[320,384]{1,0:T(8,128)(2,1)S(1)}, u32[]{:S(2)}, u32[]{:S(2)}) collective-permute-start(bf16[320,384]{1,0:T(8,128)(2,1)S(1)} %broadcast_select_fusion.41), channel_id=1, source_target_pairs={{0,8},{4,12},{8,0},{12,4},{16,24},{20,28},{24,16},{28,20},{1,9},{5... | collective-permute-start | bytes 737288 | tf_op jit(solution)/shard_map/ppermute | solution.py:169
  241.0 11.8 %collective-permute-start.56 = (bf16[320,384]{1,0:T(8,128)(2,1)S(1)}, bf16[320,384]{1,0:T(8,128)(2,1)S(1)}, u32[]{:S(2)}, u32[]{:S(2)}) collective-permute-start(bf16[320,384]{1,0:T(8,128)(2,1)S(1)} %collective-permute-done.46), channel_id=1, source_target_pairs={{8,16},{12,20},{16,8},{20,12},{9,17},{13,21},{17,9},{21,13},{10,18... | collective-permute-start | bytes 737288 | tf_op jit(solution)/shard_map/ppermute | solution.py:169
  241.7 11.1 %collective-permute-start.55 = (bf16[320,384]{1,0:T(8,128)(2,1)S(1)}, bf16[320,384]{1,0:T(8,128)(2,1)S(1)}, u32[]{:S(2)}, u32[]{:S(2)}) collective-permute-start(bf16[320,384]{1,0:T(8,128)(2,1)S(1)} %broadcast_select_fusion.35), channel_id=1, source_target_pairs={{0,8},{4,12},{8,0},{12,4},{16,24},{20,28},{24,16},{28,20},{1,9},{5... | collective-permute-start | bytes 737288 | tf_op jit(solution)/shard_map/ppermute | solution.py:169
  248.2 11.1 %collective-permute-start.54 = (bf16[320,384]{1,0:T(8,128)(2,1)S(1)}, bf16[320,384]{1,0:T(8,128)(2,1)S(1)}, u32[]{:S(2)}, u32[]{:S(2)}) collective-permute-start(bf16[320,384]{1,0:T(8,128)(2,1)S(1)} %collective-permute-done.51), channel_id=1, source_target_pairs={{8,16},{12,20},{16,8},{20,12},{9,17},{13,21},{17,9},{21,13},{10,18... | collective-permute-start | bytes 737288 | tf_op jit(solution)/shard_map/ppermute | solution.py:169
  252.9 11.2 %collective-permute-start.58 = (bf16[320,384]{1,0:T(8,128)(2,1)S(1)}, bf16[320,384]{1,0:T(8,128)(2,1)S(1)}, u32[]{:S(2)}, u32[]{:S(2)}) collective-permute-start(bf16[320,384]{1,0:T(8,128)(2,1)S(1)} %collective-permute-done.55), channel_id=1, source_target_pairs={{8,16},{12,20},{16,8},{20,12},{9,17},{13,21},{17,9},{21,13},{10,18... | collective-permute-start | bytes 737288 | tf_op jit(solution)/shard_map/ppermute | solution.py:169
  253.6 10.5 %collective-permute-start.57 = (bf16[320,384]{1,0:T(8,128)(2,1)S(1)}, bf16[320,384]{1,0:T(8,128)(2,1)S(1)}, u32[]{:S(2)}, u32[]{:S(2)}) collective-permute-start(bf16[320,384]{1,0:T(8,128)(2,1)S(1)} %broadcast_select_fusion.30), channel_id=1, source_target_pairs={{0,8},{4,12},{8,0},{12,4},{16,24},{20,28},{24,16},{28,20},{1,9},{5... | collective-permute-start | bytes 737288 | tf_op jit(solution)/shard_map/ppermute | solution.py:169
  259.4 11.4 %collective-permute-start.62 = (bf16[320,384]{1,0:T(8,128)(2,1)S(1)}, bf16[320,384]{1,0:T(8,128)(2,1)S(1)}, u32[]{:S(2)}, u32[]{:S(2)}) collective-permute-start(bf16[320,384]{1,0:T(8,128)(2,1)S(1)} %collective-permute-done.53), channel_id=1, source_target_pairs={{8,16},{12,20},{16,8},{20,12},{9,17},{13,21},{17,9},{21,13},{10,18... | collective-permute-start | bytes 737288 | tf_op jit(solution)/shard_map/ppermute | solution.py:169
  260.1 10.6 %collective-permute-start.61 = (bf16[320,384]{1,0:T(8,128)(2,1)S(1)}, bf16[320,384]{1,0:T(8,128)(2,1)S(1)}, u32[]{:S(2)}, u32[]{:S(2)}) collective-permute-start(bf16[320,384]{1,0:T(8,128)(2,1)S(1)} %broadcast_select_fusion.28), channel_id=1, source_target_pairs={{0,8},{4,12},{8,0},{12,4},{16,24},{20,28},{24,16},{28,20},{1,9},{5... | collective-permute-start | bytes 737288 | tf_op jit(solution)/shard_map/ppermute | solution.py:169
  264.2 10.9 %collective-permute-start.60 = (bf16[320,384]{1,0:T(8,128)(2,1)S(1)}, bf16[320,384]{1,0:T(8,128)(2,1)S(1)}, u32[]{:S(2)}, u32[]{:S(2)}) collective-permute-start(bf16[320,384]{1,0:T(8,128)(2,1)S(1)} %collective-permute-done.57), channel_id=1, source_target_pairs={{8,16},{12,20},{16,8},{20,12},{9,17},{13,21},{17,9},{21,13},{10,18... | collective-permute-start | bytes 737288 | tf_op jit(solution)/shard_map/ppermute | solution.py:169
  270.9 12.6 %collective-permute-start.64 = (bf16[320,384]{1,0:T(8,128)(2,1)S(1)}, bf16[320,384]{1,0:T(8,128)(2,1)S(1)}, u32[]{:S(2)}, u32[]{:S(2)}) collective-permute-start(bf16[320,384]{1,0:T(8,128)(2,1)S(1)} %collective-permute-done.61), channel_id=1, source_target_pairs={{8,16},{12,20},{16,8},{20,12},{9,17},{13,21},{17,9},{21,13},{10,18... | collective-permute-start | bytes 737288 | tf_op jit(solution)/shard_map/ppermute | solution.py:169
  271.6 11.9 %collective-permute-start.63 = (bf16[320,384]{1,0:T(8,128)(2,1)S(1)}, bf16[320,384]{1,0:T(8,128)(2,1)S(1)}, u32[]{:S(2)}, u32[]{:S(2)}) collective-permute-start(bf16[320,384]{1,0:T(8,128)(2,1)S(1)} %broadcast_select_fusion.23), channel_id=1, source_target_pairs={{0,8},{4,12},{8,0},{12,4},{16,24},{20,28},{24,16},{28,20},{1,9},{5... | collective-permute-start | bytes 737288 | tf_op jit(solution)/shard_map/ppermute | solution.py:169
  275.2 10.7 %collective-permute-start.70 = (bf16[320,384]{1,0:T(8,128)(2,1)S(1)}, bf16[320,384]{1,0:T(8,128)(2,1)S(1)}, u32[]{:S(2)}, u32[]{:S(2)}) collective-permute-start(bf16[320,384]{1,0:T(8,128)(2,1)S(1)} %collective-permute-done.59), channel_id=1, source_target_pairs={{8,16},{12,20},{16,8},{20,12},{9,17},{13,21},{17,9},{21,13},{10,18... | collective-permute-start | bytes 737288 | tf_op jit(solution)/shard_map/ppermute | solution.py:169
  283.5 11.7 %collective-permute-start.65 = (bf16[320,384]{1,0:T(8,128)(2,1)S(1)}, bf16[320,384]{1,0:T(8,128)(2,1)S(1)}, u32[]{:S(2)}, u32[]{:S(2)}) collective-permute-start(bf16[320,384]{1,0:T(8,128)(2,1)S(1)} %broadcast_select_fusion.18), channel_id=1, source_target_pairs={{0,8},{4,12},{8,0},{12,4},{16,24},{20,28},{24,16},{28,20},{1,9},{5... | collective-permute-start | bytes 737288 | tf_op jit(solution)/shard_map/ppermute | solution.py:169
  283.8 11.4 %collective-permute-start.66 = (bf16[320,384]{1,0:T(8,128)(2,1)S(1)}, bf16[320,384]{1,0:T(8,128)(2,1)S(1)}, u32[]{:S(2)}, u32[]{:S(2)}) collective-permute-start(bf16[320,384]{1,0:T(8,128)(2,1)S(1)} %collective-permute-done.63), channel_id=1, source_target_pairs={{8,16},{12,20},{16,8},{20,12},{9,17},{13,21},{17,9},{21,13},{10,18... | collective-permute-start | bytes 737288 | tf_op jit(solution)/shard_map/ppermute | solution.py:169
  286.7 10.5 %collective-permute-start.71 = (bf16[320,384]{1,0:T(8,128)(2,1)S(1)}, bf16[320,384]{1,0:T(8,128)(2,1)S(1)}, u32[]{:S(2)}, u32[]{:S(2)}) collective-permute-start(bf16[320,384]{1,0:T(8,128)(2,1)S(1)} %broadcast_select_fusion.16), channel_id=1, source_target_pairs={{0,8},{4,12},{8,0},{12,4},{16,24},{20,28},{24,16},{28,20},{1,9},{5... | collective-permute-start | bytes 737288 | tf_op jit(solution)/shard_map/ppermute | solution.py:169
  293.0 26.4 %collective-permute-start.80 = (bf16[768,384]{1,0:T(8,128)(2,1)S(1)}, bf16[768,384]{1,0:T(8,128)(2,1)S(1)}, u32[]{:S(2)}, u32[]{:S(2)}) collective-permute-start(bf16[768,384]{1,0:T(8,128)(2,1)S(1)} %fusion.11), channel_id=1, source_target_pairs={{0,4},{4,0},{8,12},{12,8},{16,20},{20,16},{24,28},{28,24},{1,5},{5... | collective-permute-start | bytes 1769480 | tf_op jit(solution)/shard_map/ppermute | solution.py:183
  295.2 10.9 %collective-permute-start.67 = (bf16[320,384]{1,0:T(8,128)(2,1)S(1)}, bf16[320,384]{1,0:T(8,128)(2,1)S(1)}, u32[]{:S(2)}, u32[]{:S(2)}) collective-permute-start(bf16[320,384]{1,0:T(8,128)(2,1)S(1)} %pad_select_fusion.1), channel_id=1, source_target_pairs={{0,8},{4,12},{8,0},{12,4},{16,24},{20,28},{24,16},{28,20},{1,9},{5... | collective-permute-start | bytes 737288 | tf_op jit(solution)/shard_map/ppermute | solution.py:169
  295.3 12.2 %collective-permute-start.68 = (bf16[320,384]{1,0:T(8,128)(2,1)S(1)}, bf16[320,384]{1,0:T(8,128)(2,1)S(1)}, u32[]{:S(2)}, u32[]{:S(2)}) collective-permute-start(bf16[320,384]{1,0:T(8,128)(2,1)S(1)} %collective-permute-done.65), channel_id=1, source_target_pairs={{8,16},{12,20},{16,8},{20,12},{9,17},{13,21},{17,9},{21,13},{10,18... | collective-permute-start | bytes 737288 | tf_op jit(solution)/shard_map/ppermute | solution.py:169
  297.3 12.1 %collective-permute-start.74 = (bf16[320,384]{1,0:T(8,128)(2,1)S(1)}, bf16[320,384]{1,0:T(8,128)(2,1)S(1)}, u32[]{:S(2)}, u32[]{:S(2)}) collective-permute-start(bf16[320,384]{1,0:T(8,128)(2,1)S(1)} %collective-permute-done.71), channel_id=1, source_target_pairs={{8,16},{12,20},{16,8},{20,12},{9,17},{13,21},{17,9},{21,13},{10,18... | collective-permute-start | bytes 737288 | tf_op jit(solution)/shard_map/ppermute | solution.py:169
  298.0 11.4 %collective-permute-start.73 = (bf16[320,384]{1,0:T(8,128)(2,1)S(1)}, bf16[320,384]{1,0:T(8,128)(2,1)S(1)}, u32[]{:S(2)}, u32[]{:S(2)}) collective-permute-start(bf16[320,384]{1,0:T(8,128)(2,1)S(1)} %pad_select_fusion), channel_id=1, source_target_pairs={{0,8},{4,12},{8,0},{12,4},{16,24},{20,28},{24,16},{28,20},{1,9},{5... | collective-permute-start | bytes 737288 | tf_op jit(solution)/shard_map/ppermute | solution.py:169
  306.2 17.4 %collective-permute-start.79 = (bf16[768,384]{1,0:T(8,128)(2,1)S(1)}, bf16[768,384]{1,0:T(8,128)(2,1)S(1)}, u32[]{:S(2)}, u32[]{:S(2)}) collective-permute-start(bf16[768,384]{1,0:T(8,128)(2,1)S(1)} %fusion.10), channel_id=1, source_target_pairs={{0,4},{4,0},{8,12},{12,8},{16,20},{20,16},{24,28},{28,24},{1,5},{5... | collective-permute-start | bytes 1769480 | tf_op jit(solution)/shard_map/ppermute | solution.py:183
  313.8 20.8 %collective-permute-start.78 = (bf16[768,384]{1,0:T(8,128)(2,1)S(1)}, bf16[768,384]{1,0:T(8,128)(2,1)S(1)}, u32[]{:S(2)}, u32[]{:S(2)}) collective-permute-start(bf16[768,384]{1,0:T(8,128)(2,1)S(1)} %fusion.9), channel_id=1, source_target_pairs={{0,4},{4,0},{8,12},{12,8},{16,20},{20,16},{24,28},{28,24},{1,5},{5... | collective-permute-start | bytes 1769480 | tf_op jit(solution)/shard_map/ppermute | solution.py:183
  317.7 23.2 %collective-permute-start.77 = (bf16[768,384]{1,0:T(8,128)(2,1)S(1)}, bf16[768,384]{1,0:T(8,128)(2,1)S(1)}, u32[]{:S(2)}, u32[]{:S(2)}) collective-permute-start(bf16[768,384]{1,0:T(8,128)(2,1)S(1)} %fusion.8), channel_id=1, source_target_pairs={{0,4},{4,0},{8,12},{12,8},{16,20},{20,16},{24,28},{28,24},{1,5},{5... | collective-permute-start | bytes 1769480 | tf_op jit(solution)/shard_map/ppermute | solution.py:183
  (66 other events, 442.9 us)

commit v2 on v1

--- a/solution.py
+++ b/solution.py
@@ -209,10 +209,6 @@
             rows, weight[-1] = lax.optimization_barrier((rows, weight[-1]))
         weight.append([rows] + [turn(rows, -step) for step in range(1, inner)])
 
-    def weight_piece(piece):
-        cols = slices[piece % lot]
-        return jnp.concatenate([rows[:, cols] for rows in weight[piece // lot]], axis=0)
-
     gather_weight()
     target_other = swap_end(target)
 
@@ -254,9 +250,8 @@
     rows_each = batch_rows // streams
     parts = [slice(part * rows_each, (part + 1) * rows_each) for part in range(streams)]
     features, scales, predicted, errors = [], [], [], []
-    sums, preact, partial, delta = {}, {}, {}, {}
+    sums, preact, delta = {}, {}, {}
     ends, middles = {}, {}
-    whole_parts = {}
     early, pending, outs = {}, {}, None
 
     def wide(value):
@@ -265,17 +260,21 @@
     def group_features(group):
         return make_features(jnp.concatenate([outbound[group], inbound[group]], axis=0))
 
-    def partial_sums(unit):
+    joined = {}
+
+    def partial_sums(group, side, which):
+        if which not in joined:
+            joined[which] = jnp.concatenate(weight[which], axis=0)
+        left = features[group][side * batch_rows :][:batch_rows]
+        return dot32(left, joined[which]).astype(jnp.bfloat16)
+
+    def sums_of(unit, side, rows=slice(None)):
         group, piece = divmod(unit, pieces)
-        right = weight_piece(piece)
-        return [
-            dot32(features[group][side * batch_rows :][:batch_rows], right).astype(jnp.bfloat16)
-            for side in range(2)
-        ]
-
-    def finished(part, unit, before):
+        return sums[group, side, piece // lot][rows, slices[piece % lot]]
+
+    def finished(unit, before):
         group, piece = divmod(unit, pieces)
-        value = (wide(sums[unit][1][parts[part]]) + wide(before)) * scales[group][parts[part]]
+        value = (wide(sums_of(unit, 1)) + wide(before)) * scales[group]
         active = gelu_tanh(value).astype(jnp.bfloat16)
         return value, dot32(active, readout[slices[piece]])
 
@@ -287,7 +286,7 @@
             (((1,), (1,)), ((), ())),
             preferred_element_type=jnp.float32,
         )
-        slope = gelu_slope(preact[part, unit])
+        slope = gelu_slope(preact[unit][parts[part]])
         return (back * slope * scales[group][parts[part]]).astype(jnp.bfloat16)
 
     def gradient_term(unit, rows):
@@ -304,15 +303,16 @@
         )
 
     features.append(group_features(0))
-    sums[0] = partial_sums(0)
+    sums[0, 0, 0] = partial_sums(0, 0, 0)
     gather_weight()
+    late = streams - 1
     side_work = {
-        (0, 0): [1, "scales"],
-        (0, streams - 1): ["features"],
-        (1, 0): [4, 5],
-        (1, streams - 1): [2],
-        (2, 0): [3],
-        (2, streams - 1): [6, 7],
+        (0, 0): [(0, 1, 0), "scales", "features"],
+        (0, late): [(1, 0, 0), (1, 1, 0)],
+        (1, late): [(0, 0, 1)],
+        (2, late): [(0, 1, 1)],
+        (3, late): [(1, 0, 1)],
+        (4, late): [(1, 1, 1)],
     }
     for tick, part in [(t, p) for t in range(2 * units + line) for p in range(streams)]:
         back_tick = tick - units
@@ -326,27 +326,23 @@
                 value = pending.pop((box, key))
                 if box == "sums":
                     sums[key] = value
-                elif box == "preact":
-                    preact[key], partial[key] = value
                 elif box == "delta":
                     delta[key] = value
                 elif box == "early":
                     early[key] = value
-                elif box == "features":
-                    features.append(value)
                 else:
                     scales = all_scales(value)
 
         from_end = from_middle = None
         if tick < units:
-            from_end = sums[tick][0][parts[part]]
+            from_end = sums_of(tick, 0, parts[part])
         elif back_tick < units:
             from_end = delta[part, back_tick]
         elif back_tick == units:
             narrow = predicted[1][parts[part]].astype(jnp.bfloat16)
             from_end = jnp.pad(narrow, ((0, 0), (0, cut - patch_width)))
         if 2 <= tick < units + 2:
-            from_middle = (wide(sums[tick - 2][1][parts[part]]) + wide(was_middle)).astype(jnp.bfloat16)
+            from_middle = (wide(sums_of(tick - 2, 1, parts[part])) + wide(was_middle)).astype(jnp.bfloat16)
         elif 2 <= back_tick < units + 2:
             from_middle = was_middle
         if from_end is None or from_middle is None:
@@ -356,7 +352,7 @@
         if payload is not None:
             ends[part, tick] = swap_end(payload)
         if 1 <= tick < units + 1:
-            payload = (wide(sums[tick - 1][0][parts[part]]) + wide(was_end)).astype(jnp.bfloat16)
+            payload = (wide(sums_of(tick - 1, 0, parts[part])) + wide(was_end)).astype(jnp.bfloat16)
             middles[part, tick] = swap_middle(payload)
         elif 1 <= back_tick < units + 1:
             middles[part, tick] = swap_middle(was_end)
@@ -365,26 +361,30 @@
             if work == "scales":
                 pending["scales", None] = local_scales()
             elif work == "features":
-                pending["features", None] = group_features(1)
+                features.append(group_features(1))
             else:
-                pending["sums", work] = partial_sums(work)
-
-        unit = tick - line + 1
-        if 0 <= unit < units:
-            group, piece = divmod(unit, pieces)
-            value = finished(part, unit, was_end)
-            pending["preact", (part, unit)] = value
-            if piece == pieces - 1:
-                whole = sum(partial[part, unit - back] for back in range(1, pieces)) + value[1]
-                whole_parts[part] = whole
-                if part == streams - 1:
-                    whole = [whole_parts[other] for other in range(streams)]
-                    predicted.append(mp_sum(jnp.concatenate(whole, axis=0), jnp.bfloat16))
-                    errors.append((predicted[-1] - wide(goals[group])).astype(jnp.bfloat16))
+                group = work[0]
+                if tick > 1:
+                    features[group] = lax.optimization_barrier((features[group], was_end))[0]
+                pending["sums", work] = partial_sums(*work)
+
+        group, piece = divmod(tick - line + 1, pieces)
+        if 0 <= group < groups and piece == pieces - 1 and part == late:
+            total = 0.0
+            for unit in range(group * pieces, (group + 1) * pieces):
+                arrived = [ends[other, unit + 2] for other in range(streams)]
+                preact[unit], value = finished(unit, jnp.concatenate(arrived, axis=0))
+                total += value
+            predicted.append(mp_sum(total, jnp.bfloat16))
+            errors.append((predicted[-1] - wide(goals[group])).astype(jnp.bfloat16))
 
         unit = back_tick + 1
         if 0 <= unit < units:
-            pending["delta", (part, unit)] = new_delta(part, unit, was_end)
+            value = new_delta(part, unit, was_end)
+            if unit % pieces:
+                pending["delta", (part, unit)] = value
+            else:
+                delta[part, unit] = value
 
         unit = back_tick - line + 1
         if 0 <= unit < units and part == streams - 1:

time: 348 us -> 369 us (1.060)
  waiting for transfers between devices: 91.7 us -> 115 us
  matrix products: 62.8 us -> 54.1 us
  other arithmetic: 12.4 us -> 17.7 us
    ppermute x69, waiting for transfers between devices: 64.1 us -> 94.3 us  [swap(): return lax.ppermute(value, 'dp', pairs)]
    dot_general x37 -> x21, matrix products: 38 us -> 29.3 us  [dot32(): return jnp.dot(left, right, preferred_element_type=jnp.float32)]
    slice x9 -> x4, local copies, waits for them, and re-layouts: 8.35 us -> 1.39 us  [the longest x1 1.05 us: sums_of(): return sums[group, side, piece // lot][rows, slices[piece % lot]]]
  transfers between devices with their start and end apart: 82 -> 82, of which waited for: 26 -> 33; matrix products, arithmetic and copies ran while one was open for 22% -> 19% of each run, Pallas kernels for 3% -> 2%
where the time goes in v2:
time: 369 us; the launch traced here: 364 us
  starting transfers between devices  144 us (39%)
  waiting for transfers between devices  115 us (31%)
  matrix products  54.1 us (15%)
  other arithmetic  17.7 us (5%)
  Pallas kernels  11.7 us (3%)
  local copies, waits for them, and re-layouts  10.6 us (3%)
  blocking collectives  7.72 us (2%)
    ppermute x69, starting transfers between devices, swap(): return lax.ppermute(value, 'dp', pairs)  124 us
    ppermute x69, waiting for transfers between devices, swap(): return lax.ppermute(value, 'dp', pairs)  94.3 us
    dot_general x21, matrix products, dot32(): return jnp.dot(left, right, preferred_element_type=jnp.float32)  29.3 us
    dot_general x12, matrix products, gradient_term(): lax.dot_general(features[unit // pieces][:, rows], jnp.concatenate(arrive...  18.7 us
    pallas_call x4, Pallas kernels, adam_piece(): pl.pallas_call(adam_kernel, grid=(3,), in_specs=[piece, piece, column, co...  11.7 us
    all_to_all x1, waiting for transfers between devices, route(): lax.all_to_all(outgoing.reshape(devices_all, line * lot, patch_width), ('...  10.5 us
    ppermute x6, waiting for transfers between devices, turn(): return lax.ppermute(value, 'dp', pairs)  7.8 us
    all_gather x1, blocking collectives, shards(): lax.all_gather(blocks.reshape(line, block_rows, -1), 'mp', axis=1, tiled=...  7.72 us
  transfers between devices with their start and end apart: 82, of which 33 were waited for; matrix products, arithmetic and copies ran while one was open for 19% of the time, Pallas kernels for 2%

profile of v2, /device:TPU:0, one launch (start us, length us, event | category | flops | bytes accessed | tf_op | source)
XLA Modules:
  0.0 364.5 jit_solution(7136342791461622604)
XLA Ops:
  1.4 2.6 convert.14
  8.0 7.3 %all-to-all-start = ((bf16[32,64,128]{2,1,0:T(8,128)(2,1)}), bf16[32,64,128]{2,1,0:T(8,128)(2,1)S(1)}, u32[]{:S(2)}, u32[]{:S(2)}) async-start(bf16[32,64,128]{2,1,0:T(8,128)(2,1)} %bitcast.4), calls=%async_computation | async-start | bytes 1048576 | tf_op jit(solution)/shard_map/all_to_all | solution.py:74
  20.3 10.5 %all-to-all-done = bf16[32,64,128]{2,1,0:T(8,128)(2,1)S(1)} async-done(((bf16[32,64,128]{2,1,0:T(8,128)(2,1)}), bf16[32,64,128]{2,1,0:T(8,128)(2,1)S(1)}, u32[]{:S(2)}, u32[]{:S(2)}) %all-to-all-start) | async-done | bytes 524320 | tf_op jit(solution)/shard_map/all_to_all | solution.py:74
  32.2 7.7 %all_gather.3 = bf16[4,640,128]{2,1,0:T(8,128)(2,1)S(1)} all-gather(bf16[4,160,128]{2,1,0:T(8,128)(2,1)S(1)} %bitcast.75), channel_id=1, replica_groups=mesh['dp'=8,'mp'=4] {'mp'}, dimensions={1}, use_global_device_ids=true | all-gather | bytes 819200 | tf_op jit(solution)/shard_map/all_gather | solution.py:216
  40.0 3.5 fusion.3
  43.5 2.9 fusion.5
  46.4 2.9 fusion.1
  61.9 2.6 fusion.39
  64.5 13.2 %collective-permute-done.1 = bf16[320,384]{1,0:T(8,128)(2,1)S(1)} collective-permute-done((bf16[320,384]{1,0:T(8,128)(2,1)S(1)}, bf16[320,384]{1,0:T(8,128)(2,1)S(1)}, u32[]{:S(2)}, u32[]{:S(2)}) %collective-permute-start.1) | collective-permute-done | bytes 245792 | tf_op jit(solution)/shard_map/ppermute | solution.py:169
  88.7 6.1 %collective-permute-start.5 = (bf16[320,384]{1,0:T(8,128)(2,1)S(1)}, bf16[320,384]{1,0:T(8,128)(2,1)S(1)}, u32[]{:S(2)}, u32[]{:S(2)}) collective-permute-start(bf16[320,384]{1,0:T(8,128)(2,1)S(1)} %get-tuple-element.279), channel_id=1, source_target_pairs={{0,8},{4,12},{8,0},{12,4},{16,24},{20,28},{24,16},{28,20},{1,9},{5... | collective-permute-start | bytes 737288 | tf_op jit(solution)/shard_map/ppermute | solution.py:169
  97.9 6.5 %collective-permute-done.10 = bf16[320,384]{1,0:T(8,128)(2,1)S(1)} collective-permute-done((bf16[320,384]{1,0:T(8,128)(2,1)S(1)}, bf16[320,384]{1,0:T(8,128)(2,1)S(1)}, u32[]{:S(2)}, u32[]{:S(2)}) %collective-permute-start.10) | collective-permute-done | bytes 245792 | tf_op jit(solution)/shard_map/ppermute | solution.py:169
  105.4 7.5 %collective-permute-start.14 = (bf16[320,384]{1,0:T(8,128)(2,1)S(1)}, bf16[320,384]{1,0:T(8,128)(2,1)S(1)}, u32[]{:S(2)}, u32[]{:S(2)}) collective-permute-start(bf16[320,384]{1,0:T(8,128)(2,1)S(1)} %get-tuple-element.277), channel_id=1, source_target_pairs={{0,8},{4,12},{8,0},{12,4},{16,24},{20,28},{24,16},{28,20},{1,9},{5... | collective-permute-start | bytes 737288 | tf_op jit(solution)/shard_map/ppermute | solution.py:169
  113.0 2.6 fusion.33
  115.7 2.8 collective-permute-done.14
  121.4 7.4 %collective-permute-start.18 = (bf16[320,384]{1,0:T(8,128)(2,1)S(1)}, bf16[320,384]{1,0:T(8,128)(2,1)S(1)}, u32[]{:S(2)}, u32[]{:S(2)}) collective-permute-start(bf16[320,384]{1,0:T(8,128)(2,1)S(1)} %get-tuple-element.275), channel_id=1, source_target_pairs={{0,8},{4,12},{8,0},{12,4},{16,24},{20,28},{24,16},{28,20},{1,9},{5... | collective-permute-start | bytes 737288 | tf_op jit(solution)/shard_map/ppermute | solution.py:169
  136.8 3.0 collective-permute-start.22
  139.9 4.1 %collective-permute-done.22 = bf16[320,384]{1,0:T(8,128)(2,1)S(1)} collective-permute-done((bf16[320,384]{1,0:T(8,128)(2,1)S(1)}, bf16[320,384]{1,0:T(8,128)(2,1)S(1)}, u32[]{:S(2)}, u32[]{:S(2)}) %collective-permute-start.22) | collective-permute-done | bytes 245792 | tf_op jit(solution)/shard_map/ppermute | solution.py:169
  149.5 3.2 collective-permute-start.46
  155.1 4.6 %collective-permute-start.28 = (bf16[320,384]{1,0:T(8,128)(2,1)S(1)}, bf16[320,384]{1,0:T(8,128)(2,1)S(1)}, u32[]{:S(2)}, u32[]{:S(2)}) collective-permute-start(bf16[320,384]{1,0:T(8,128)(2,1)S(1)} %get-tuple-element.271), channel_id=1, source_target_pairs={{0,8},{4,12},{8,0},{12,4},{16,24},{20,28},{24,16},{28,20},{1,9},{5... | collective-permute-start | bytes 737288 | tf_op jit(solution)/shard_map/ppermute | solution.py:169
  168.7 4.4 %collective-permute-done.30 = bf16[320,384]{1,0:T(8,128)(2,1)S(1)} collective-permute-done((bf16[320,384]{1,0:T(8,128)(2,1)S(1)}, bf16[320,384]{1,0:T(8,128)(2,1)S(1)}, u32[]{:S(2)}, u32[]{:S(2)}) %collective-permute-start.30) | collective-permute-done | bytes 245792 | tf_op jit(solution)/shard_map/ppermute | solution.py:169
  173.4 4.4 %collective-permute-start.32 = (bf16[320,384]{1,0:T(8,128)(2,1)S(1)}, bf16[320,384]{1,0:T(8,128)(2,1)S(1)}, u32[]{:S(2)}, u32[]{:S(2)}) collective-permute-start(bf16[320,384]{1,0:T(8,128)(2,1)S(1)} %get-tuple-element.269), channel_id=1, source_target_pairs={{0,8},{4,12},{8,0},{12,4},{16,24},{20,28},{24,16},{28,20},{1,9},{5... | collective-permute-start | bytes 737288 | tf_op jit(solution)/shard_map/ppermute | solution.py:169
  178.7 6.0 %collective-permute-done.32 = bf16[320,384]{1,0:T(8,128)(2,1)S(1)} collective-permute-done((bf16[320,384]{1,0:T(8,128)(2,1)S(1)}, bf16[320,384]{1,0:T(8,128)(2,1)S(1)}, u32[]{:S(2)}, u32[]{:S(2)}) %collective-permute-start.32) | collective-permute-done | bytes 245792 | tf_op jit(solution)/shard_map/ppermute | solution.py:169
  188.1 10.1 %collective-permute-start.36 = (bf16[320,384]{1,0:T(8,128)(2,1)S(1)}, bf16[320,384]{1,0:T(8,128)(2,1)S(1)}, u32[]{:S(2)}, u32[]{:S(2)}) collective-permute-start(bf16[320,384]{1,0:T(8,128)(2,1)S(1)} %get-tuple-element.295), channel_id=1, source_target_pairs={{0,8},{4,12},{8,0},{12,4},{16,24},{20,28},{24,16},{28,20},{1,9},{5... | collective-permute-start | bytes 737288 | tf_op jit(solution)/shard_map/ppermute | solution.py:169
  199.3 3.1 collective-permute-done.36
  206.5 7.1 %collective-permute-start.40 = (bf16[320,384]{1,0:T(8,128)(2,1)S(1)}, bf16[320,384]{1,0:T(8,128)(2,1)S(1)}, u32[]{:S(2)}, u32[]{:S(2)}) collective-permute-start(bf16[320,384]{1,0:T(8,128)(2,1)S(1)} %get-tuple-element.291), channel_id=1, source_target_pairs={{0,8},{4,12},{8,0},{12,4},{16,24},{20,28},{24,16},{28,20},{1,9},{5... | collective-permute-start | bytes 737288 | tf_op jit(solution)/shard_map/ppermute | solution.py:169
  214.1 5.0 %collective-permute-done.40 = bf16[320,384]{1,0:T(8,128)(2,1)S(1)} collective-permute-done((bf16[320,384]{1,0:T(8,128)(2,1)S(1)}, bf16[320,384]{1,0:T(8,128)(2,1)S(1)}, u32[]{:S(2)}, u32[]{:S(2)}) %collective-permute-start.40) | collective-permute-done | bytes 245792 | tf_op jit(solution)/shard_map/ppermute | solution.py:169
  220.1 2.9 collective-permute-done.42
  223.8 4.3 %collective-permute-start.47 = (bf16[320,384]{1,0:T(8,128)(2,1)S(1)}, bf16[320,384]{1,0:T(8,128)(2,1)S(1)}, u32[]{:S(2)}, u32[]{:S(2)}) collective-permute-start(bf16[320,384]{1,0:T(8,128)(2,1)S(1)} %broadcast_select_fusion.43), channel_id=1, source_target_pairs={{0,8},{4,12},{8,0},{12,4},{16,24},{20,28},{24,16},{28,20},{1,9},{5... | collective-permute-start | bytes 737288 | tf_op jit(solution)/shard_map/ppermute | solution.py:169
  235.3 4.9 %collective-permute-done.51 = bf16[320,384]{1,0:T(8,128)(2,1)S(1)} collective-permute-done((bf16[320,384]{1,0:T(8,128)(2,1)S(1)}, bf16[320,384]{1,0:T(8,128)(2,1)S(1)}, u32[]{:S(2)}, u32[]{:S(2)}) %collective-permute-start.51) | collective-permute-done | bytes 245792 | tf_op jit(solution)/shard_map/ppermute | solution.py:169
  241.0 2.6 collective-permute-start.49
  246.1 4.3 %collective-permute-done.49 = bf16[320,384]{1,0:T(8,128)(2,1)S(1)} collective-permute-done((bf16[320,384]{1,0:T(8,128)(2,1)S(1)}, bf16[320,384]{1,0:T(8,128)(2,1)S(1)}, u32[]{:S(2)}, u32[]{:S(2)}) %collective-permute-start.49) | collective-permute-done | bytes 245792 | tf_op jit(solution)/shard_map/ppermute | solution.py:169
  250.9 3.5 collective-permute-done.55
  256.3 6.3 %collective-permute-start.57 = (bf16[320,384]{1,0:T(8,128)(2,1)S(1)}, bf16[320,384]{1,0:T(8,128)(2,1)S(1)}, u32[]{:S(2)}, u32[]{:S(2)}) collective-permute-start(bf16[320,384]{1,0:T(8,128)(2,1)S(1)} %get-tuple-element.355), channel_id=1, source_target_pairs={{0,8},{4,12},{8,0},{12,4},{16,24},{20,28},{24,16},{28,20},{1,9},{5... | collective-permute-start | bytes 737288 | tf_op jit(solution)/shard_map/ppermute | solution.py:169
  265.7 6.1 %collective-permute-done.53 = bf16[320,384]{1,0:T(8,128)(2,1)S(1)} collective-permute-done((bf16[320,384]{1,0:T(8,128)(2,1)S(1)}, bf16[320,384]{1,0:T(8,128)(2,1)S(1)}, u32[]{:S(2)}, u32[]{:S(2)}) %collective-permute-start.53) | collective-permute-done | bytes 245792 | tf_op jit(solution)/shard_map/ppermute | solution.py:169
  273.8 6.3 %collective-permute-start.61 = (bf16[320,384]{1,0:T(8,128)(2,1)S(1)}, bf16[320,384]{1,0:T(8,128)(2,1)S(1)}, u32[]{:S(2)}, u32[]{:S(2)}) collective-permute-start(bf16[320,384]{1,0:T(8,128)(2,1)S(1)} %broadcast_select_fusion.28), channel_id=1, source_target_pairs={{0,8},{4,12},{8,0},{12,4},{16,24},{20,28},{24,16},{28,20},{1,9},{5... | collective-permute-start | bytes 737288 | tf_op jit(solution)/shard_map/ppermute | solution.py:169
  282.8 2.4 collective-permute-done.61
  289.3 6.3 %collective-permute-start.63 = (bf16[320,384]{1,0:T(8,128)(2,1)S(1)}, bf16[320,384]{1,0:T(8,128)(2,1)S(1)}, u32[]{:S(2)}, u32[]{:S(2)}) collective-permute-start(bf16[320,384]{1,0:T(8,128)(2,1)S(1)} %broadcast_select_fusion.23), channel_id=1, source_target_pairs={{0,8},{4,12},{8,0},{12,4},{16,24},{20,28},{24,16},{28,20},{1,9},{5... | collective-permute-start | bytes 737288 | tf_op jit(solution)/shard_map/ppermute | solution.py:169
  298.3 4.1 %collective-permute-done.69 = bf16[320,384]{1,0:T(8,128)(2,1)S(1)} collective-permute-done((bf16[320,384]{1,0:T(8,128)(2,1)S(1)}, bf16[320,384]{1,0:T(8,128)(2,1)S(1)}, u32[]{:S(2)}, u32[]{:S(2)}) %collective-permute-start.69) | collective-permute-done | bytes 245792 | tf_op jit(solution)/shard_map/ppermute | solution.py:169
  304.0 6.6 %collective-permute-start.71 = (bf16[320,384]{1,0:T(8,128)(2,1)S(1)}, bf16[320,384]{1,0:T(8,128)(2,1)S(1)}, u32[]{:S(2)}, u32[]{:S(2)}) collective-permute-start(bf16[320,384]{1,0:T(8,128)(2,1)S(1)} %broadcast_select_fusion.16), channel_id=1, source_target_pairs={{0,8},{4,12},{8,0},{12,4},{16,24},{20,28},{24,16},{28,20},{1,9},{5... | collective-permute-start | bytes 737288 | tf_op jit(solution)/shard_map/ppermute | solution.py:169
  315.7 3.3 collective-permute-done.65
  319.7 4.6 %collective-permute-start.73 = (bf16[320,384]{1,0:T(8,128)(2,1)S(1)}, bf16[320,384]{1,0:T(8,128)(2,1)S(1)}, u32[]{:S(2)}, u32[]{:S(2)}) collective-permute-start(bf16[320,384]{1,0:T(8,128)(2,1)S(1)} %pad_select_fusion), channel_id=1, source_target_pairs={{0,8},{4,12},{8,0},{12,4},{16,24},{20,28},{24,16},{28,20},{1,9},{5... | collective-permute-start | bytes 737288 | tf_op jit(solution)/shard_map/ppermute | solution.py:169
  327.0 4.3 %collective-permute-done.73 = bf16[320,384]{1,0:T(8,128)(2,1)S(1)} collective-permute-done((bf16[320,384]{1,0:T(8,128)(2,1)S(1)}, bf16[320,384]{1,0:T(8,128)(2,1)S(1)}, u32[]{:S(2)}, u32[]{:S(2)}) %collective-permute-start.73) | collective-permute-done | bytes 245792 | tf_op jit(solution)/shard_map/ppermute | solution.py:169
  344.3 2.9 adam_piece.4
  348.5 2.9 adam_piece.5
  351.4 3.6 collective-permute-done.78.came_ref
  355.0 2.9 adam_piece.6
  357.9 3.4 collective-permute-done.77.came_ref
  361.4 2.9 adam_piece.7
  (356 shorter events, 128.5 us)
Async XLA Ops:
  8.0 22.9 %all-to-all-start = ((bf16[32,64,128]{2,1,0:T(8,128)(2,1)}), bf16[32,64,128]{2,1,0:T(8,128)(2,1)S(1)}, u32[]{:S(2)}, u32[]{:S(2)}) async-start(bf16[32,64,128]{2,1,0:T(8,128)(2,1)} %bitcast.4), calls=%async_computation | async-start | bytes 1048576 | tf_op jit(solution)/shard_map/all_to_all | solution.py:74
  15.3 34.1 %collective-permute-start = (bf16[768,768]{1,0:T(8,128)(2,1)S(1)}, bf16[768,768]{1,0:T(8,128)(2,1)}, u32[]{:S(2)}, u32[]{:S(2)}) collective-permute-start(bf16[768,768]{1,0:T(8,128)(2,1)S(1)} %get-tuple-element.135), channel_id=1, source_target_pairs={{0,4},{4,0},{8,12},{12,8},{16,20},{20,16},{24,28},{28,24},{1,5},{5... | collective-permute-start | bytes 3538952 | tf_op jit(solution)/shard_map/ppermute | solution.py:183
  55.2 28.4 %collective-permute-start.4 = (bf16[768,768]{1,0:T(8,128)(2,1)S(1)}, bf16[768,768]{1,0:T(8,128)(2,1)}, u32[]{:S(2)}, u32[]{:S(2)}) collective-permute-start(bf16[768,768]{1,0:T(8,128)(2,1)S(1)} %get-tuple-element.138), channel_id=1, source_target_pairs={{0,4},{4,0},{8,12},{12,8},{16,20},{20,16},{24,28},{28,24},{1,5},{5... | collective-permute-start | bytes 3538952 | tf_op jit(solution)/shard_map/ppermute | solution.py:183
  59.2 18.5 %collective-permute-start.8 = (bf16[320,384]{1,0:T(8,128)(2,1)S(1)}, bf16[320,384]{1,0:T(8,128)(2,1)S(1)}, u32[]{:S(2)}, u32[]{:S(2)}) collective-permute-start(bf16[320,384]{1,0:T(8,128)(2,1)S(1)} %get-tuple-element.306), channel_id=1, source_target_pairs={{0,8},{4,12},{8,0},{12,4},{16,24},{20,28},{24,16},{28,20},{1,9},{5... | collective-permute-start | bytes 737288 | tf_op jit(solution)/shard_map/ppermute | solution.py:169
  59.9 22.9 %collective-permute-start.7 = (bf16[320,384]{1,0:T(8,128)(2,1)}, bf16[320,384]{1,0:T(8,128)(2,1)S(1)}, u32[]{:S(2)}, u32[]{:S(2)}) collective-permute-start(bf16[320,384]{1,0:T(8,128)(2,1)} %get-tuple-element.307), channel_id=1, source_target_pairs={{0,8},{4,12},{8,0},{12,4},{16,24},{20,28},{24,16},{28,20},{1,9},{5... | collective-permute-start | bytes 737288 | tf_op jit(solution)/shard_map/ppermute | solution.py:169
  61.2 16.4 %collective-permute-start.1 = (bf16[320,384]{1,0:T(8,128)(2,1)S(1)}, bf16[320,384]{1,0:T(8,128)(2,1)S(1)}, u32[]{:S(2)}, u32[]{:S(2)}) collective-permute-start(bf16[320,384]{1,0:T(8,128)(2,1)S(1)} %get-tuple-element.308), channel_id=1, source_target_pairs={{0,8},{4,12},{8,0},{12,4},{16,24},{20,28},{24,16},{28,20},{1,9},{5... | collective-permute-start | bytes 737288 | tf_op jit(solution)/shard_map/ppermute | solution.py:169
  88.7 15.8 %collective-permute-start.5 = (bf16[320,384]{1,0:T(8,128)(2,1)S(1)}, bf16[320,384]{1,0:T(8,128)(2,1)S(1)}, u32[]{:S(2)}, u32[]{:S(2)}) collective-permute-start(bf16[320,384]{1,0:T(8,128)(2,1)S(1)} %get-tuple-element.279), channel_id=1, source_target_pairs={{0,8},{4,12},{8,0},{12,4},{16,24},{20,28},{24,16},{28,20},{1,9},{5... | collective-permute-start | bytes 737288 | tf_op jit(solution)/shard_map/ppermute | solution.py:169
  104.5 11.1 %collective-permute-start.15 = (bf16[320,384]{1,0:T(8,128)(2,1)S(1)}, bf16[320,384]{1,0:T(8,128)(2,1)S(1)}, u32[]{:S(2)}, u32[]{:S(2)}) collective-permute-start(bf16[320,384]{1,0:T(8,128)(2,1)S(1)} %add_convert_fusion.28), channel_id=1, source_target_pairs={{8,16},{12,20},{16,8},{20,12},{9,17},{13,21},{17,9},{21,13},{10,18... | collective-permute-start | bytes 737288 | tf_op jit(solution)/shard_map/ppermute | solution.py:169
  105.4 13.0 %collective-permute-start.14 = (bf16[320,384]{1,0:T(8,128)(2,1)S(1)}, bf16[320,384]{1,0:T(8,128)(2,1)S(1)}, u32[]{:S(2)}, u32[]{:S(2)}) collective-permute-start(bf16[320,384]{1,0:T(8,128)(2,1)S(1)} %get-tuple-element.277), channel_id=1, source_target_pairs={{0,8},{4,12},{8,0},{12,4},{16,24},{20,28},{24,16},{28,20},{1,9},{5... | collective-permute-start | bytes 737288 | tf_op jit(solution)/shard_map/ppermute | solution.py:169
  119.3 12.0 %collective-permute-start.19 = (bf16[320,384]{1,0:T(8,128)(2,1)S(1)}, bf16[320,384]{1,0:T(8,128)(2,1)S(1)}, u32[]{:S(2)}, u32[]{:S(2)}) collective-permute-start(bf16[320,384]{1,0:T(8,128)(2,1)S(1)} %get-tuple-element.299), channel_id=1, source_target_pairs={{8,16},{12,20},{16,8},{20,12},{9,17},{13,21},{17,9},{21,13},{10,18... | collective-permute-start | bytes 737288 | tf_op jit(solution)/shard_map/ppermute | solution.py:169
  121.4 11.6 %collective-permute-start.18 = (bf16[320,384]{1,0:T(8,128)(2,1)S(1)}, bf16[320,384]{1,0:T(8,128)(2,1)S(1)}, u32[]{:S(2)}, u32[]{:S(2)}) collective-permute-start(bf16[320,384]{1,0:T(8,128)(2,1)S(1)} %get-tuple-element.275), channel_id=1, source_target_pairs={{0,8},{4,12},{8,0},{12,4},{16,24},{20,28},{24,16},{28,20},{1,9},{5... | collective-permute-start | bytes 737288 | tf_op jit(solution)/shard_map/ppermute | solution.py:169
  139.9 13.7 %collective-permute-start.24 = (bf16[320,384]{1,0:T(8,128)(2,1)}, bf16[320,384]{1,0:T(8,128)(2,1)}, u32[]{:S(2)}, u32[]{:S(2)}) collective-permute-start(bf16[320,384]{1,0:T(8,128)(2,1)} %get-tuple-element.274), channel_id=1, source_target_pairs={{0,8},{4,12},{8,0},{12,4},{16,24},{20,28},{24,16},{28,20},{1,9},{5... | collective-permute-start | bytes 737288 | tf_op jit(solution)/shard_map/ppermute | solution.py:169
  149.5 96.4 %collective-permute-start.46 = (bf16[640,128]{1,0:T(8,128)(2,1)S(1)}, bf16[640,128]{1,0:T(8,128)(2,1)S(1)}, u32[]{:S(2)}, u32[]{:S(2)}) collective-permute-start(bf16[640,128]{1,0:T(8,128)(2,1)S(1)} %copy-done.20), channel_id=1, source_target_pairs={{0,8},{4,12},{8,0},{12,4},{16,24},{20,28},{24,16},{28,20},{1,9},{5... | collective-permute-start | bytes 491528 | tf_op jit(solution)/shard_map/ppermute | solution.py:169
  152.9 13.0 %collective-permute-start.29 = (bf16[320,384]{1,0:T(8,128)(2,1)}, bf16[320,384]{1,0:T(8,128)(2,1)S(1)}, u32[]{:S(2)}, u32[]{:S(2)}) collective-permute-start(bf16[320,384]{1,0:T(8,128)(2,1)} %get-tuple-element.297), channel_id=1, source_target_pairs={{8,16},{12,20},{16,8},{20,12},{9,17},{13,21},{17,9},{21,13},{10,18... | collective-permute-start | bytes 737288 | tf_op jit(solution)/shard_map/ppermute | solution.py:169
  155.1 12.5 %collective-permute-start.28 = (bf16[320,384]{1,0:T(8,128)(2,1)S(1)}, bf16[320,384]{1,0:T(8,128)(2,1)S(1)}, u32[]{:S(2)}, u32[]{:S(2)}) collective-permute-start(bf16[320,384]{1,0:T(8,128)(2,1)S(1)} %get-tuple-element.271), channel_id=1, source_target_pairs={{0,8},{4,12},{8,0},{12,4},{16,24},{20,28},{24,16},{28,20},{1,9},{5... | collective-permute-start | bytes 737288 | tf_op jit(solution)/shard_map/ppermute | solution.py:169
  165.8 12.0 %collective-permute-start.27 = (bf16[640,128]{1,0:T(8,128)(2,1)S(1)}, bf16[640,128]{1,0:T(8,128)(2,1)S(1)}, u32[]{:S(2)}, u32[]{:S(2)}) collective-permute-start(bf16[640,128]{1,0:T(8,128)(2,1)S(1)} %add_convert_fusion.37), channel_id=1, source_target_pairs={{0,2},{1,3},{2,0},{3,1},{4,6},{5,7},{6,4},{7,5},{8,10},{9,11},{10,... | collective-permute-start | bytes 491528 | tf_op jit(solution)/shard_map/ppermute | solution.py:189
  167.6 11.0 %collective-permute-start.33 = (bf16[320,384]{1,0:T(8,128)(2,1)S(1)}, bf16[320,384]{1,0:T(8,128)(2,1)S(1)}, u32[]{:S(2)}, u32[]{:S(2)}) collective-permute-start(bf16[320,384]{1,0:T(8,128)(2,1)S(1)} %add_convert_fusion.12), channel_id=1, source_target_pairs={{8,16},{12,20},{16,8},{20,12},{9,17},{13,21},{17,9},{21,13},{10,18... | collective-permute-start | bytes 737288 | tf_op jit(solution)/shard_map/ppermute | solution.py:169
  173.4 11.3 %collective-permute-start.32 = (bf16[320,384]{1,0:T(8,128)(2,1)S(1)}, bf16[320,384]{1,0:T(8,128)(2,1)S(1)}, u32[]{:S(2)}, u32[]{:S(2)}) collective-permute-start(bf16[320,384]{1,0:T(8,128)(2,1)S(1)} %get-tuple-element.269), channel_id=1, source_target_pairs={{0,8},{4,12},{8,0},{12,4},{16,24},{20,28},{24,16},{28,20},{1,9},{5... | collective-permute-start | bytes 737288 | tf_op jit(solution)/shard_map/ppermute | solution.py:169
  177.8 10.1 %collective-permute-start.34 = (bf16[320,384]{1,0:T(8,128)(2,1)S(1)}, bf16[320,384]{1,0:T(8,128)(2,1)S(1)}, u32[]{:S(2)}, u32[]{:S(2)}) collective-permute-start(bf16[320,384]{1,0:T(8,128)(2,1)S(1)} %get-tuple-element.270), channel_id=1, source_target_pairs={{0,8},{4,12},{8,0},{12,4},{16,24},{20,28},{24,16},{28,20},{1,9},{5... | collective-permute-start | bytes 737288 | tf_op jit(solution)/shard_map/ppermute | solution.py:169
  184.8 14.5 %collective-permute-start.37 = (bf16[320,384]{1,0:T(8,128)(2,1)S(1)}, bf16[320,384]{1,0:T(8,128)(2,1)S(1)}, u32[]{:S(2)}, u32[]{:S(2)}) collective-permute-start(bf16[320,384]{1,0:T(8,128)(2,1)S(1)} %get-tuple-element.293), channel_id=1, source_target_pairs={{8,16},{12,20},{16,8},{20,12},{9,17},{13,21},{17,9},{21,13},{10,18... | collective-permute-start | bytes 737288 | tf_op jit(solution)/shard_map/ppermute | solution.py:169
  188.1 14.3 %collective-permute-start.36 = (bf16[320,384]{1,0:T(8,128)(2,1)S(1)}, bf16[320,384]{1,0:T(8,128)(2,1)S(1)}, u32[]{:S(2)}, u32[]{:S(2)}) collective-permute-start(bf16[320,384]{1,0:T(8,128)(2,1)S(1)} %get-tuple-element.295), channel_id=1, source_target_pairs={{0,8},{4,12},{8,0},{12,4},{16,24},{20,28},{24,16},{28,20},{1,9},{5... | collective-permute-start | bytes 737288 | tf_op jit(solution)/shard_map/ppermute | solution.py:169
  202.4 11.6 %collective-permute-start.41 = (bf16[320,384]{1,0:T(8,128)(2,1)S(1)}, bf16[320,384]{1,0:T(8,128)(2,1)S(1)}, u32[]{:S(2)}, u32[]{:S(2)}) collective-permute-start(bf16[320,384]{1,0:T(8,128)(2,1)S(1)} %collective-permute-done.36), channel_id=1, source_target_pairs={{8,16},{12,20},{16,8},{20,12},{9,17},{13,21},{17,9},{21,13},{10,18... | collective-permute-start | bytes 737288 | tf_op jit(solution)/shard_map/ppermute | solution.py:169
  205.6 17.5 %collective-permute-start.43 = (bf16[320,384]{1,0:T(8,128)(2,1)S(1)}, bf16[320,384]{1,0:T(8,128)(2,1)S(1)}, u32[]{:S(2)}, u32[]{:S(2)}) collective-permute-start(bf16[320,384]{1,0:T(8,128)(2,1)S(1)} %collective-permute-done.38), channel_id=1, source_target_pairs={{8,16},{12,20},{16,8},{20,12},{9,17},{13,21},{17,9},{21,13},{10,18... | collective-permute-start | bytes 737288 | tf_op jit(solution)/shard_map/ppermute | solution.py:169
  206.5 12.6 %collective-permute-start.40 = (bf16[320,384]{1,0:T(8,128)(2,1)S(1)}, bf16[320,384]{1,0:T(8,128)(2,1)S(1)}, u32[]{:S(2)}, u32[]{:S(2)}) collective-permute-start(bf16[320,384]{1,0:T(8,128)(2,1)S(1)} %get-tuple-element.291), channel_id=1, source_target_pairs={{0,8},{4,12},{8,0},{12,4},{16,24},{20,28},{24,16},{28,20},{1,9},{5... | collective-permute-start | bytes 737288 | tf_op jit(solution)/shard_map/ppermute | solution.py:169
  219.1 15.5 %collective-permute-start.48 = (bf16[320,384]{1,0:T(8,128)(2,1)S(1)}, bf16[320,384]{1,0:T(8,128)(2,1)S(1)}, u32[]{:S(2)}, u32[]{:S(2)}) collective-permute-start(bf16[320,384]{1,0:T(8,128)(2,1)S(1)} %collective-permute-done.40), channel_id=1, source_target_pairs={{8,16},{12,20},{16,8},{20,12},{9,17},{13,21},{17,9},{21,13},{10,18... | collective-permute-start | bytes 737288 | tf_op jit(solution)/shard_map/ppermute | solution.py:169
  223.1 17.1 %collective-permute-start.52 = (bf16[320,384]{1,0:T(8,128)(2,1)S(1)}, bf16[320,384]{1,0:T(8,128)(2,1)S(1)}, u32[]{:S(2)}, u32[]{:S(2)}) collective-permute-start(bf16[320,384]{1,0:T(8,128)(2,1)S(1)} %collective-permute-done.42), channel_id=1, source_target_pairs={{8,16},{12,20},{16,8},{20,12},{9,17},{13,21},{17,9},{21,13},{10,18... | collective-permute-start | bytes 737288 | tf_op jit(solution)/shard_map/ppermute | solution.py:169
  232.3 13.7 %collective-permute-start.45 = (bf16[640,128]{1,0:T(8,128)(2,1)S(1)}, bf16[640,128]{1,0:T(8,128)(2,1)S(1)}, u32[]{:S(2)}, u32[]{:S(2)}) collective-permute-start(bf16[640,128]{1,0:T(8,128)(2,1)S(1)} %add_convert_fusion.36), channel_id=1, source_target_pairs={{0,2},{1,3},{2,0},{3,1},{4,6},{5,7},{6,4},{7,5},{8,10},{9,11},{10,... | collective-permute-start | bytes 491528 | tf_op jit(solution)/shard_map/ppermute | solution.py:189
  234.6 15.9 %collective-permute-start.50 = (bf16[320,384]{1,0:T(8,128)(2,1)S(1)}, bf16[320,384]{1,0:T(8,128)(2,1)S(1)}, u32[]{:S(2)}, u32[]{:S(2)}) collective-permute-start(bf16[320,384]{1,0:T(8,128)(2,1)S(1)} %collective-permute-done.47), channel_id=1, source_target_pairs={{8,16},{12,20},{16,8},{20,12},{9,17},{13,21},{17,9},{21,13},{10,18... | collective-permute-start | bytes 737288 | tf_op jit(solution)/shard_map/ppermute | solution.py:169
  240.3 14.0 %collective-permute-start.56 = (bf16[320,384]{1,0:T(8,128)(2,1)S(1)}, bf16[320,384]{1,0:T(8,128)(2,1)S(1)}, u32[]{:S(2)}, u32[]{:S(2)}) collective-permute-start(bf16[320,384]{1,0:T(8,128)(2,1)S(1)} %collective-permute-done.51), channel_id=1, source_target_pairs={{8,16},{12,20},{16,8},{20,12},{9,17},{13,21},{17,9},{21,13},{10,18... | collective-permute-start | bytes 737288 | tf_op jit(solution)/shard_map/ppermute | solution.py:169
  254.4 17.9 %collective-permute-start.58 = (bf16[320,384]{1,0:T(8,128)(2,1)S(1)}, bf16[320,384]{1,0:T(8,128)(2,1)S(1)}, u32[]{:S(2)}, u32[]{:S(2)}) collective-permute-start(bf16[320,384]{1,0:T(8,128)(2,1)S(1)} %collective-permute-done.55), channel_id=1, source_target_pairs={{8,16},{12,20},{16,8},{20,12},{9,17},{13,21},{17,9},{21,13},{10,18... | collective-permute-start | bytes 737288 | tf_op jit(solution)/shard_map/ppermute | solution.py:169
  255.1 10.7 %collective-permute-start.54 = (bf16[320,384]{1,0:T(8,128)(2,1)S(1)}, bf16[320,384]{1,0:T(8,128)(2,1)S(1)}, u32[]{:S(2)}, u32[]{:S(2)}) collective-permute-start(bf16[320,384]{1,0:T(8,128)(2,1)S(1)} %collective-permute-done.49), channel_id=1, source_target_pairs={{8,16},{12,20},{16,8},{20,12},{9,17},{13,21},{17,9},{21,13},{10,18... | collective-permute-start | bytes 737288 | tf_op jit(solution)/shard_map/ppermute | solution.py:169
  256.3 15.9 %collective-permute-start.57 = (bf16[320,384]{1,0:T(8,128)(2,1)S(1)}, bf16[320,384]{1,0:T(8,128)(2,1)S(1)}, u32[]{:S(2)}, u32[]{:S(2)}) collective-permute-start(bf16[320,384]{1,0:T(8,128)(2,1)S(1)} %get-tuple-element.355), channel_id=1, source_target_pairs={{0,8},{4,12},{8,0},{12,4},{16,24},{20,28},{24,16},{28,20},{1,9},{5... | collective-permute-start | bytes 737288 | tf_op jit(solution)/shard_map/ppermute | solution.py:169
  272.3 15.6 %collective-permute-start.60 = (bf16[320,384]{1,0:T(8,128)(2,1)S(1)}, bf16[320,384]{1,0:T(8,128)(2,1)S(1)}, u32[]{:S(2)}, u32[]{:S(2)}) collective-permute-start(bf16[320,384]{1,0:T(8,128)(2,1)S(1)} %collective-permute-done.57), channel_id=1, source_target_pairs={{8,16},{12,20},{16,8},{20,12},{9,17},{13,21},{17,9},{21,13},{10,18... | collective-permute-start | bytes 737288 | tf_op jit(solution)/shard_map/ppermute | solution.py:169
  272.9 12.3 %collective-permute-start.62 = (bf16[320,384]{1,0:T(8,128)(2,1)S(1)}, bf16[320,384]{1,0:T(8,128)(2,1)S(1)}, u32[]{:S(2)}, u32[]{:S(2)}) collective-permute-start(bf16[320,384]{1,0:T(8,128)(2,1)S(1)} %collective-permute-done.53), channel_id=1, source_target_pairs={{8,16},{12,20},{16,8},{20,12},{9,17},{13,21},{17,9},{21,13},{10,18... | collective-permute-start | bytes 737288 | tf_op jit(solution)/shard_map/ppermute | solution.py:169
  273.8 11.4 %collective-permute-start.61 = (bf16[320,384]{1,0:T(8,128)(2,1)S(1)}, bf16[320,384]{1,0:T(8,128)(2,1)S(1)}, u32[]{:S(2)}, u32[]{:S(2)}) collective-permute-start(bf16[320,384]{1,0:T(8,128)(2,1)S(1)} %broadcast_select_fusion.28), channel_id=1, source_target_pairs={{0,8},{4,12},{8,0},{12,4},{16,24},{20,28},{24,16},{28,20},{1,9},{5... | collective-permute-start | bytes 737288 | tf_op jit(solution)/shard_map/ppermute | solution.py:169
  287.9 14.5 %collective-permute-start.70 = (bf16[320,384]{1,0:T(8,128)(2,1)S(1)}, bf16[320,384]{1,0:T(8,128)(2,1)S(1)}, u32[]{:S(2)}, u32[]{:S(2)}) collective-permute-start(bf16[320,384]{1,0:T(8,128)(2,1)S(1)} %collective-permute-done.59), channel_id=1, source_target_pairs={{8,16},{12,20},{16,8},{20,12},{9,17},{13,21},{17,9},{21,13},{10,18... | collective-permute-start | bytes 737288 | tf_op jit(solution)/shard_map/ppermute | solution.py:169
  288.6 14.6 %collective-permute-start.64 = (bf16[320,384]{1,0:T(8,128)(2,1)S(1)}, bf16[320,384]{1,0:T(8,128)(2,1)S(1)}, u32[]{:S(2)}, u32[]{:S(2)}) collective-permute-start(bf16[320,384]{1,0:T(8,128)(2,1)S(1)} %collective-permute-done.61), channel_id=1, source_target_pairs={{8,16},{12,20},{16,8},{20,12},{9,17},{13,21},{17,9},{21,13},{10,18... | collective-permute-start | bytes 737288 | tf_op jit(solution)/shard_map/ppermute | solution.py:169
  289.3 13.8 %collective-permute-start.63 = (bf16[320,384]{1,0:T(8,128)(2,1)S(1)}, bf16[320,384]{1,0:T(8,128)(2,1)S(1)}, u32[]{:S(2)}, u32[]{:S(2)}) collective-permute-start(bf16[320,384]{1,0:T(8,128)(2,1)S(1)} %broadcast_select_fusion.23), channel_id=1, source_target_pairs={{0,8},{4,12},{8,0},{12,4},{16,24},{20,28},{24,16},{28,20},{1,9},{5... | collective-permute-start | bytes 737288 | tf_op jit(solution)/shard_map/ppermute | solution.py:169
  302.4 11.8 %collective-permute-start.72 = (bf16[320,384]{1,0:T(8,128)(2,1)S(1)}, bf16[320,384]{1,0:T(8,128)(2,1)S(1)}, u32[]{:S(2)}, u32[]{:S(2)}) collective-permute-start(bf16[320,384]{1,0:T(8,128)(2,1)S(1)} %collective-permute-done.69), channel_id=1, source_target_pairs={{8,16},{12,20},{16,8},{20,12},{9,17},{13,21},{17,9},{21,13},{10,18... | collective-permute-start | bytes 737288 | tf_op jit(solution)/shard_map/ppermute | solution.py:169
  303.2 15.7 %collective-permute-start.66 = (bf16[320,384]{1,0:T(8,128)(2,1)S(1)}, bf16[320,384]{1,0:T(8,128)(2,1)S(1)}, u32[]{:S(2)}, u32[]{:S(2)}) collective-permute-start(bf16[320,384]{1,0:T(8,128)(2,1)S(1)} %collective-permute-done.63), channel_id=1, source_target_pairs={{8,16},{12,20},{16,8},{20,12},{9,17},{13,21},{17,9},{21,13},{10,18... | collective-permute-start | bytes 737288 | tf_op jit(solution)/shard_map/ppermute | solution.py:169
  304.0 10.8 %collective-permute-start.71 = (bf16[320,384]{1,0:T(8,128)(2,1)S(1)}, bf16[320,384]{1,0:T(8,128)(2,1)S(1)}, u32[]{:S(2)}, u32[]{:S(2)}) collective-permute-start(bf16[320,384]{1,0:T(8,128)(2,1)S(1)} %broadcast_select_fusion.16), channel_id=1, source_target_pairs={{0,8},{4,12},{8,0},{12,4},{16,24},{20,28},{24,16},{28,20},{1,9},{5... | collective-permute-start | bytes 737288 | tf_op jit(solution)/shard_map/ppermute | solution.py:169
  311.9 32.4 %collective-permute-start.80 = (bf16[768,384]{1,0:T(8,128)(2,1)S(1)}, bf16[768,384]{1,0:T(8,128)(2,1)S(1)}, u32[]{:S(2)}, u32[]{:S(2)}) collective-permute-start(bf16[768,384]{1,0:T(8,128)(2,1)S(1)} %add_convert_fusion), channel_id=1, source_target_pairs={{0,4},{4,0},{8,12},{12,8},{16,20},{20,16},{24,28},{28,24},{1,5},{5... | collective-permute-start | bytes 1769480 | tf_op jit(solution)/shard_map/ppermute | solution.py:183
  314.7 17.6 %collective-permute-start.74 = (bf16[320,384]{1,0:T(8,128)(2,1)S(1)}, bf16[320,384]{1,0:T(8,128)(2,1)S(1)}, u32[]{:S(2)}, u32[]{:S(2)}) collective-permute-start(bf16[320,384]{1,0:T(8,128)(2,1)S(1)} %collective-permute-done.71), channel_id=1, source_target_pairs={{8,16},{12,20},{16,8},{20,12},{9,17},{13,21},{17,9},{21,13},{10,18... | collective-permute-start | bytes 737288 | tf_op jit(solution)/shard_map/ppermute | solution.py:169
  319.0 15.4 %collective-permute-start.68 = (bf16[320,384]{1,0:T(8,128)(2,1)S(1)}, bf16[320,384]{1,0:T(8,128)(2,1)S(1)}, u32[]{:S(2)}, u32[]{:S(2)}) collective-permute-start(bf16[320,384]{1,0:T(8,128)(2,1)S(1)} %collective-permute-done.65), channel_id=1, source_target_pairs={{8,16},{12,20},{16,8},{20,12},{9,17},{13,21},{17,9},{21,13},{10,18... | collective-permute-start | bytes 737288 | tf_op jit(solution)/shard_map/ppermute | solution.py:169
  319.7 11.5 %collective-permute-start.73 = (bf16[320,384]{1,0:T(8,128)(2,1)S(1)}, bf16[320,384]{1,0:T(8,128)(2,1)S(1)}, u32[]{:S(2)}, u32[]{:S(2)}) collective-permute-start(bf16[320,384]{1,0:T(8,128)(2,1)S(1)} %pad_select_fusion), channel_id=1, source_target_pairs={{0,8},{4,12},{8,0},{12,4},{16,24},{20,28},{24,16},{28,20},{1,9},{5... | collective-permute-start | bytes 737288 | tf_op jit(solution)/shard_map/ppermute | solution.py:169
  331.2 17.3 %collective-permute-start.79 = (bf16[768,384]{1,0:T(8,128)(2,1)S(1)}, bf16[768,384]{1,0:T(8,128)(2,1)S(1)}, u32[]{:S(2)}, u32[]{:S(2)}) collective-permute-start(bf16[768,384]{1,0:T(8,128)(2,1)S(1)} %add_convert_fusion.1), channel_id=1, source_target_pairs={{0,4},{4,0},{8,12},{12,8},{16,20},{20,16},{24,28},{28,24},{1,5},{5... | collective-permute-start | bytes 1769480 | tf_op jit(solution)/shard_map/ppermute | solution.py:183
  338.7 16.4 %collective-permute-start.78 = (bf16[768,384]{1,0:T(8,128)(2,1)S(1)}, bf16[768,384]{1,0:T(8,128)(2,1)S(1)}, u32[]{:S(2)}, u32[]{:S(2)}) collective-permute-start(bf16[768,384]{1,0:T(8,128)(2,1)S(1)} %add_convert_fusion.2), channel_id=1, source_target_pairs={{0,4},{4,0},{8,12},{12,8},{16,20},{20,16},{24,28},{28,24},{1,5},{5... | collective-permute-start | bytes 1769480 | tf_op jit(solution)/shard_map/ppermute | solution.py:183
  342.4 18.9 %collective-permute-start.77 = (bf16[768,384]{1,0:T(8,128)(2,1)S(1)}, bf16[768,384]{1,0:T(8,128)(2,1)S(1)}, u32[]{:S(2)}, u32[]{:S(2)}) collective-permute-start(bf16[768,384]{1,0:T(8,128)(2,1)S(1)} %add_convert_fusion.3), channel_id=1, source_target_pairs={{0,4},{4,0},{8,12},{12,8},{16,20},{20,16},{24,28},{28,24},{1,5},{5... | collective-permute-start | bytes 1769480 | tf_op jit(solution)/shard_map/ppermute | solution.py:183
  (73 other events, 545.8 us)

commit v3 on v2

--- a/solution.py
+++ b/solution.py
@@ -310,9 +310,8 @@
         (0, 0): [(0, 1, 0), "scales", "features"],
         (0, late): [(1, 0, 0), (1, 1, 0)],
         (1, late): [(0, 0, 1)],
-        (2, late): [(0, 1, 1)],
-        (3, late): [(1, 0, 1)],
-        (4, late): [(1, 1, 1)],
+        (2, 0): [(0, 1, 1)],
+        (2, late): [(1, 0, 1), (1, 1, 1)],
     }
     for tick, part in [(t, p) for t in range(2 * units + line) for p in range(streams)]:
         back_tick = tick - units
@@ -330,7 +329,7 @@
                     delta[key] = value
                 elif box == "early":
                     early[key] = value
-                else:
+                elif box == "scales":
                     scales = all_scales(value)
 
         from_end = from_middle = None
@@ -350,6 +349,8 @@
         else:
             payload = jnp.where(at_end, from_end, from_middle)
         if payload is not None:
+            if tick < units + 2:
+                pending["sent", "end"] = payload
             ends[part, tick] = swap_end(payload)
         if 1 <= tick < units + 1:
             payload = (wide(sums_of(tick - 1, 0, parts[part])) + wide(was_end)).astype(jnp.bfloat16)
@@ -357,6 +358,8 @@
         elif 1 <= back_tick < units + 1:
             middles[part, tick] = swap_middle(was_end)
 
+        if payload is not None and tick < 99:
+            pending["sent", "last"] = payload
         for work in side_work.get((tick, part), ()):
             if work == "scales":
                 pending["scales", None] = local_scales()
@@ -380,11 +383,7 @@
 
         unit = back_tick + 1
         if 0 <= unit < units:
-            value = new_delta(part, unit, was_end)
-            if unit % pieces:
-                pending["delta", (part, unit)] = value
-            else:
-                delta[part, unit] = value
+            pending["delta", (part, unit)] = new_delta(part, unit, was_end)
 
         unit = back_tick - line + 1
         if 0 <= unit < units and part == streams - 1:

time: 369 us -> 319 us (0.86)
  waiting for transfers between devices: 115 us -> 59.8 us
  starting transfers between devices: 144 us -> 148 us
    ppermute x69, waiting for transfers between devices: 94.3 us -> 25.7 us  [swap(): return lax.ppermute(value, 'dp', pairs)]
    ppermute x6, waiting for transfers between devices: 7.8 us -> 16 us  [turn(): return lax.ppermute(value, 'dp', pairs)]
    ppermute x6, waiting for transfers between devices: 2.74 us -> 9 us  [mp_sum(): lax.ppermute(value, 'mp', [(m, m ^ step) for m in range(model_count)])]
    ppermute x69, starting transfers between devices: 124 us -> 129 us  [swap(): return lax.ppermute(value, 'dp', pairs)]
  transfers between devices with their start and end apart: 82 -> 82, of which waited for: 33 -> 20; matrix products, arithmetic and copies ran while one was open for 19% -> 24% of each run, Pallas kernels for 2% -> 3%
where the time goes in v3:
time: 319 us; the launch traced here: 314 us
  starting transfers between devices  148 us (46%)
  waiting for transfers between devices  59.8 us (19%)
  matrix products  55.4 us (17%)
  other arithmetic  15.5 us (5%)
  local copies, waits for them, and re-layouts  13 us (4%)
  Pallas kernels  11.7 us (4%)
  blocking collectives  8.07 us (3%)
  between operations  3.33 us (1%)
    ppermute x69, starting transfers between devices, swap(): return lax.ppermute(value, 'dp', pairs)  129 us
    dot_general x21, matrix products, dot32(): return jnp.dot(left, right, preferred_element_type=jnp.float32)  30.8 us
    ppermute x69, waiting for transfers between devices, swap(): return lax.ppermute(value, 'dp', pairs)  25.7 us
    dot_general x12, matrix products, gradient_term(): lax.dot_general(features[unit // pieces][:, rows], jnp.concatenate(arrive...  18.7 us
    ppermute x6, waiting for transfers between devices, turn(): return lax.ppermute(value, 'dp', pairs)  16 us
    pallas_call x4, Pallas kernels, adam_piece(): pl.pallas_call(adam_kernel, grid=(3,), in_specs=[piece, piece, column, co...  11.7 us
    all_to_all x1, waiting for transfers between devices, route(): lax.all_to_all(outgoing.reshape(devices_all, line * lot, patch_width), ('...  9.05 us
    ppermute x6, waiting for transfers between devices, mp_sum(): lax.ppermute(value, 'mp', [(m, m ^ step) for m in range(model_count)])  9 us
  transfers between devices with their start and end apart: 82, of which 20 were waited for; matrix products, arithmetic and copies ran while one was open for 24% of the time, Pallas kernels for 3%

profile of v3, /device:TPU:0, one launch (start us, length us, event | category | flops | bytes accessed | tf_op | source)
XLA Modules:
  0.0 314.2 jit_solution(2476112246482111303)
XLA Ops:
  1.4 2.6 convert.14
  8.0 7.3 %all-to-all-start = ((bf16[32,64,128]{2,1,0:T(8,128)(2,1)}), bf16[32,64,128]{2,1,0:T(8,128)(2,1)S(1)}, u32[]{:S(2)}, u32[]{:S(2)}) async-start(bf16[32,64,128]{2,1,0:T(8,128)(2,1)} %bitcast.4), calls=%async_computation | async-start | bytes 1048576 | tf_op jit(solution)/shard_map/all_to_all | solution.py:74
  21.8 9.1 %all-to-all-done = bf16[32,64,128]{2,1,0:T(8,128)(2,1)S(1)} async-done(((bf16[32,64,128]{2,1,0:T(8,128)(2,1)}), bf16[32,64,128]{2,1,0:T(8,128)(2,1)S(1)}, u32[]{:S(2)}, u32[]{:S(2)}) %all-to-all-start) | async-done | bytes 524320 | tf_op jit(solution)/shard_map/all_to_all | solution.py:74
  32.2 8.1 %all_gather.3 = bf16[4,640,128]{2,1,0:T(8,128)(2,1)S(1)} all-gather(bf16[4,160,128]{2,1,0:T(8,128)(2,1)S(1)} %bitcast.75), channel_id=1, replica_groups=mesh['dp'=8,'mp'=4] {'mp'}, dimensions={1}, use_global_device_ids=true | all-gather | bytes 819200 | tf_op jit(solution)/shard_map/all_gather | solution.py:216
  40.3 3.5 %fusion.3 = f32[320]{0:T(512)S(1)} fusion(bf16[128,6144]{1,0:T(8,128)(2,1)S(1)} %copy-done.9, bf16[160,128]{1,0:T(8,128)(2,1)S(1)} %get-tuple-element.341, bf16[160,128]{1,0:T(8,128)(2,1)S(1)} %get-tuple-element.342), kind=kOutput, calls=%fused_computation.6 | convolution fusion | flops 521174720 | bytes 1656064 | tf_op jit(solution)/shard_map/dot_general | solution.py:37
  43.8 2.9 fusion.5
  46.8 2.9 fusion.1
  60.0 2.6 fusion.39
  65.8 2.7 collective-permute-done.1
  69.8 3.9 %collective-permute-done.4 = bf16[320,384]{1,0:T(8,128)(2,1)} collective-permute-done((bf16[320,384]{1,0:T(8,128)(2,1)}, bf16[320,384]{1,0:T(8,128)(2,1)}, u32[]{:S(2)}, u32[]{:S(2)}) %collective-permute-start.4) | collective-permute-done | bytes 245792 | tf_op jit(solution)/shard_map/ppermute | solution.py:169
  78.7 5.2 %collective-permute-done.5 = bf16[768,768]{1,0:T(8,128)(2,1)} collective-permute-done((bf16[768,768]{1,0:T(8,128)(2,1)S(1)}, bf16[768,768]{1,0:T(8,128)(2,1)}, u32[]{:S(2)}, u32[]{:S(2)}) %collective-permute-start.5) | collective-permute-done | bytes 1179680 | tf_op jit(solution)/shard_map/ppermute | solution.py:183
  84.7 2.4 constant_dynamic-update-slice_fusion.2
  87.1 4.1 %fusion.27 = bf16[640,768]{1,0:T(8,128)(2,1)S(1)} fusion(bf16[1536,768]{1,0:T(8,128)(2,1)} %constant_dynamic-update-slice_fusion.2, bf16[1280,1536]{1,0:T(8,128)(2,1)} %copy-done.15), kind=kOutput, calls=%fused_computation.37 | convolution fusion | flops 1510440960 | bytes 5308416 | tf_op jit(solution)/shard_map/dot_general | solution.py:37
  92.1 5.3 %collective-permute-start.6 = (bf16[320,384]{1,0:T(8,128)(2,1)S(1)}, bf16[320,384]{1,0:T(8,128)(2,1)S(1)}, u32[]{:S(2)}, u32[]{:S(2)}) collective-permute-start(bf16[320,384]{1,0:T(8,128)(2,1)S(1)} %fusion.176), channel_id=1, source_target_pairs={{0,8},{4,12},{8,0},{12,4},{16,24},{20,28},{24,16},{28,20},{1,9},{5... | collective-permute-start | bytes 737288 | tf_op jit(solution)/shard_map/ppermute | solution.py:169
  105.4 6.6 %collective-permute-start.14 = (bf16[320,384]{1,0:T(8,128)(2,1)S(1)}, bf16[320,384]{1,0:T(8,128)(2,1)S(1)}, u32[]{:S(2)}, u32[]{:S(2)}) collective-permute-start(bf16[320,384]{1,0:T(8,128)(2,1)S(1)} %fusion.178), channel_id=1, source_target_pairs={{0,8},{4,12},{8,0},{12,4},{16,24},{20,28},{24,16},{28,20},{1,9},{5... | collective-permute-start | bytes 737288 | tf_op jit(solution)/shard_map/ppermute | solution.py:169
  112.8 3.6 %collective-permute-start.16 = (bf16[320,384]{1,0:T(8,128)(2,1)S(1)}, bf16[320,384]{1,0:T(8,128)(2,1)S(1)}, u32[]{:S(2)}, u32[]{:S(2)}) collective-permute-start(bf16[320,384]{1,0:T(8,128)(2,1)S(1)} %fusion.179), channel_id=1, source_target_pairs={{0,8},{4,12},{8,0},{12,4},{16,24},{20,28},{24,16},{28,20},{1,9},{5... | collective-permute-start | bytes 737288 | tf_op jit(solution)/shard_map/ppermute | solution.py:169
  119.4 4.3 %collective-permute-start.18 = (bf16[320,384]{1,0:T(8,128)(2,1)S(1)}, bf16[320,384]{1,0:T(8,128)(2,1)S(1)}, u32[]{:S(2)}, u32[]{:S(2)}) collective-permute-start(bf16[320,384]{1,0:T(8,128)(2,1)S(1)} %fusion.180), channel_id=1, source_target_pairs={{0,8},{4,12},{8,0},{12,4},{16,24},{20,28},{24,16},{28,20},{1,9},{5... | collective-permute-start | bytes 737288 | tf_op jit(solution)/shard_map/ppermute | solution.py:169
  126.0 3.1 collective-permute-done.18
  129.9 4.6 %collective-permute-start.22 = (bf16[320,384]{1,0:T(8,128)(2,1)S(1)}, bf16[320,384]{1,0:T(8,128)(2,1)S(1)}, u32[]{:S(2)}, u32[]{:S(2)}) collective-permute-start(bf16[320,384]{1,0:T(8,128)(2,1)S(1)} %fusion.182), channel_id=1, source_target_pairs={{0,8},{4,12},{8,0},{12,4},{16,24},{20,28},{24,16},{28,20},{1,9},{5... | collective-permute-start | bytes 737288 | tf_op jit(solution)/shard_map/ppermute | solution.py:169
  135.4 4.5 %collective-permute-start.24 = (bf16[320,384]{1,0:T(8,128)(2,1)S(1)}, bf16[320,384]{1,0:T(8,128)(2,1)S(1)}, u32[]{:S(2)}, u32[]{:S(2)}) collective-permute-start(bf16[320,384]{1,0:T(8,128)(2,1)S(1)} %fusion.183), channel_id=1, source_target_pairs={{0,8},{4,12},{8,0},{12,4},{16,24},{20,28},{24,16},{28,20},{1,9},{5... | collective-permute-start | bytes 737288 | tf_op jit(solution)/shard_map/ppermute | solution.py:169
  140.7 4.6 %collective-permute-start.28 = (bf16[320,384]{1,0:T(8,128)(2,1)S(1)}, bf16[320,384]{1,0:T(8,128)(2,1)S(1)}, u32[]{:S(2)}, u32[]{:S(2)}) collective-permute-start(bf16[320,384]{1,0:T(8,128)(2,1)S(1)} %fusion.184), channel_id=1, source_target_pairs={{0,8},{4,12},{8,0},{12,4},{16,24},{20,28},{24,16},{28,20},{1,9},{5... | collective-permute-start | bytes 737288 | tf_op jit(solution)/shard_map/ppermute | solution.py:169
  153.2 4.0 %collective-permute-done.27 = bf16[640,128]{1,0:T(8,128)(2,1)S(1)} collective-permute-done((bf16[640,128]{1,0:T(8,128)(2,1)S(1)}, bf16[640,128]{1,0:T(8,128)(2,1)S(1)}, u32[]{:S(2)}, u32[]{:S(2)}) %collective-permute-start.27) | collective-permute-done | bytes 163872 | tf_op jit(solution)/shard_map/ppermute | solution.py:189
  157.2 3.1 collective-permute-start.32
  162.8 2.5 collective-permute-start.34
  167.1 3.9 %collective-permute-start.36 = (bf16[320,384]{1,0:T(8,128)(2,1)S(1)}, bf16[320,384]{1,0:T(8,128)(2,1)S(1)}, u32[]{:S(2)}, u32[]{:S(2)}) collective-permute-start(bf16[320,384]{1,0:T(8,128)(2,1)S(1)} %fusion.188), channel_id=1, source_target_pairs={{0,8},{4,12},{8,0},{12,4},{16,24},{20,28},{24,16},{28,20},{1,9},{5... | collective-permute-start | bytes 737288 | tf_op jit(solution)/shard_map/ppermute | solution.py:169
  175.0 2.8 collective-permute-done.36
  178.6 4.5 %collective-permute-start.40 = (bf16[320,384]{1,0:T(8,128)(2,1)S(1)}, bf16[320,384]{1,0:T(8,128)(2,1)S(1)}, u32[]{:S(2)}, u32[]{:S(2)}) collective-permute-start(bf16[320,384]{1,0:T(8,128)(2,1)S(1)} %fusion.190), channel_id=1, source_target_pairs={{0,8},{4,12},{8,0},{12,4},{16,24},{20,28},{24,16},{28,20},{1,9},{5... | collective-permute-start | bytes 737288 | tf_op jit(solution)/shard_map/ppermute | solution.py:169
  184.3 3.4 %collective-permute-start.42 = (bf16[320,384]{1,0:T(8,128)(2,1)S(1)}, bf16[320,384]{1,0:T(8,128)(2,1)S(1)}, u32[]{:S(2)}, u32[]{:S(2)}) collective-permute-start(bf16[320,384]{1,0:T(8,128)(2,1)S(1)} %fusion.191), channel_id=1, source_target_pairs={{0,8},{4,12},{8,0},{12,4},{16,24},{20,28},{24,16},{28,20},{1,9},{5... | collective-permute-start | bytes 737288 | tf_op jit(solution)/shard_map/ppermute | solution.py:169
  190.7 4.2 %collective-permute-start.49 = (bf16[320,384]{1,0:T(8,128)(2,1)S(1)}, bf16[320,384]{1,0:T(8,128)(2,1)S(1)}, u32[]{:S(2)}, u32[]{:S(2)}) collective-permute-start(bf16[320,384]{1,0:T(8,128)(2,1)S(1)} %broadcast_select_fusion.43), channel_id=1, source_target_pairs={{0,8},{4,12},{8,0},{12,4},{16,24},{20,28},{24,16},{28,20},{1,9},{5... | collective-permute-start | bytes 737288 | tf_op jit(solution)/shard_map/ppermute | solution.py:169
  196.6 4.1 %collective-permute-start.46 = (bf16[320,384]{1,0:T(8,128)(2,1)S(1)}, bf16[320,384]{1,0:T(8,128)(2,1)S(1)}, u32[]{:S(2)}, u32[]{:S(2)}) collective-permute-start(bf16[320,384]{1,0:T(8,128)(2,1)S(1)} %broadcast_select_fusion.42), channel_id=1, source_target_pairs={{0,8},{4,12},{8,0},{12,4},{16,24},{20,28},{24,16},{28,20},{1,9},{5... | collective-permute-start | bytes 737288 | tf_op jit(solution)/shard_map/ppermute | solution.py:169
  207.4 3.2 %collective-permute-done.45 = bf16[640,128]{1,0:T(8,128)(2,1)S(1)} collective-permute-done((bf16[640,128]{1,0:T(8,128)(2,1)S(1)}, bf16[640,128]{1,0:T(8,128)(2,1)S(1)}, u32[]{:S(2)}, u32[]{:S(2)}) %collective-permute-start.45) | collective-permute-done | bytes 163872 | tf_op jit(solution)/shard_map/ppermute | solution.py:189
  212.7 4.2 %collective-permute-start.55 = (bf16[320,384]{1,0:T(8,128)(2,1)S(1)}, bf16[320,384]{1,0:T(8,128)(2,1)S(1)}, u32[]{:S(2)}, u32[]{:S(2)}) collective-permute-start(bf16[320,384]{1,0:T(8,128)(2,1)S(1)} %broadcast_select_fusion.36), channel_id=1, source_target_pairs={{0,8},{4,12},{8,0},{12,4},{16,24},{20,28},{24,16},{28,20},{1,9},{5... | collective-permute-start | bytes 737288 | tf_op jit(solution)/shard_map/ppermute | solution.py:169
  223.8 3.1 %collective-permute-start.57 = (bf16[320,384]{1,0:T(8,128)(2,1)S(1)}, bf16[320,384]{1,0:T(8,128)(2,1)S(1)}, u32[]{:S(2)}, u32[]{:S(2)}) collective-permute-start(bf16[320,384]{1,0:T(8,128)(2,1)S(1)} %broadcast_select_fusion.30), channel_id=1, source_target_pairs={{0,8},{4,12},{8,0},{12,4},{16,24},{20,28},{24,16},{28,20},{1,9},{5... | collective-permute-start | bytes 737288 | tf_op jit(solution)/shard_map/ppermute | solution.py:169
  230.3 3.5 %collective-permute-start.61 = (bf16[320,384]{1,0:T(8,128)(2,1)S(1)}, bf16[320,384]{1,0:T(8,128)(2,1)S(1)}, u32[]{:S(2)}, u32[]{:S(2)}) collective-permute-start(bf16[320,384]{1,0:T(8,128)(2,1)S(1)} %broadcast_select_fusion.29), channel_id=1, source_target_pairs={{0,8},{4,12},{8,0},{12,4},{16,24},{20,28},{24,16},{28,20},{1,9},{5... | collective-permute-start | bytes 737288 | tf_op jit(solution)/shard_map/ppermute | solution.py:169
  235.0 4.1 %collective-permute-start.59 = (bf16[320,384]{1,0:T(8,128)(2,1)S(1)}, bf16[320,384]{1,0:T(8,128)(2,1)S(1)}, u32[]{:S(2)}, u32[]{:S(2)}) collective-permute-start(bf16[320,384]{1,0:T(8,128)(2,1)S(1)} %broadcast_select_fusion.28), channel_id=1, source_target_pairs={{0,8},{4,12},{8,0},{12,4},{16,24},{20,28},{24,16},{28,20},{1,9},{5... | collective-permute-start | bytes 737288 | tf_op jit(solution)/shard_map/ppermute | solution.py:169
  239.2 2.2 fusion.124
  245.5 4.2 %collective-permute-start.67 = (bf16[320,384]{1,0:T(8,128)(2,1)S(1)}, bf16[320,384]{1,0:T(8,128)(2,1)S(1)}, u32[]{:S(2)}, u32[]{:S(2)}) collective-permute-start(bf16[320,384]{1,0:T(8,128)(2,1)S(1)} %broadcast_select_fusion.18), channel_id=1, source_target_pairs={{0,8},{4,12},{8,0},{12,4},{16,24},{20,28},{24,16},{28,20},{1,9},{5... | collective-permute-start | bytes 737288 | tf_op jit(solution)/shard_map/ppermute | solution.py:169
  249.7 2.2 fusion.132
  253.7 2.9 collective-permute-done.67
  257.4 4.5 %collective-permute-start.71 = (bf16[320,384]{1,0:T(8,128)(2,1)S(1)}, bf16[320,384]{1,0:T(8,128)(2,1)S(1)}, u32[]{:S(2)}, u32[]{:S(2)}) collective-permute-start(bf16[320,384]{1,0:T(8,128)(2,1)S(1)} %broadcast_select_fusion.16), channel_id=1, source_target_pairs={{0,8},{4,12},{8,0},{12,4},{16,24},{20,28},{24,16},{28,20},{1,9},{5... | collective-permute-start | bytes 737288 | tf_op jit(solution)/shard_map/ppermute | solution.py:169
  268.2 5.6 %collective-permute-start.73 = (bf16[320,384]{1,0:T(8,128)(2,1)S(1)}, bf16[320,384]{1,0:T(8,128)(2,1)S(1)}, u32[]{:S(2)}, u32[]{:S(2)}) collective-permute-start(bf16[320,384]{1,0:T(8,128)(2,1)S(1)} %pad_select_fusion), channel_id=1, source_target_pairs={{0,8},{4,12},{8,0},{12,4},{16,24},{20,28},{24,16},{28,20},{1,9},{5... | collective-permute-start | bytes 737288 | tf_op jit(solution)/shard_map/ppermute | solution.py:169
  277.5 3.2 %collective-permute-done.73 = bf16[320,384]{1,0:T(8,128)(2,1)S(1)} collective-permute-done((bf16[320,384]{1,0:T(8,128)(2,1)S(1)}, bf16[320,384]{1,0:T(8,128)(2,1)S(1)}, u32[]{:S(2)}, u32[]{:S(2)}) %collective-permute-start.73) | collective-permute-done | bytes 245792 | tf_op jit(solution)/shard_map/ppermute | solution.py:169
  290.3 2.9 adam_piece.4
  294.5 2.9 adam_piece.5
  297.4 7.4 %collective-permute-done.78.came_ref = bf16[768,384]{1,0:T(8,128)(2,1)S(1)} collective-permute-done((bf16[768,384]{1,0:T(8,128)(2,1)S(1)}, bf16[768,384]{1,0:T(8,128)(2,1)S(1)}, u32[]{:S(2)}, u32[]{:S(2)}) %collective-permute-start.78) | collective-permute-done | bytes 589856 | tf_op jit(solution)/shard_map/ppermute | solution.py:183
  304.7 2.9 adam_piece.6
  307.6 3.4 %collective-permute-done.77.came_ref = bf16[768,384]{1,0:T(8,128)(2,1)S(1)} collective-permute-done((bf16[768,384]{1,0:T(8,128)(2,1)S(1)}, bf16[768,384]{1,0:T(8,128)(2,1)S(1)}, u32[]{:S(2)}, u32[]{:S(2)}) %collective-permute-start.77) | collective-permute-done | bytes 589856 | tf_op jit(solution)/shard_map/ppermute | solution.py:183
  311.1 2.9 adam_piece.7
  (343 shorter events, 119.0 us)
Async XLA Ops:
  8.0 22.9 %all-to-all-start = ((bf16[32,64,128]{2,1,0:T(8,128)(2,1)}), bf16[32,64,128]{2,1,0:T(8,128)(2,1)S(1)}, u32[]{:S(2)}, u32[]{:S(2)}) async-start(bf16[32,64,128]{2,1,0:T(8,128)(2,1)} %bitcast.4), calls=%async_computation | async-start | bytes 1048576 | tf_op jit(solution)/shard_map/all_to_all | solution.py:74
  15.3 190.3 %collective-permute-start.48 = (bf16[640,128]{1,0:T(8,128)(2,1)}, bf16[640,128]{1,0:T(8,128)(2,1)}, u32[]{:S(2)}, u32[]{:S(2)}) collective-permute-start(bf16[640,128]{1,0:T(8,128)(2,1)} %param.18), channel_id=1, source_target_pairs={{0,8},{4,12},{8,0},{12,4},{16,24},{20,28},{24,16},{28,20},{1,9},{5... | collective-permute-start | bytes 491528 | tf_op jit(solution)/shard_map/ppermute | solution.py:169
  17.1 32.6 %collective-permute-start = (bf16[768,768]{1,0:T(8,128)(2,1)S(1)}, bf16[768,768]{1,0:T(8,128)(2,1)}, u32[]{:S(2)}, u32[]{:S(2)}) collective-permute-start(bf16[768,768]{1,0:T(8,128)(2,1)S(1)} %get-tuple-element.141), channel_id=1, source_target_pairs={{0,4},{4,0},{8,12},{12,8},{16,20},{20,16},{24,28},{28,24},{1,5},{5... | collective-permute-start | bytes 3538952 | tf_op jit(solution)/shard_map/ppermute | solution.py:183
  55.5 28.4 %collective-permute-start.5 = (bf16[768,768]{1,0:T(8,128)(2,1)S(1)}, bf16[768,768]{1,0:T(8,128)(2,1)}, u32[]{:S(2)}, u32[]{:S(2)}) collective-permute-start(bf16[768,768]{1,0:T(8,128)(2,1)S(1)} %get-tuple-element.145), channel_id=1, source_target_pairs={{0,4},{4,0},{8,12},{12,8},{16,20},{20,16},{24,28},{28,24},{1,5},{5... | collective-permute-start | bytes 3538952 | tf_op jit(solution)/shard_map/ppermute | solution.py:183
  62.6 11.1 %collective-permute-start.4 = (bf16[320,384]{1,0:T(8,128)(2,1)}, bf16[320,384]{1,0:T(8,128)(2,1)}, u32[]{:S(2)}, u32[]{:S(2)}) collective-permute-start(bf16[320,384]{1,0:T(8,128)(2,1)} %get-tuple-element.294), channel_id=1, source_target_pairs={{0,8},{4,12},{8,0},{12,4},{16,24},{20,28},{24,16},{28,20},{1,9},{5... | collective-permute-start | bytes 737288 | tf_op jit(solution)/shard_map/ppermute | solution.py:169
  65.3 33.9 %collective-permute-start.8 = (bf16[320,384]{1,0:T(8,128)(2,1)S(1)}, bf16[320,384]{1,0:T(8,128)(2,1)}, u32[]{:S(2)}, u32[]{:S(2)}) collective-permute-start(bf16[320,384]{1,0:T(8,128)(2,1)S(1)} %get-tuple-element.292), channel_id=1, source_target_pairs={{0,8},{4,12},{8,0},{12,4},{16,24},{20,28},{24,16},{28,20},{1,9},{5... | collective-permute-start | bytes 737288 | tf_op jit(solution)/shard_map/ppermute | solution.py:169
  73.7 17.5 %collective-permute-start.2 = (bf16[320,384]{1,0:T(8,128)(2,1)}, bf16[320,384]{1,0:T(8,128)(2,1)S(1)}, u32[]{:S(2)}, u32[]{:S(2)}) collective-permute-start(bf16[320,384]{1,0:T(8,128)(2,1)} %get-tuple-element.293), channel_id=1, source_target_pairs={{0,8},{4,12},{8,0},{12,4},{16,24},{20,28},{24,16},{28,20},{1,9},{5... | collective-permute-start | bytes 737288 | tf_op jit(solution)/shard_map/ppermute | solution.py:169
  77.9 13.4 %collective-permute-start.3 = (bf16[320,384]{1,0:T(8,128)(2,1)S(1)}, bf16[320,384]{1,0:T(8,128)(2,1)S(1)}, u32[]{:S(2)}, u32[]{:S(2)}) collective-permute-start(bf16[320,384]{1,0:T(8,128)(2,1)S(1)} %add_convert_fusion.35), channel_id=1, source_target_pairs={{8,16},{12,20},{16,8},{20,12},{9,17},{13,21},{17,9},{21,13},{10,18... | collective-permute-start | bytes 737288 | tf_op jit(solution)/shard_map/ppermute | solution.py:169
  83.9 15.3 %collective-permute-start.9 = (bf16[320,384]{1,0:T(8,128)(2,1)S(1)}, bf16[320,384]{1,0:T(8,128)(2,1)S(1)}, u32[]{:S(2)}, u32[]{:S(2)}) collective-permute-start(bf16[320,384]{1,0:T(8,128)(2,1)S(1)} %add_convert_fusion.34), channel_id=1, source_target_pairs={{8,16},{12,20},{16,8},{20,12},{9,17},{13,21},{17,9},{21,13},{10,18... | collective-permute-start | bytes 737288 | tf_op jit(solution)/shard_map/ppermute | solution.py:169
  91.3 13.2 %collective-permute-start.7 = (bf16[320,384]{1,0:T(8,128)(2,1)S(1)}, bf16[320,384]{1,0:T(8,128)(2,1)S(1)}, u32[]{:S(2)}, u32[]{:S(2)}) collective-permute-start(bf16[320,384]{1,0:T(8,128)(2,1)S(1)} %add_convert_fusion.32), channel_id=1, source_target_pairs={{8,16},{12,20},{16,8},{20,12},{9,17},{13,21},{17,9},{21,13},{10,18... | collective-permute-start | bytes 737288 | tf_op jit(solution)/shard_map/ppermute | solution.py:169
  92.1 12.4 %collective-permute-start.6 = (bf16[320,384]{1,0:T(8,128)(2,1)S(1)}, bf16[320,384]{1,0:T(8,128)(2,1)S(1)}, u32[]{:S(2)}, u32[]{:S(2)}) collective-permute-start(bf16[320,384]{1,0:T(8,128)(2,1)S(1)} %fusion.176), channel_id=1, source_target_pairs={{0,8},{4,12},{8,0},{12,4},{16,24},{20,28},{24,16},{28,20},{1,9},{5... | collective-permute-start | bytes 737288 | tf_op jit(solution)/shard_map/ppermute | solution.py:169
  104.6 11.8 %collective-permute-start.15 = (bf16[320,384]{1,0:T(8,128)(2,1)S(1)}, bf16[320,384]{1,0:T(8,128)(2,1)S(1)}, u32[]{:S(2)}, u32[]{:S(2)}) collective-permute-start(bf16[320,384]{1,0:T(8,128)(2,1)S(1)} %add_convert_fusion.28), channel_id=1, source_target_pairs={{8,16},{12,20},{16,8},{20,12},{9,17},{13,21},{17,9},{21,13},{10,18... | collective-permute-start | bytes 737288 | tf_op jit(solution)/shard_map/ppermute | solution.py:169
  105.4 13.2 %collective-permute-start.14 = (bf16[320,384]{1,0:T(8,128)(2,1)S(1)}, bf16[320,384]{1,0:T(8,128)(2,1)S(1)}, u32[]{:S(2)}, u32[]{:S(2)}) collective-permute-start(bf16[320,384]{1,0:T(8,128)(2,1)S(1)} %fusion.178), channel_id=1, source_target_pairs={{0,8},{4,12},{8,0},{12,4},{16,24},{20,28},{24,16},{28,20},{1,9},{5... | collective-permute-start | bytes 737288 | tf_op jit(solution)/shard_map/ppermute | solution.py:169
  112.0 11.7 %collective-permute-start.17 = (bf16[320,384]{1,0:T(8,128)(2,1)S(1)}, bf16[320,384]{1,0:T(8,128)(2,1)S(1)}, u32[]{:S(2)}, u32[]{:S(2)}) collective-permute-start(bf16[320,384]{1,0:T(8,128)(2,1)S(1)} %add_convert_fusion.26), channel_id=1, source_target_pairs={{8,16},{12,20},{16,8},{20,12},{9,17},{13,21},{17,9},{21,13},{10,18... | collective-permute-start | bytes 737288 | tf_op jit(solution)/shard_map/ppermute | solution.py:169
  112.8 11.0 %collective-permute-start.16 = (bf16[320,384]{1,0:T(8,128)(2,1)S(1)}, bf16[320,384]{1,0:T(8,128)(2,1)S(1)}, u32[]{:S(2)}, u32[]{:S(2)}) collective-permute-start(bf16[320,384]{1,0:T(8,128)(2,1)S(1)} %fusion.179), channel_id=1, source_target_pairs={{0,8},{4,12},{8,0},{12,4},{16,24},{20,28},{24,16},{28,20},{1,9},{5... | collective-permute-start | bytes 737288 | tf_op jit(solution)/shard_map/ppermute | solution.py:169
  134.6 10.8 %collective-permute-start.25 = (bf16[320,384]{1,0:T(8,128)(2,1)S(1)}, bf16[320,384]{1,0:T(8,128)(2,1)S(1)}, u32[]{:S(2)}, u32[]{:S(2)}) collective-permute-start(bf16[320,384]{1,0:T(8,128)(2,1)S(1)} %add_convert_fusion.18), channel_id=1, source_target_pairs={{8,16},{12,20},{16,8},{20,12},{9,17},{13,21},{17,9},{21,13},{10,18... | collective-permute-start | bytes 737288 | tf_op jit(solution)/shard_map/ppermute | solution.py:169
  140.0 10.8 %collective-permute-start.29 = (bf16[320,384]{1,0:T(8,128)(2,1)S(1)}, bf16[320,384]{1,0:T(8,128)(2,1)S(1)}, u32[]{:S(2)}, u32[]{:S(2)}) collective-permute-start(bf16[320,384]{1,0:T(8,128)(2,1)S(1)} %add_convert_fusion.16), channel_id=1, source_target_pairs={{8,16},{12,20},{16,8},{20,12},{9,17},{13,21},{17,9},{21,13},{10,18... | collective-permute-start | bytes 737288 | tf_op jit(solution)/shard_map/ppermute | solution.py:169
  140.7 11.6 %collective-permute-start.28 = (bf16[320,384]{1,0:T(8,128)(2,1)S(1)}, bf16[320,384]{1,0:T(8,128)(2,1)S(1)}, u32[]{:S(2)}, u32[]{:S(2)}) collective-permute-start(bf16[320,384]{1,0:T(8,128)(2,1)S(1)} %fusion.184), channel_id=1, source_target_pairs={{0,8},{4,12},{8,0},{12,4},{16,24},{20,28},{24,16},{28,20},{1,9},{5... | collective-permute-start | bytes 737288 | tf_op jit(solution)/shard_map/ppermute | solution.py:169
  148.3 13.3 %collective-permute-start.30 = (bf16[320,384]{1,0:T(8,128)(2,1)S(1)}, bf16[320,384]{1,0:T(8,128)(2,1)S(1)}, u32[]{:S(2)}, u32[]{:S(2)}) collective-permute-start(bf16[320,384]{1,0:T(8,128)(2,1)S(1)} %fusion.185), channel_id=1, source_target_pairs={{0,8},{4,12},{8,0},{12,4},{16,24},{20,28},{24,16},{28,20},{1,9},{5... | collective-permute-start | bytes 737288 | tf_op jit(solution)/shard_map/ppermute | solution.py:169
  150.0 11.6 %collective-permute-start.31 = (bf16[320,384]{1,0:T(8,128)(2,1)S(1)}, bf16[320,384]{1,0:T(8,128)(2,1)S(1)}, u32[]{:S(2)}, u32[]{:S(2)}) collective-permute-start(bf16[320,384]{1,0:T(8,128)(2,1)S(1)} %add_convert_fusion.14), channel_id=1, source_target_pairs={{8,16},{12,20},{16,8},{20,12},{9,17},{13,21},{17,9},{21,13},{10,18... | collective-permute-start | bytes 737288 | tf_op jit(solution)/shard_map/ppermute | solution.py:169
  152.4 13.2 %collective-permute-start.33 = (bf16[320,384]{1,0:T(8,128)(2,1)S(1)}, bf16[320,384]{1,0:T(8,128)(2,1)S(1)}, u32[]{:S(2)}, u32[]{:S(2)}) collective-permute-start(bf16[320,384]{1,0:T(8,128)(2,1)S(1)} %add_convert_fusion.12), channel_id=1, source_target_pairs={{8,16},{12,20},{16,8},{20,12},{9,17},{13,21},{17,9},{21,13},{10,18... | collective-permute-start | bytes 737288 | tf_op jit(solution)/shard_map/ppermute | solution.py:169
  167.1 10.8 %collective-permute-start.36 = (bf16[320,384]{1,0:T(8,128)(2,1)S(1)}, bf16[320,384]{1,0:T(8,128)(2,1)S(1)}, u32[]{:S(2)}, u32[]{:S(2)}) collective-permute-start(bf16[320,384]{1,0:T(8,128)(2,1)S(1)} %fusion.188), channel_id=1, source_target_pairs={{0,8},{4,12},{8,0},{12,4},{16,24},{20,28},{24,16},{28,20},{1,9},{5... | collective-permute-start | bytes 737288 | tf_op jit(solution)/shard_map/ppermute | solution.py:169
  172.2 11.3 %collective-permute-start.38 = (bf16[320,384]{1,0:T(8,128)(2,1)S(1)}, bf16[320,384]{1,0:T(8,128)(2,1)S(1)}, u32[]{:S(2)}, u32[]{:S(2)}) collective-permute-start(bf16[320,384]{1,0:T(8,128)(2,1)S(1)} %fusion.189), channel_id=1, source_target_pairs={{0,8},{4,12},{8,0},{12,4},{16,24},{20,28},{24,16},{28,20},{1,9},{5... | collective-permute-start | bytes 737288 | tf_op jit(solution)/shard_map/ppermute | solution.py:169
  177.9 12.1 %collective-permute-start.41 = (bf16[320,384]{1,0:T(8,128)(2,1)S(1)}, bf16[320,384]{1,0:T(8,128)(2,1)S(1)}, u32[]{:S(2)}, u32[]{:S(2)}) collective-permute-start(bf16[320,384]{1,0:T(8,128)(2,1)S(1)} %collective-permute-done.36), channel_id=1, source_target_pairs={{8,16},{12,20},{16,8},{20,12},{9,17},{13,21},{17,9},{21,13},{10,18... | collective-permute-start | bytes 737288 | tf_op jit(solution)/shard_map/ppermute | solution.py:169
  178.6 11.3 %collective-permute-start.40 = (bf16[320,384]{1,0:T(8,128)(2,1)S(1)}, bf16[320,384]{1,0:T(8,128)(2,1)S(1)}, u32[]{:S(2)}, u32[]{:S(2)}) collective-permute-start(bf16[320,384]{1,0:T(8,128)(2,1)S(1)} %fusion.190), channel_id=1, source_target_pairs={{0,8},{4,12},{8,0},{12,4},{16,24},{20,28},{24,16},{28,20},{1,9},{5... | collective-permute-start | bytes 737288 | tf_op jit(solution)/shard_map/ppermute | solution.py:169
  183.6 11.7 %collective-permute-start.43 = (bf16[320,384]{1,0:T(8,128)(2,1)S(1)}, bf16[320,384]{1,0:T(8,128)(2,1)S(1)}, u32[]{:S(2)}, u32[]{:S(2)}) collective-permute-start(bf16[320,384]{1,0:T(8,128)(2,1)S(1)} %collective-permute-done.38), channel_id=1, source_target_pairs={{8,16},{12,20},{16,8},{20,12},{9,17},{13,21},{17,9},{21,13},{10,18... | collective-permute-start | bytes 737288 | tf_op jit(solution)/shard_map/ppermute | solution.py:169
  184.3 10.9 %collective-permute-start.42 = (bf16[320,384]{1,0:T(8,128)(2,1)S(1)}, bf16[320,384]{1,0:T(8,128)(2,1)S(1)}, u32[]{:S(2)}, u32[]{:S(2)}) collective-permute-start(bf16[320,384]{1,0:T(8,128)(2,1)S(1)} %fusion.191), channel_id=1, source_target_pairs={{0,8},{4,12},{8,0},{12,4},{16,24},{20,28},{24,16},{28,20},{1,9},{5... | collective-permute-start | bytes 737288 | tf_op jit(solution)/shard_map/ppermute | solution.py:169
  190.0 12.8 %collective-permute-start.50 = (bf16[320,384]{1,0:T(8,128)(2,1)S(1)}, bf16[320,384]{1,0:T(8,128)(2,1)S(1)}, u32[]{:S(2)}, u32[]{:S(2)}) collective-permute-start(bf16[320,384]{1,0:T(8,128)(2,1)S(1)} %collective-permute-done.40), channel_id=1, source_target_pairs={{8,16},{12,20},{16,8},{20,12},{9,17},{13,21},{17,9},{21,13},{10,18... | collective-permute-start | bytes 737288 | tf_op jit(solution)/shard_map/ppermute | solution.py:169
  190.7 12.0 %collective-permute-start.49 = (bf16[320,384]{1,0:T(8,128)(2,1)S(1)}, bf16[320,384]{1,0:T(8,128)(2,1)S(1)}, u32[]{:S(2)}, u32[]{:S(2)}) collective-permute-start(bf16[320,384]{1,0:T(8,128)(2,1)S(1)} %broadcast_select_fusion.43), channel_id=1, source_target_pairs={{0,8},{4,12},{8,0},{12,4},{16,24},{20,28},{24,16},{28,20},{1,9},{5... | collective-permute-start | bytes 737288 | tf_op jit(solution)/shard_map/ppermute | solution.py:169
  195.3 16.6 %collective-permute-start.47 = (bf16[320,384]{1,0:T(8,128)(2,1)S(1)}, bf16[320,384]{1,0:T(8,128)(2,1)S(1)}, u32[]{:S(2)}, u32[]{:S(2)}) collective-permute-start(bf16[320,384]{1,0:T(8,128)(2,1)S(1)} %collective-permute-done.42), channel_id=1, source_target_pairs={{8,16},{12,20},{16,8},{20,12},{9,17},{13,21},{17,9},{21,13},{10,18... | collective-permute-start | bytes 737288 | tf_op jit(solution)/shard_map/ppermute | solution.py:169
  196.6 15.3 %collective-permute-start.46 = (bf16[320,384]{1,0:T(8,128)(2,1)S(1)}, bf16[320,384]{1,0:T(8,128)(2,1)S(1)}, u32[]{:S(2)}, u32[]{:S(2)}) collective-permute-start(bf16[320,384]{1,0:T(8,128)(2,1)S(1)} %broadcast_select_fusion.42), channel_id=1, source_target_pairs={{0,8},{4,12},{8,0},{12,4},{16,24},{20,28},{24,16},{28,20},{1,9},{5... | collective-permute-start | bytes 737288 | tf_op jit(solution)/shard_map/ppermute | solution.py:169
  202.8 16.8 %collective-permute-start.52 = (bf16[320,384]{1,0:T(8,128)(2,1)S(1)}, bf16[320,384]{1,0:T(8,128)(2,1)S(1)}, u32[]{:S(2)}, u32[]{:S(2)}) collective-permute-start(bf16[320,384]{1,0:T(8,128)(2,1)S(1)} %collective-permute-done.49), channel_id=1, source_target_pairs={{8,16},{12,20},{16,8},{20,12},{9,17},{13,21},{17,9},{21,13},{10,18... | collective-permute-start | bytes 737288 | tf_op jit(solution)/shard_map/ppermute | solution.py:169
  205.6 14.0 %collective-permute-start.51 = (bf16[320,384]{1,0:T(8,128)(2,1)S(1)}, bf16[320,384]{1,0:T(8,128)(2,1)S(1)}, u32[]{:S(2)}, u32[]{:S(2)}) collective-permute-start(bf16[320,384]{1,0:T(8,128)(2,1)S(1)} %broadcast_select_fusion.41), channel_id=1, source_target_pairs={{0,8},{4,12},{8,0},{12,4},{16,24},{20,28},{24,16},{28,20},{1,9},{5... | collective-permute-start | bytes 737288 | tf_op jit(solution)/shard_map/ppermute | solution.py:169
  222.7 11.6 %collective-permute-start.58 = (bf16[320,384]{1,0:T(8,128)(2,1)S(1)}, bf16[320,384]{1,0:T(8,128)(2,1)S(1)}, u32[]{:S(2)}, u32[]{:S(2)}) collective-permute-start(bf16[320,384]{1,0:T(8,128)(2,1)S(1)} %collective-permute-done.55), channel_id=1, source_target_pairs={{8,16},{12,20},{16,8},{20,12},{9,17},{13,21},{17,9},{21,13},{10,18... | collective-permute-start | bytes 737288 | tf_op jit(solution)/shard_map/ppermute | solution.py:169
  229.6 12.2 %collective-permute-start.62 = (bf16[320,384]{1,0:T(8,128)(2,1)S(1)}, bf16[320,384]{1,0:T(8,128)(2,1)S(1)}, u32[]{:S(2)}, u32[]{:S(2)}) collective-permute-start(bf16[320,384]{1,0:T(8,128)(2,1)S(1)} %collective-permute-done.53), channel_id=1, source_target_pairs={{8,16},{12,20},{16,8},{20,12},{9,17},{13,21},{17,9},{21,13},{10,18... | collective-permute-start | bytes 737288 | tf_op jit(solution)/shard_map/ppermute | solution.py:169
  230.3 11.4 %collective-permute-start.61 = (bf16[320,384]{1,0:T(8,128)(2,1)S(1)}, bf16[320,384]{1,0:T(8,128)(2,1)S(1)}, u32[]{:S(2)}, u32[]{:S(2)}) collective-permute-start(bf16[320,384]{1,0:T(8,128)(2,1)S(1)} %broadcast_select_fusion.29), channel_id=1, source_target_pairs={{0,8},{4,12},{8,0},{12,4},{16,24},{20,28},{24,16},{28,20},{1,9},{5... | collective-permute-start | bytes 737288 | tf_op jit(solution)/shard_map/ppermute | solution.py:169
  244.7 11.9 %collective-permute-start.68 = (bf16[320,384]{1,0:T(8,128)(2,1)S(1)}, bf16[320,384]{1,0:T(8,128)(2,1)S(1)}, u32[]{:S(2)}, u32[]{:S(2)}) collective-permute-start(bf16[320,384]{1,0:T(8,128)(2,1)S(1)} %collective-permute-done.59), channel_id=1, source_target_pairs={{8,16},{12,20},{16,8},{20,12},{9,17},{13,21},{17,9},{21,13},{10,18... | collective-permute-start | bytes 737288 | tf_op jit(solution)/shard_map/ppermute | solution.py:169
  245.5 11.1 %collective-permute-start.67 = (bf16[320,384]{1,0:T(8,128)(2,1)S(1)}, bf16[320,384]{1,0:T(8,128)(2,1)S(1)}, u32[]{:S(2)}, u32[]{:S(2)}) collective-permute-start(bf16[320,384]{1,0:T(8,128)(2,1)S(1)} %broadcast_select_fusion.18), channel_id=1, source_target_pairs={{0,8},{4,12},{8,0},{12,4},{16,24},{20,28},{24,16},{28,20},{1,9},{5... | collective-permute-start | bytes 737288 | tf_op jit(solution)/shard_map/ppermute | solution.py:169
  252.4 13.0 %collective-permute-start.65 = (bf16[320,384]{1,0:T(8,128)(2,1)S(1)}, bf16[320,384]{1,0:T(8,128)(2,1)S(1)}, u32[]{:S(2)}, u32[]{:S(2)}) collective-permute-start(bf16[320,384]{1,0:T(8,128)(2,1)S(1)} %broadcast_select_fusion.17), channel_id=1, source_target_pairs={{0,8},{4,12},{8,0},{12,4},{16,24},{20,28},{24,16},{28,20},{1,9},{5... | collective-permute-start | bytes 737288 | tf_op jit(solution)/shard_map/ppermute | solution.py:169
  252.9 12.4 %collective-permute-start.66 = (bf16[320,384]{1,0:T(8,128)(2,1)S(1)}, bf16[320,384]{1,0:T(8,128)(2,1)S(1)}, u32[]{:S(2)}, u32[]{:S(2)}) collective-permute-start(bf16[320,384]{1,0:T(8,128)(2,1)S(1)} %collective-permute-done.63), channel_id=1, source_target_pairs={{8,16},{12,20},{16,8},{20,12},{9,17},{13,21},{17,9},{21,13},{10,18... | collective-permute-start | bytes 737288 | tf_op jit(solution)/shard_map/ppermute | solution.py:169
  263.1 27.1 %collective-permute-start.80 = (bf16[768,384]{1,0:T(8,128)(2,1)S(1)}, bf16[768,384]{1,0:T(8,128)(2,1)S(1)}, u32[]{:S(2)}, u32[]{:S(2)}) collective-permute-start(bf16[768,384]{1,0:T(8,128)(2,1)S(1)} %add_convert_fusion), channel_id=1, source_target_pairs={{0,4},{4,0},{8,12},{12,8},{16,20},{20,16},{24,28},{28,24},{1,5},{5... | collective-permute-start | bytes 1769480 | tf_op jit(solution)/shard_map/ppermute | solution.py:183
  265.4 10.8 %collective-permute-start.69 = (bf16[320,384]{1,0:T(8,128)(2,1)S(1)}, bf16[320,384]{1,0:T(8,128)(2,1)S(1)}, u32[]{:S(2)}, u32[]{:S(2)}) collective-permute-start(bf16[320,384]{1,0:T(8,128)(2,1)S(1)} %pad_select_fusion.1), channel_id=1, source_target_pairs={{0,8},{4,12},{8,0},{12,4},{16,24},{20,28},{24,16},{28,20},{1,9},{5... | collective-permute-start | bytes 737288 | tf_op jit(solution)/shard_map/ppermute | solution.py:169
  265.5 11.9 %collective-permute-start.70 = (bf16[320,384]{1,0:T(8,128)(2,1)S(1)}, bf16[320,384]{1,0:T(8,128)(2,1)S(1)}, u32[]{:S(2)}, u32[]{:S(2)}) collective-permute-start(bf16[320,384]{1,0:T(8,128)(2,1)S(1)} %collective-permute-done.65), channel_id=1, source_target_pairs={{8,16},{12,20},{16,8},{20,12},{9,17},{13,21},{17,9},{21,13},{10,18... | collective-permute-start | bytes 737288 | tf_op jit(solution)/shard_map/ppermute | solution.py:169
  267.3 13.4 %collective-permute-start.74 = (bf16[320,384]{1,0:T(8,128)(2,1)S(1)}, bf16[320,384]{1,0:T(8,128)(2,1)S(1)}, u32[]{:S(2)}, u32[]{:S(2)}) collective-permute-start(bf16[320,384]{1,0:T(8,128)(2,1)S(1)} %collective-permute-done.71), channel_id=1, source_target_pairs={{8,16},{12,20},{16,8},{20,12},{9,17},{13,21},{17,9},{21,13},{10,18... | collective-permute-start | bytes 737288 | tf_op jit(solution)/shard_map/ppermute | solution.py:169
  268.2 12.4 %collective-permute-start.73 = (bf16[320,384]{1,0:T(8,128)(2,1)S(1)}, bf16[320,384]{1,0:T(8,128)(2,1)S(1)}, u32[]{:S(2)}, u32[]{:S(2)}) collective-permute-start(bf16[320,384]{1,0:T(8,128)(2,1)S(1)} %pad_select_fusion), channel_id=1, source_target_pairs={{0,8},{4,12},{8,0},{12,4},{16,24},{20,28},{24,16},{28,20},{1,9},{5... | collective-permute-start | bytes 737288 | tf_op jit(solution)/shard_map/ppermute | solution.py:169
  276.3 18.2 %collective-permute-start.79 = (bf16[768,384]{1,0:T(8,128)(2,1)S(1)}, bf16[768,384]{1,0:T(8,128)(2,1)S(1)}, u32[]{:S(2)}, u32[]{:S(2)}) collective-permute-start(bf16[768,384]{1,0:T(8,128)(2,1)S(1)} %add_convert_fusion.1), channel_id=1, source_target_pairs={{0,4},{4,0},{8,12},{12,8},{16,20},{20,16},{24,28},{28,24},{1,5},{5... | collective-permute-start | bytes 1769480 | tf_op jit(solution)/shard_map/ppermute | solution.py:183
  285.0 19.7 %collective-permute-start.78 = (bf16[768,384]{1,0:T(8,128)(2,1)S(1)}, bf16[768,384]{1,0:T(8,128)(2,1)S(1)}, u32[]{:S(2)}, u32[]{:S(2)}) collective-permute-start(bf16[768,384]{1,0:T(8,128)(2,1)S(1)} %add_convert_fusion.2), channel_id=1, source_target_pairs={{0,4},{4,0},{8,12},{12,8},{16,20},{20,16},{24,28},{28,24},{1,5},{5... | collective-permute-start | bytes 1769480 | tf_op jit(solution)/shard_map/ppermute | solution.py:183
  288.3 22.8 %collective-permute-start.77 = (bf16[768,384]{1,0:T(8,128)(2,1)S(1)}, bf16[768,384]{1,0:T(8,128)(2,1)S(1)}, u32[]{:S(2)}, u32[]{:S(2)}) collective-permute-start(bf16[768,384]{1,0:T(8,128)(2,1)S(1)} %add_convert_fusion.3), channel_id=1, source_target_pairs={{0,4},{4,0},{8,12},{12,8},{16,20},{20,16},{24,28},{28,24},{1,5},{5... | collective-permute-start | bytes 1769480 | tf_op jit(solution)/shard_map/ppermute | solution.py:183
  (59 other events, 427.4 us)

commit v4 on v3

--- a/solution.py
+++ b/solution.py
@@ -260,9 +260,16 @@
     def group_features(group):
         return make_features(jnp.concatenate([outbound[group], inbound[group]], axis=0))
 
-    joined = {}
+    joined, own_sums = {}, {}
 
     def partial_sums(group, side, which):
+        if (group, side, which) in own_sums:
+            value = own_sums[group, side, which]
+            for step in range(1, inner):
+                rows = slice(step * depth, (step + 1) * depth)
+                left = features[group][side * batch_rows :][:batch_rows, rows]
+                value += dot32(left, weight[which][step])
+            return value.astype(jnp.bfloat16)
         if which not in joined:
             joined[which] = jnp.concatenate(weight[which], axis=0)
         left = features[group][side * batch_rows :][:batch_rows]
@@ -308,7 +315,7 @@
     late = streams - 1
     side_work = {
         (0, 0): [(0, 1, 0), "scales", "features"],
-        (0, late): [(1, 0, 0), (1, 1, 0)],
+        (0, late): [(1, 0, 0), (1, 1, 0), "own"],
         (1, late): [(0, 0, 1)],
         (2, 0): [(0, 1, 1)],
         (2, late): [(1, 0, 1), (1, 1, 1)],
@@ -327,6 +334,8 @@
                     sums[key] = value
                 elif box == "delta":
                     delta[key] = value
+                elif box == "own":
+                    own_sums[key] = value
                 elif box == "early":
                     early[key] = value
                 elif box == "scales":
@@ -363,12 +372,16 @@
         for work in side_work.get((tick, part), ()):
             if work == "scales":
                 pending["scales", None] = local_scales()
+            elif work == "own":
+                left = features[0][:batch_rows, :depth]
+                pending["own", (0, 0, 1)] = dot32(left, weight_own[1])
             elif work == "features":
                 features.append(group_features(1))
             else:
                 group = work[0]
-                if tick > 1:
-                    features[group] = lax.optimization_barrier((features[group], was_end))[0]
+                if tick != 1:
+                    hold = was_end if tick else payload
+                    features[group] = lax.optimization_barrier((features[group], hold))[0]
                 pending["sums", work] = partial_sums(*work)
 
         group, piece = divmod(tick - line + 1, pieces)

time: 319 us -> 314 us (0.984)
  waiting for transfers between devices: 59.8 us -> 47.2 us
  starting transfers between devices: 148 us -> 154 us
    ppermute x69, starting transfers between devices: 129 us -> 135 us  [swap(): return lax.ppermute(value, 'dp', pairs)]
    ppermute x69, waiting for transfers between devices: 25.7 us -> 19.4 us  [swap(): return lax.ppermute(value, 'dp', pairs)]
    ppermute x6, waiting for transfers between devices: 16 us -> 11.8 us  [turn(): return lax.ppermute(value, 'dp', pairs)]
    unnamed x48 -> x52, local copies, waits for them, and re-layouts: 3.39 us -> 7.07 us
    dot_general x21 -> x22, matrix products: 30.8 us -> 30.4 us  [dot32(): return jnp.dot(left, right, preferred_element_type=jnp.float32)]
  transfers between devices with their start and end apart: 82 -> 82, of which waited for: 20 -> 22; matrix products, arithmetic and copies ran while one was open for 24% -> 25% of each run, Pallas kernels for 3% -> 3%
where the time goes in v4:
time: 314 us; the launch traced here: 310 us
  starting transfers between devices  154 us (49%)
  matrix products  55 us (18%)
  waiting for transfers between devices  47.2 us (15%)
  local copies, waits for them, and re-layouts  16.1 us (5%)
  other arithmetic  14.9 us (5%)
  Pallas kernels  11.7 us (4%)
  blocking collectives  7.72 us (2%)
  between operations  3.35 us (1%)
    ppermute x69, starting transfers between devices, swap(): return lax.ppermute(value, 'dp', pairs)  135 us
    dot_general x22, matrix products, dot32(): return jnp.dot(left, right, preferred_element_type=jnp.float32)  30.4 us
    ppermute x69, waiting for transfers between devices, swap(): return lax.ppermute(value, 'dp', pairs)  19.4 us
    dot_general x12, matrix products, gradient_term(): lax.dot_general(features[unit // pieces][:, rows], jnp.concatenate(arrive...  18.7 us
    ppermute x6, waiting for transfers between devices, turn(): return lax.ppermute(value, 'dp', pairs)  11.8 us
    pallas_call x4, Pallas kernels, adam_piece(): pl.pallas_call(adam_kernel, grid=(3,), in_specs=[piece, piece, column, co...  11.7 us
    ppermute x6, waiting for transfers between devices, mp_sum(): lax.ppermute(value, 'mp', [(m, m ^ step) for m in range(model_count)])  8.23 us
    all_to_all x1, waiting for transfers between devices, route(): lax.all_to_all(outgoing.reshape(devices_all, line * lot, patch_width), ('...  7.78 us
  transfers between devices with their start and end apart: 82, of which 22 were waited for; matrix products, arithmetic and copies ran while one was open for 25% of the time, Pallas kernels for 3%

profile of v4, /device:TPU:0, one launch (start us, length us, event | category | flops | bytes accessed | tf_op | source)
XLA Modules:
  0.0 309.8 jit_solution(15713457004875057695)
XLA Ops:
  1.4 2.6 convert.14
  8.9 7.3 %all-to-all-start = ((bf16[32,64,128]{2,1,0:T(8,128)(2,1)}), bf16[32,64,128]{2,1,0:T(8,128)(2,1)S(1)}, u32[]{:S(2)}, u32[]{:S(2)}) async-start(bf16[32,64,128]{2,1,0:T(8,128)(2,1)} %bitcast.4), calls=%async_computation | async-start | bytes 1048576 | tf_op jit(solution)/shard_map/all_to_all | solution.py:74
  21.6 2.4 constant_dynamic-update-slice_fusion.1
  24.0 7.8 %all-to-all-done = bf16[32,64,128]{2,1,0:T(8,128)(2,1)S(1)} async-done(((bf16[32,64,128]{2,1,0:T(8,128)(2,1)}), bf16[32,64,128]{2,1,0:T(8,128)(2,1)S(1)}, u32[]{:S(2)}, u32[]{:S(2)}) %all-to-all-start) | async-done | bytes 524320 | tf_op jit(solution)/shard_map/all_to_all | solution.py:74
  33.1 7.7 %all_gather.3 = bf16[4,640,128]{2,1,0:T(8,128)(2,1)S(1)} all-gather(bf16[4,160,128]{2,1,0:T(8,128)(2,1)S(1)} %bitcast.75), channel_id=1, replica_groups=mesh['dp'=8,'mp'=4] {'mp'}, dimensions={1}, use_global_device_ids=true | all-gather | bytes 819200 | tf_op jit(solution)/shard_map/all_gather | solution.py:216
  40.9 3.5 %fusion.3 = f32[320]{0:T(512)S(1)} fusion(bf16[128,6144]{1,0:T(8,128)(2,1)S(1)} %copy-done.11, bf16[160,128]{1,0:T(8,128)(2,1)S(1)} %get-tuple-element.349, bf16[160,128]{1,0:T(8,128)(2,1)S(1)} %get-tuple-element.350), kind=kOutput, calls=%fused_computation.6 | convolution fusion | flops 521174720 | bytes 1656064 | tf_op jit(solution)/shard_map/dot_general | solution.py:37
  44.4 2.9 fusion.5
  47.3 2.9 fusion.1
  51.6 3.1 %constant_dynamic-update-slice_fusion.3 = bf16[1536,768]{1,0:T(8,128)(2,1)} fusion(bf16[768,768]{1,0:T(8,128)(2,1)} %get-tuple-element.153), kind=kLoop, calls=%fused_computation.367 | loop fusion | bytes 2359296
  70.4 2.5 collective-permute-done.4
  79.8 2.5 fusion.135
  84.5 7.6 %collective-permute-start.6 = (bf16[320,384]{1,0:T(8,128)(2,1)S(1)}, bf16[320,384]{1,0:T(8,128)(2,1)S(1)}, u32[]{:S(2)}, u32[]{:S(2)}) collective-permute-start(bf16[320,384]{1,0:T(8,128)(2,1)S(1)} %fusion.175), channel_id=1, source_target_pairs={{0,8},{4,12},{8,0},{12,4},{16,24},{20,28},{24,16},{28,20},{1,9},{5... | collective-permute-start | bytes 737288 | tf_op jit(solution)/shard_map/ppermute | solution.py:169
  100.7 6.6 %collective-permute-start.14 = (bf16[320,384]{1,0:T(8,128)(2,1)S(1)}, bf16[320,384]{1,0:T(8,128)(2,1)S(1)}, u32[]{:S(2)}, u32[]{:S(2)}) collective-permute-start(bf16[320,384]{1,0:T(8,128)(2,1)S(1)} %fusion.177), channel_id=1, source_target_pairs={{0,8},{4,12},{8,0},{12,4},{16,24},{20,28},{24,16},{28,20},{1,9},{5... | collective-permute-start | bytes 737288 | tf_op jit(solution)/shard_map/ppermute | solution.py:169
  108.1 5.4 %collective-permute-start.16 = (bf16[320,384]{1,0:T(8,128)(2,1)S(1)}, bf16[320,384]{1,0:T(8,128)(2,1)S(1)}, u32[]{:S(2)}, u32[]{:S(2)}) collective-permute-start(bf16[320,384]{1,0:T(8,128)(2,1)S(1)} %fusion.178), channel_id=1, source_target_pairs={{0,8},{4,12},{8,0},{12,4},{16,24},{20,28},{24,16},{28,20},{1,9},{5... | collective-permute-start | bytes 737288 | tf_op jit(solution)/shard_map/ppermute | solution.py:169
  114.4 4.2 %collective-permute-start.18 = (bf16[320,384]{1,0:T(8,128)(2,1)S(1)}, bf16[320,384]{1,0:T(8,128)(2,1)S(1)}, u32[]{:S(2)}, u32[]{:S(2)}) collective-permute-start(bf16[320,384]{1,0:T(8,128)(2,1)S(1)} %fusion.179), channel_id=1, source_target_pairs={{0,8},{4,12},{8,0},{12,4},{16,24},{20,28},{24,16},{28,20},{1,9},{5... | collective-permute-start | bytes 737288 | tf_op jit(solution)/shard_map/ppermute | solution.py:169
  124.8 5.1 %collective-permute-start.22 = (bf16[320,384]{1,0:T(8,128)(2,1)S(1)}, bf16[320,384]{1,0:T(8,128)(2,1)S(1)}, u32[]{:S(2)}, u32[]{:S(2)}) collective-permute-start(bf16[320,384]{1,0:T(8,128)(2,1)S(1)} %fusion.181), channel_id=1, source_target_pairs={{0,8},{4,12},{8,0},{12,4},{16,24},{20,28},{24,16},{28,20},{1,9},{5... | collective-permute-start | bytes 737288 | tf_op jit(solution)/shard_map/ppermute | solution.py:169
  130.7 4.4 %collective-permute-start.24 = (bf16[320,384]{1,0:T(8,128)(2,1)S(1)}, bf16[320,384]{1,0:T(8,128)(2,1)S(1)}, u32[]{:S(2)}, u32[]{:S(2)}) collective-permute-start(bf16[320,384]{1,0:T(8,128)(2,1)S(1)} %fusion.182), channel_id=1, source_target_pairs={{0,8},{4,12},{8,0},{12,4},{16,24},{20,28},{24,16},{28,20},{1,9},{5... | collective-permute-start | bytes 737288 | tf_op jit(solution)/shard_map/ppermute | solution.py:169
  136.0 4.6 %collective-permute-start.28 = (bf16[320,384]{1,0:T(8,128)(2,1)S(1)}, bf16[320,384]{1,0:T(8,128)(2,1)S(1)}, u32[]{:S(2)}, u32[]{:S(2)}) collective-permute-start(bf16[320,384]{1,0:T(8,128)(2,1)S(1)} %fusion.183), channel_id=1, source_target_pairs={{0,8},{4,12},{8,0},{12,4},{16,24},{20,28},{24,16},{28,20},{1,9},{5... | collective-permute-start | bytes 737288 | tf_op jit(solution)/shard_map/ppermute | solution.py:169
  148.4 4.0 %collective-permute-done.27 = bf16[640,128]{1,0:T(8,128)(2,1)S(1)} collective-permute-done((bf16[640,128]{1,0:T(8,128)(2,1)S(1)}, bf16[640,128]{1,0:T(8,128)(2,1)S(1)}, u32[]{:S(2)}, u32[]{:S(2)}) %collective-permute-start.27) | collective-permute-done | bytes 163872 | tf_op jit(solution)/shard_map/ppermute | solution.py:189
  152.4 3.1 collective-permute-start.32
  157.8 2.6 collective-permute-start.34
  162.7 4.2 %collective-permute-start.36 = (bf16[320,384]{1,0:T(8,128)(2,1)S(1)}, bf16[320,384]{1,0:T(8,128)(2,1)S(1)}, u32[]{:S(2)}, u32[]{:S(2)}) collective-permute-start(bf16[320,384]{1,0:T(8,128)(2,1)S(1)} %fusion.187), channel_id=1, source_target_pairs={{0,8},{4,12},{8,0},{12,4},{16,24},{20,28},{24,16},{28,20},{1,9},{5... | collective-permute-start | bytes 737288 | tf_op jit(solution)/shard_map/ppermute | solution.py:169
  169.6 4.2 %collective-permute-done.36 = bf16[320,384]{1,0:T(8,128)(2,1)S(1)} collective-permute-done((bf16[320,384]{1,0:T(8,128)(2,1)S(1)}, bf16[320,384]{1,0:T(8,128)(2,1)S(1)}, u32[]{:S(2)}, u32[]{:S(2)}) %collective-permute-start.36) | collective-permute-done | bytes 245792 | tf_op jit(solution)/shard_map/ppermute | solution.py:169
  174.6 4.1 %collective-permute-start.40 = (bf16[320,384]{1,0:T(8,128)(2,1)S(1)}, bf16[320,384]{1,0:T(8,128)(2,1)S(1)}, u32[]{:S(2)}, u32[]{:S(2)}) collective-permute-start(bf16[320,384]{1,0:T(8,128)(2,1)S(1)} %fusion.189), channel_id=1, source_target_pairs={{0,8},{4,12},{8,0},{12,4},{16,24},{20,28},{24,16},{28,20},{1,9},{5... | collective-permute-start | bytes 737288 | tf_op jit(solution)/shard_map/ppermute | solution.py:169
  179.9 3.6 %collective-permute-start.42 = (bf16[320,384]{1,0:T(8,128)(2,1)S(1)}, bf16[320,384]{1,0:T(8,128)(2,1)S(1)}, u32[]{:S(2)}, u32[]{:S(2)}) collective-permute-start(bf16[320,384]{1,0:T(8,128)(2,1)S(1)} %fusion.190), channel_id=1, source_target_pairs={{0,8},{4,12},{8,0},{12,4},{16,24},{20,28},{24,16},{28,20},{1,9},{5... | collective-permute-start | bytes 737288 | tf_op jit(solution)/shard_map/ppermute | solution.py:169
  185.5 3.7 %collective-permute-start.49 = (bf16[320,384]{1,0:T(8,128)(2,1)S(1)}, bf16[320,384]{1,0:T(8,128)(2,1)S(1)}, u32[]{:S(2)}, u32[]{:S(2)}) collective-permute-start(bf16[320,384]{1,0:T(8,128)(2,1)S(1)} %broadcast_select_fusion.43), channel_id=1, source_target_pairs={{0,8},{4,12},{8,0},{12,4},{16,24},{20,28},{24,16},{28,20},{1,9},{5... | collective-permute-start | bytes 737288 | tf_op jit(solution)/shard_map/ppermute | solution.py:169
  191.6 3.6 %collective-permute-start.46 = (bf16[320,384]{1,0:T(8,128)(2,1)S(1)}, bf16[320,384]{1,0:T(8,128)(2,1)S(1)}, u32[]{:S(2)}, u32[]{:S(2)}) collective-permute-start(bf16[320,384]{1,0:T(8,128)(2,1)S(1)} %broadcast_select_fusion.42), channel_id=1, source_target_pairs={{0,8},{4,12},{8,0},{12,4},{16,24},{20,28},{24,16},{28,20},{1,9},{5... | collective-permute-start | bytes 737288 | tf_op jit(solution)/shard_map/ppermute | solution.py:169
  200.1 2.5 collective-permute-start.51
  202.6 2.5 collective-permute-done.45
  207.4 4.0 %collective-permute-start.55 = (bf16[320,384]{1,0:T(8,128)(2,1)S(1)}, bf16[320,384]{1,0:T(8,128)(2,1)S(1)}, u32[]{:S(2)}, u32[]{:S(2)}) collective-permute-start(bf16[320,384]{1,0:T(8,128)(2,1)S(1)} %broadcast_select_fusion.36), channel_id=1, source_target_pairs={{0,8},{4,12},{8,0},{12,4},{16,24},{20,28},{24,16},{28,20},{1,9},{5... | collective-permute-start | bytes 737288 | tf_op jit(solution)/shard_map/ppermute | solution.py:169
  211.4 2.2 fusion.103
  214.8 3.1 collective-permute-start.53
  219.2 3.6 %collective-permute-start.57 = (bf16[320,384]{1,0:T(8,128)(2,1)S(1)}, bf16[320,384]{1,0:T(8,128)(2,1)S(1)}, u32[]{:S(2)}, u32[]{:S(2)}) collective-permute-start(bf16[320,384]{1,0:T(8,128)(2,1)S(1)} %broadcast_select_fusion.30), channel_id=1, source_target_pairs={{0,8},{4,12},{8,0},{12,4},{16,24},{20,28},{24,16},{28,20},{1,9},{5... | collective-permute-start | bytes 737288 | tf_op jit(solution)/shard_map/ppermute | solution.py:169
  222.8 2.2 fusion.111
  226.2 2.9 collective-permute-start.61
  230.4 3.6 %collective-permute-start.59 = (bf16[320,384]{1,0:T(8,128)(2,1)S(1)}, bf16[320,384]{1,0:T(8,128)(2,1)S(1)}, u32[]{:S(2)}, u32[]{:S(2)}) collective-permute-start(bf16[320,384]{1,0:T(8,128)(2,1)S(1)} %broadcast_select_fusion.28), channel_id=1, source_target_pairs={{0,8},{4,12},{8,0},{12,4},{16,24},{20,28},{24,16},{28,20},{1,9},{5... | collective-permute-start | bytes 737288 | tf_op jit(solution)/shard_map/ppermute | solution.py:169
  234.0 2.2 fusion.119
  237.4 3.3 %collective-permute-start.63 = (bf16[320,384]{1,0:T(8,128)(2,1)S(1)}, bf16[320,384]{1,0:T(8,128)(2,1)S(1)}, u32[]{:S(2)}, u32[]{:S(2)}) collective-permute-start(bf16[320,384]{1,0:T(8,128)(2,1)S(1)} %broadcast_select_fusion.23), channel_id=1, source_target_pairs={{0,8},{4,12},{8,0},{12,4},{16,24},{20,28},{24,16},{28,20},{1,9},{5... | collective-permute-start | bytes 737288 | tf_op jit(solution)/shard_map/ppermute | solution.py:169
  241.8 3.8 %collective-permute-start.67 = (bf16[320,384]{1,0:T(8,128)(2,1)S(1)}, bf16[320,384]{1,0:T(8,128)(2,1)S(1)}, u32[]{:S(2)}, u32[]{:S(2)}) collective-permute-start(bf16[320,384]{1,0:T(8,128)(2,1)S(1)} %broadcast_select_fusion.18), channel_id=1, source_target_pairs={{0,8},{4,12},{8,0},{12,4},{16,24},{20,28},{24,16},{28,20},{1,9},{5... | collective-permute-start | bytes 737288 | tf_op jit(solution)/shard_map/ppermute | solution.py:169
  253.2 4.1 %collective-permute-start.71 = (bf16[320,384]{1,0:T(8,128)(2,1)S(1)}, bf16[320,384]{1,0:T(8,128)(2,1)S(1)}, u32[]{:S(2)}, u32[]{:S(2)}) collective-permute-start(bf16[320,384]{1,0:T(8,128)(2,1)S(1)} %broadcast_select_fusion.16), channel_id=1, source_target_pairs={{0,8},{4,12},{8,0},{12,4},{16,24},{20,28},{24,16},{28,20},{1,9},{5... | collective-permute-start | bytes 737288 | tf_op jit(solution)/shard_map/ppermute | solution.py:169
  264.0 5.3 %collective-permute-start.73 = (bf16[320,384]{1,0:T(8,128)(2,1)S(1)}, bf16[320,384]{1,0:T(8,128)(2,1)S(1)}, u32[]{:S(2)}, u32[]{:S(2)}) collective-permute-start(bf16[320,384]{1,0:T(8,128)(2,1)S(1)} %pad_select_fusion), channel_id=1, source_target_pairs={{0,8},{4,12},{8,0},{12,4},{16,24},{20,28},{24,16},{28,20},{1,9},{5... | collective-permute-start | bytes 737288 | tf_op jit(solution)/shard_map/ppermute | solution.py:169
  272.9 3.2 %collective-permute-done.73 = bf16[320,384]{1,0:T(8,128)(2,1)S(1)} collective-permute-done((bf16[320,384]{1,0:T(8,128)(2,1)S(1)}, bf16[320,384]{1,0:T(8,128)(2,1)S(1)}, u32[]{:S(2)}, u32[]{:S(2)}) %collective-permute-start.73) | collective-permute-done | bytes 245792 | tf_op jit(solution)/shard_map/ppermute | solution.py:169
  285.8 2.9 adam_piece.4
  289.9 2.9 adam_piece.5
  292.8 7.5 %collective-permute-done.78.came_ref = bf16[768,384]{1,0:T(8,128)(2,1)S(1)} collective-permute-done((bf16[768,384]{1,0:T(8,128)(2,1)S(1)}, bf16[768,384]{1,0:T(8,128)(2,1)S(1)}, u32[]{:S(2)}, u32[]{:S(2)}) %collective-permute-start.78) | collective-permute-done | bytes 589856 | tf_op jit(solution)/shard_map/ppermute | solution.py:183
  300.4 2.9 adam_piece.6
  303.3 3.4 %collective-permute-done.77.came_ref = bf16[768,384]{1,0:T(8,128)(2,1)S(1)} collective-permute-done((bf16[768,384]{1,0:T(8,128)(2,1)S(1)}, bf16[768,384]{1,0:T(8,128)(2,1)S(1)}, u32[]{:S(2)}, u32[]{:S(2)}) %collective-permute-start.77) | collective-permute-done | bytes 589856 | tf_op jit(solution)/shard_map/ppermute | solution.py:183
  306.7 2.9 adam_piece.7
  (349 shorter events, 119.2 us)
Async XLA Ops:
  8.9 22.9 %all-to-all-start = ((bf16[32,64,128]{2,1,0:T(8,128)(2,1)}), bf16[32,64,128]{2,1,0:T(8,128)(2,1)S(1)}, u32[]{:S(2)}, u32[]{:S(2)}) async-start(bf16[32,64,128]{2,1,0:T(8,128)(2,1)} %bitcast.4), calls=%async_computation | async-start | bytes 1048576 | tf_op jit(solution)/shard_map/all_to_all | solution.py:74
  16.2 183.9 %collective-permute-start.48 = (bf16[640,128]{1,0:T(8,128)(2,1)}, bf16[640,128]{1,0:T(8,128)(2,1)}, u32[]{:S(2)}, u32[]{:S(2)}) collective-permute-start(bf16[640,128]{1,0:T(8,128)(2,1)} %param.18), channel_id=1, source_target_pairs={{0,8},{4,12},{8,0},{12,4},{16,24},{20,28},{24,16},{28,20},{1,9},{5... | collective-permute-start | bytes 491528 | tf_op jit(solution)/shard_map/ppermute | solution.py:169
  18.0 32.4 %collective-permute-start = (bf16[768,768]{1,0:T(8,128)(2,1)}, bf16[768,768]{1,0:T(8,128)(2,1)}, u32[]{:S(2)}, u32[]{:S(2)}) collective-permute-start(bf16[768,768]{1,0:T(8,128)(2,1)} %get-tuple-element.145), channel_id=1, source_target_pairs={{0,4},{4,0},{8,12},{12,8},{16,20},{20,16},{24,28},{28,24},{1,5},{5... | collective-permute-start | bytes 3538952 | tf_op jit(solution)/shard_map/ppermute | solution.py:183
  50.4 28.4 %collective-permute-start.5 = (bf16[768,768]{1,0:T(8,128)(2,1)}, bf16[768,768]{1,0:T(8,128)(2,1)}, u32[]{:S(2)}, u32[]{:S(2)}) collective-permute-start(bf16[768,768]{1,0:T(8,128)(2,1)} %get-tuple-element.153), channel_id=1, source_target_pairs={{0,4},{4,0},{8,12},{12,8},{16,20},{20,16},{24,28},{28,24},{1,5},{5... | collective-permute-start | bytes 3538952 | tf_op jit(solution)/shard_map/ppermute | solution.py:183
  59.6 13.4 %collective-permute-start.4 = (bf16[320,384]{1,0:T(8,128)(2,1)}, bf16[320,384]{1,0:T(8,128)(2,1)}, u32[]{:S(2)}, u32[]{:S(2)}) collective-permute-start(bf16[320,384]{1,0:T(8,128)(2,1)} %get-tuple-element.302), channel_id=1, source_target_pairs={{0,8},{4,12},{8,0},{12,4},{16,24},{20,28},{24,16},{28,20},{1,9},{5... | collective-permute-start | bytes 737288 | tf_op jit(solution)/shard_map/ppermute | solution.py:169
  66.4 28.7 %collective-permute-start.8 = (bf16[320,384]{1,0:T(8,128)(2,1)}, bf16[320,384]{1,0:T(8,128)(2,1)S(1)}, u32[]{:S(2)}, u32[]{:S(2)}) collective-permute-start(bf16[320,384]{1,0:T(8,128)(2,1)} %get-tuple-element.300), channel_id=1, source_target_pairs={{0,8},{4,12},{8,0},{12,4},{16,24},{20,28},{24,16},{28,20},{1,9},{5... | collective-permute-start | bytes 737288 | tf_op jit(solution)/shard_map/ppermute | solution.py:169
  78.9 16.3 %collective-permute-start.9 = (bf16[320,384]{1,0:T(8,128)(2,1)S(1)}, bf16[320,384]{1,0:T(8,128)(2,1)S(1)}, u32[]{:S(2)}, u32[]{:S(2)}) collective-permute-start(bf16[320,384]{1,0:T(8,128)(2,1)S(1)} %add_convert_fusion.35), channel_id=1, source_target_pairs={{8,16},{12,20},{16,8},{20,12},{9,17},{13,21},{17,9},{21,13},{10,18... | collective-permute-start | bytes 737288 | tf_op jit(solution)/shard_map/ppermute | solution.py:169
  83.6 16.3 %collective-permute-start.7 = (bf16[320,384]{1,0:T(8,128)(2,1)S(1)}, bf16[320,384]{1,0:T(8,128)(2,1)S(1)}, u32[]{:S(2)}, u32[]{:S(2)}) collective-permute-start(bf16[320,384]{1,0:T(8,128)(2,1)S(1)} %add_convert_fusion.33), channel_id=1, source_target_pairs={{8,16},{12,20},{16,8},{20,12},{9,17},{13,21},{17,9},{21,13},{10,18... | collective-permute-start | bytes 737288 | tf_op jit(solution)/shard_map/ppermute | solution.py:169
  84.5 15.3 %collective-permute-start.6 = (bf16[320,384]{1,0:T(8,128)(2,1)S(1)}, bf16[320,384]{1,0:T(8,128)(2,1)S(1)}, u32[]{:S(2)}, u32[]{:S(2)}) collective-permute-start(bf16[320,384]{1,0:T(8,128)(2,1)S(1)} %fusion.175), channel_id=1, source_target_pairs={{0,8},{4,12},{8,0},{12,4},{16,24},{20,28},{24,16},{28,20},{1,9},{5... | collective-permute-start | bytes 737288 | tf_op jit(solution)/shard_map/ppermute | solution.py:169
  99.9 13.6 %collective-permute-start.15 = (bf16[320,384]{1,0:T(8,128)(2,1)S(1)}, bf16[320,384]{1,0:T(8,128)(2,1)S(1)}, u32[]{:S(2)}, u32[]{:S(2)}) collective-permute-start(bf16[320,384]{1,0:T(8,128)(2,1)S(1)} %add_convert_fusion.29), channel_id=1, source_target_pairs={{8,16},{12,20},{16,8},{20,12},{9,17},{13,21},{17,9},{21,13},{10,18... | collective-permute-start | bytes 737288 | tf_op jit(solution)/shard_map/ppermute | solution.py:169
  100.7 12.8 %collective-permute-start.14 = (bf16[320,384]{1,0:T(8,128)(2,1)S(1)}, bf16[320,384]{1,0:T(8,128)(2,1)S(1)}, u32[]{:S(2)}, u32[]{:S(2)}) collective-permute-start(bf16[320,384]{1,0:T(8,128)(2,1)S(1)} %fusion.177), channel_id=1, source_target_pairs={{0,8},{4,12},{8,0},{12,4},{16,24},{20,28},{24,16},{28,20},{1,9},{5... | collective-permute-start | bytes 737288 | tf_op jit(solution)/shard_map/ppermute | solution.py:169
  107.3 11.3 %collective-permute-start.17 = (bf16[320,384]{1,0:T(8,128)(2,1)S(1)}, bf16[320,384]{1,0:T(8,128)(2,1)S(1)}, u32[]{:S(2)}, u32[]{:S(2)}) collective-permute-start(bf16[320,384]{1,0:T(8,128)(2,1)S(1)} %add_convert_fusion.27), channel_id=1, source_target_pairs={{8,16},{12,20},{16,8},{20,12},{9,17},{13,21},{17,9},{21,13},{10,18... | collective-permute-start | bytes 737288 | tf_op jit(solution)/shard_map/ppermute | solution.py:169
  108.1 12.3 %collective-permute-start.16 = (bf16[320,384]{1,0:T(8,128)(2,1)S(1)}, bf16[320,384]{1,0:T(8,128)(2,1)S(1)}, u32[]{:S(2)}, u32[]{:S(2)}) collective-permute-start(bf16[320,384]{1,0:T(8,128)(2,1)S(1)} %fusion.178), channel_id=1, source_target_pairs={{0,8},{4,12},{8,0},{12,4},{16,24},{20,28},{24,16},{28,20},{1,9},{5... | collective-permute-start | bytes 737288 | tf_op jit(solution)/shard_map/ppermute | solution.py:169
  124.0 11.1 %collective-permute-start.23 = (bf16[320,384]{1,0:T(8,128)(2,1)S(1)}, bf16[320,384]{1,0:T(8,128)(2,1)S(1)}, u32[]{:S(2)}, u32[]{:S(2)}) collective-permute-start(bf16[320,384]{1,0:T(8,128)(2,1)S(1)} %add_convert_fusion.21), channel_id=1, source_target_pairs={{8,16},{12,20},{16,8},{20,12},{9,17},{13,21},{17,9},{21,13},{10,18... | collective-permute-start | bytes 737288 | tf_op jit(solution)/shard_map/ppermute | solution.py:169
  135.2 10.8 %collective-permute-start.29 = (bf16[320,384]{1,0:T(8,128)(2,1)S(1)}, bf16[320,384]{1,0:T(8,128)(2,1)S(1)}, u32[]{:S(2)}, u32[]{:S(2)}) collective-permute-start(bf16[320,384]{1,0:T(8,128)(2,1)S(1)} %add_convert_fusion.17), channel_id=1, source_target_pairs={{8,16},{12,20},{16,8},{20,12},{9,17},{13,21},{17,9},{21,13},{10,18... | collective-permute-start | bytes 737288 | tf_op jit(solution)/shard_map/ppermute | solution.py:169
  136.0 11.5 %collective-permute-start.28 = (bf16[320,384]{1,0:T(8,128)(2,1)S(1)}, bf16[320,384]{1,0:T(8,128)(2,1)S(1)}, u32[]{:S(2)}, u32[]{:S(2)}) collective-permute-start(bf16[320,384]{1,0:T(8,128)(2,1)S(1)} %fusion.183), channel_id=1, source_target_pairs={{0,8},{4,12},{8,0},{12,4},{16,24},{20,28},{24,16},{28,20},{1,9},{5... | collective-permute-start | bytes 737288 | tf_op jit(solution)/shard_map/ppermute | solution.py:169
  143.5 13.4 %collective-permute-start.30 = (bf16[320,384]{1,0:T(8,128)(2,1)S(1)}, bf16[320,384]{1,0:T(8,128)(2,1)S(1)}, u32[]{:S(2)}, u32[]{:S(2)}) collective-permute-start(bf16[320,384]{1,0:T(8,128)(2,1)S(1)} %fusion.184), channel_id=1, source_target_pairs={{0,8},{4,12},{8,0},{12,4},{16,24},{20,28},{24,16},{28,20},{1,9},{5... | collective-permute-start | bytes 737288 | tf_op jit(solution)/shard_map/ppermute | solution.py:169
  145.3 11.6 %collective-permute-start.31 = (bf16[320,384]{1,0:T(8,128)(2,1)S(1)}, bf16[320,384]{1,0:T(8,128)(2,1)S(1)}, u32[]{:S(2)}, u32[]{:S(2)}) collective-permute-start(bf16[320,384]{1,0:T(8,128)(2,1)S(1)} %add_convert_fusion.15), channel_id=1, source_target_pairs={{8,16},{12,20},{16,8},{20,12},{9,17},{13,21},{17,9},{21,13},{10,18... | collective-permute-start | bytes 737288 | tf_op jit(solution)/shard_map/ppermute | solution.py:169
  147.6 13.1 %collective-permute-start.33 = (bf16[320,384]{1,0:T(8,128)(2,1)S(1)}, bf16[320,384]{1,0:T(8,128)(2,1)S(1)}, u32[]{:S(2)}, u32[]{:S(2)}) collective-permute-start(bf16[320,384]{1,0:T(8,128)(2,1)S(1)} %add_convert_fusion.13), channel_id=1, source_target_pairs={{8,16},{12,20},{16,8},{20,12},{9,17},{13,21},{17,9},{21,13},{10,18... | collective-permute-start | bytes 737288 | tf_op jit(solution)/shard_map/ppermute | solution.py:169
  162.7 11.0 %collective-permute-start.36 = (bf16[320,384]{1,0:T(8,128)(2,1)S(1)}, bf16[320,384]{1,0:T(8,128)(2,1)S(1)}, u32[]{:S(2)}, u32[]{:S(2)}) collective-permute-start(bf16[320,384]{1,0:T(8,128)(2,1)S(1)} %fusion.187), channel_id=1, source_target_pairs={{0,8},{4,12},{8,0},{12,4},{16,24},{20,28},{24,16},{28,20},{1,9},{5... | collective-permute-start | bytes 737288 | tf_op jit(solution)/shard_map/ppermute | solution.py:169
  167.5 11.6 %collective-permute-start.38 = (bf16[320,384]{1,0:T(8,128)(2,1)S(1)}, bf16[320,384]{1,0:T(8,128)(2,1)S(1)}, u32[]{:S(2)}, u32[]{:S(2)}) collective-permute-start(bf16[320,384]{1,0:T(8,128)(2,1)S(1)} %fusion.188), channel_id=1, source_target_pairs={{0,8},{4,12},{8,0},{12,4},{16,24},{20,28},{24,16},{28,20},{1,9},{5... | collective-permute-start | bytes 737288 | tf_op jit(solution)/shard_map/ppermute | solution.py:169
  173.8 10.9 %collective-permute-start.41 = (bf16[320,384]{1,0:T(8,128)(2,1)S(1)}, bf16[320,384]{1,0:T(8,128)(2,1)S(1)}, u32[]{:S(2)}, u32[]{:S(2)}) collective-permute-start(bf16[320,384]{1,0:T(8,128)(2,1)S(1)} %collective-permute-done.36), channel_id=1, source_target_pairs={{8,16},{12,20},{16,8},{20,12},{9,17},{13,21},{17,9},{21,13},{10,18... | collective-permute-start | bytes 737288 | tf_op jit(solution)/shard_map/ppermute | solution.py:169
  179.1 11.2 %collective-permute-start.43 = (bf16[320,384]{1,0:T(8,128)(2,1)S(1)}, bf16[320,384]{1,0:T(8,128)(2,1)S(1)}, u32[]{:S(2)}, u32[]{:S(2)}) collective-permute-start(bf16[320,384]{1,0:T(8,128)(2,1)S(1)} %collective-permute-done.38), channel_id=1, source_target_pairs={{8,16},{12,20},{16,8},{20,12},{9,17},{13,21},{17,9},{21,13},{10,18... | collective-permute-start | bytes 737288 | tf_op jit(solution)/shard_map/ppermute | solution.py:169
  184.7 12.7 %collective-permute-start.50 = (bf16[320,384]{1,0:T(8,128)(2,1)S(1)}, bf16[320,384]{1,0:T(8,128)(2,1)S(1)}, u32[]{:S(2)}, u32[]{:S(2)}) collective-permute-start(bf16[320,384]{1,0:T(8,128)(2,1)S(1)} %collective-permute-done.40), channel_id=1, source_target_pairs={{8,16},{12,20},{16,8},{20,12},{9,17},{13,21},{17,9},{21,13},{10,18... | collective-permute-start | bytes 737288 | tf_op jit(solution)/shard_map/ppermute | solution.py:169
  185.5 11.8 %collective-permute-start.49 = (bf16[320,384]{1,0:T(8,128)(2,1)S(1)}, bf16[320,384]{1,0:T(8,128)(2,1)S(1)}, u32[]{:S(2)}, u32[]{:S(2)}) collective-permute-start(bf16[320,384]{1,0:T(8,128)(2,1)S(1)} %broadcast_select_fusion.43), channel_id=1, source_target_pairs={{0,8},{4,12},{8,0},{12,4},{16,24},{20,28},{24,16},{28,20},{1,9},{5... | collective-permute-start | bytes 737288 | tf_op jit(solution)/shard_map/ppermute | solution.py:169
  190.4 16.2 %collective-permute-start.47 = (bf16[320,384]{1,0:T(8,128)(2,1)S(1)}, bf16[320,384]{1,0:T(8,128)(2,1)S(1)}, u32[]{:S(2)}, u32[]{:S(2)}) collective-permute-start(bf16[320,384]{1,0:T(8,128)(2,1)S(1)} %collective-permute-done.42), channel_id=1, source_target_pairs={{8,16},{12,20},{16,8},{20,12},{9,17},{13,21},{17,9},{21,13},{10,18... | collective-permute-start | bytes 737288 | tf_op jit(solution)/shard_map/ppermute | solution.py:169
  191.6 14.9 %collective-permute-start.46 = (bf16[320,384]{1,0:T(8,128)(2,1)S(1)}, bf16[320,384]{1,0:T(8,128)(2,1)S(1)}, u32[]{:S(2)}, u32[]{:S(2)}) collective-permute-start(bf16[320,384]{1,0:T(8,128)(2,1)S(1)} %broadcast_select_fusion.42), channel_id=1, source_target_pairs={{0,8},{4,12},{8,0},{12,4},{16,24},{20,28},{24,16},{28,20},{1,9},{5... | collective-permute-start | bytes 737288 | tf_op jit(solution)/shard_map/ppermute | solution.py:169
  197.4 16.6 %collective-permute-start.52 = (bf16[320,384]{1,0:T(8,128)(2,1)S(1)}, bf16[320,384]{1,0:T(8,128)(2,1)S(1)}, u32[]{:S(2)}, u32[]{:S(2)}) collective-permute-start(bf16[320,384]{1,0:T(8,128)(2,1)S(1)} %collective-permute-done.49), channel_id=1, source_target_pairs={{8,16},{12,20},{16,8},{20,12},{9,17},{13,21},{17,9},{21,13},{10,18... | collective-permute-start | bytes 737288 | tf_op jit(solution)/shard_map/ppermute | solution.py:169
  200.1 13.9 %collective-permute-start.51 = (bf16[320,384]{1,0:T(8,128)(2,1)S(1)}, bf16[320,384]{1,0:T(8,128)(2,1)S(1)}, u32[]{:S(2)}, u32[]{:S(2)}) collective-permute-start(bf16[320,384]{1,0:T(8,128)(2,1)S(1)} %broadcast_select_fusion.41), channel_id=1, source_target_pairs={{0,8},{4,12},{8,0},{12,4},{16,24},{20,28},{24,16},{28,20},{1,9},{5... | collective-permute-start | bytes 737288 | tf_op jit(solution)/shard_map/ppermute | solution.py:169
  206.6 11.6 %collective-permute-start.56 = (bf16[320,384]{1,0:T(8,128)(2,1)S(1)}, bf16[320,384]{1,0:T(8,128)(2,1)S(1)}, u32[]{:S(2)}, u32[]{:S(2)}) collective-permute-start(bf16[320,384]{1,0:T(8,128)(2,1)S(1)} %collective-permute-done.46), channel_id=1, source_target_pairs={{8,16},{12,20},{16,8},{20,12},{9,17},{13,21},{17,9},{21,13},{10,18... | collective-permute-start | bytes 737288 | tf_op jit(solution)/shard_map/ppermute | solution.py:169
  207.4 10.9 %collective-permute-start.55 = (bf16[320,384]{1,0:T(8,128)(2,1)S(1)}, bf16[320,384]{1,0:T(8,128)(2,1)S(1)}, u32[]{:S(2)}, u32[]{:S(2)}) collective-permute-start(bf16[320,384]{1,0:T(8,128)(2,1)S(1)} %broadcast_select_fusion.36), channel_id=1, source_target_pairs={{0,8},{4,12},{8,0},{12,4},{16,24},{20,28},{24,16},{28,20},{1,9},{5... | collective-permute-start | bytes 737288 | tf_op jit(solution)/shard_map/ppermute | solution.py:169
  214.1 11.3 %collective-permute-start.54 = (bf16[320,384]{1,0:T(8,128)(2,1)S(1)}, bf16[320,384]{1,0:T(8,128)(2,1)S(1)}, u32[]{:S(2)}, u32[]{:S(2)}) collective-permute-start(bf16[320,384]{1,0:T(8,128)(2,1)S(1)} %collective-permute-done.51), channel_id=1, source_target_pairs={{8,16},{12,20},{16,8},{20,12},{9,17},{13,21},{17,9},{21,13},{10,18... | collective-permute-start | bytes 737288 | tf_op jit(solution)/shard_map/ppermute | solution.py:169
  218.3 11.3 %collective-permute-start.58 = (bf16[320,384]{1,0:T(8,128)(2,1)S(1)}, bf16[320,384]{1,0:T(8,128)(2,1)S(1)}, u32[]{:S(2)}, u32[]{:S(2)}) collective-permute-start(bf16[320,384]{1,0:T(8,128)(2,1)S(1)} %collective-permute-done.55), channel_id=1, source_target_pairs={{8,16},{12,20},{16,8},{20,12},{9,17},{13,21},{17,9},{21,13},{10,18... | collective-permute-start | bytes 737288 | tf_op jit(solution)/shard_map/ppermute | solution.py:169
  225.5 11.1 %collective-permute-start.62 = (bf16[320,384]{1,0:T(8,128)(2,1)S(1)}, bf16[320,384]{1,0:T(8,128)(2,1)S(1)}, u32[]{:S(2)}, u32[]{:S(2)}) collective-permute-start(bf16[320,384]{1,0:T(8,128)(2,1)S(1)} %collective-permute-done.53), channel_id=1, source_target_pairs={{8,16},{12,20},{16,8},{20,12},{9,17},{13,21},{17,9},{21,13},{10,18... | collective-permute-start | bytes 737288 | tf_op jit(solution)/shard_map/ppermute | solution.py:169
  229.7 11.3 %collective-permute-start.60 = (bf16[320,384]{1,0:T(8,128)(2,1)S(1)}, bf16[320,384]{1,0:T(8,128)(2,1)S(1)}, u32[]{:S(2)}, u32[]{:S(2)}) collective-permute-start(bf16[320,384]{1,0:T(8,128)(2,1)S(1)} %collective-permute-done.57), channel_id=1, source_target_pairs={{8,16},{12,20},{16,8},{20,12},{9,17},{13,21},{17,9},{21,13},{10,18... | collective-permute-start | bytes 737288 | tf_op jit(solution)/shard_map/ppermute | solution.py:169
  236.7 11.6 %collective-permute-start.64 = (bf16[320,384]{1,0:T(8,128)(2,1)S(1)}, bf16[320,384]{1,0:T(8,128)(2,1)S(1)}, u32[]{:S(2)}, u32[]{:S(2)}) collective-permute-start(bf16[320,384]{1,0:T(8,128)(2,1)S(1)} %collective-permute-done.61), channel_id=1, source_target_pairs={{8,16},{12,20},{16,8},{20,12},{9,17},{13,21},{17,9},{21,13},{10,18... | collective-permute-start | bytes 737288 | tf_op jit(solution)/shard_map/ppermute | solution.py:169
  237.4 10.9 %collective-permute-start.63 = (bf16[320,384]{1,0:T(8,128)(2,1)S(1)}, bf16[320,384]{1,0:T(8,128)(2,1)S(1)}, u32[]{:S(2)}, u32[]{:S(2)}) collective-permute-start(bf16[320,384]{1,0:T(8,128)(2,1)S(1)} %broadcast_select_fusion.23), channel_id=1, source_target_pairs={{0,8},{4,12},{8,0},{12,4},{16,24},{20,28},{24,16},{28,20},{1,9},{5... | collective-permute-start | bytes 737288 | tf_op jit(solution)/shard_map/ppermute | solution.py:169
  241.1 11.4 %collective-permute-start.68 = (bf16[320,384]{1,0:T(8,128)(2,1)S(1)}, bf16[320,384]{1,0:T(8,128)(2,1)S(1)}, u32[]{:S(2)}, u32[]{:S(2)}) collective-permute-start(bf16[320,384]{1,0:T(8,128)(2,1)S(1)} %collective-permute-done.59), channel_id=1, source_target_pairs={{8,16},{12,20},{16,8},{20,12},{9,17},{13,21},{17,9},{21,13},{10,18... | collective-permute-start | bytes 737288 | tf_op jit(solution)/shard_map/ppermute | solution.py:169
  248.3 12.5 %collective-permute-start.65 = (bf16[320,384]{1,0:T(8,128)(2,1)S(1)}, bf16[320,384]{1,0:T(8,128)(2,1)S(1)}, u32[]{:S(2)}, u32[]{:S(2)}) collective-permute-start(bf16[320,384]{1,0:T(8,128)(2,1)S(1)} %broadcast_select_fusion.17), channel_id=1, source_target_pairs={{0,8},{4,12},{8,0},{12,4},{16,24},{20,28},{24,16},{28,20},{1,9},{5... | collective-permute-start | bytes 737288 | tf_op jit(solution)/shard_map/ppermute | solution.py:169
  249.5 11.3 %collective-permute-start.66 = (bf16[320,384]{1,0:T(8,128)(2,1)S(1)}, bf16[320,384]{1,0:T(8,128)(2,1)S(1)}, u32[]{:S(2)}, u32[]{:S(2)}) collective-permute-start(bf16[320,384]{1,0:T(8,128)(2,1)S(1)} %collective-permute-done.63), channel_id=1, source_target_pairs={{8,16},{12,20},{16,8},{20,12},{9,17},{13,21},{17,9},{21,13},{10,18... | collective-permute-start | bytes 737288 | tf_op jit(solution)/shard_map/ppermute | solution.py:169
  258.5 27.2 %collective-permute-start.80 = (bf16[768,384]{1,0:T(8,128)(2,1)S(1)}, bf16[768,384]{1,0:T(8,128)(2,1)S(1)}, u32[]{:S(2)}, u32[]{:S(2)}) collective-permute-start(bf16[768,384]{1,0:T(8,128)(2,1)S(1)} %add_convert_fusion.1), channel_id=1, source_target_pairs={{0,4},{4,0},{8,12},{12,8},{16,20},{20,16},{24,28},{28,24},{1,5},{5... | collective-permute-start | bytes 1769480 | tf_op jit(solution)/shard_map/ppermute | solution.py:183
  260.9 10.9 %collective-permute-start.69 = (bf16[320,384]{1,0:T(8,128)(2,1)S(1)}, bf16[320,384]{1,0:T(8,128)(2,1)S(1)}, u32[]{:S(2)}, u32[]{:S(2)}) collective-permute-start(bf16[320,384]{1,0:T(8,128)(2,1)S(1)} %pad_select_fusion.1), channel_id=1, source_target_pairs={{0,8},{4,12},{8,0},{12,4},{16,24},{20,28},{24,16},{28,20},{1,9},{5... | collective-permute-start | bytes 737288 | tf_op jit(solution)/shard_map/ppermute | solution.py:169
  261.0 11.9 %collective-permute-start.70 = (bf16[320,384]{1,0:T(8,128)(2,1)S(1)}, bf16[320,384]{1,0:T(8,128)(2,1)S(1)}, u32[]{:S(2)}, u32[]{:S(2)}) collective-permute-start(bf16[320,384]{1,0:T(8,128)(2,1)S(1)} %collective-permute-done.65), channel_id=1, source_target_pairs={{8,16},{12,20},{16,8},{20,12},{9,17},{13,21},{17,9},{21,13},{10,18... | collective-permute-start | bytes 737288 | tf_op jit(solution)/shard_map/ppermute | solution.py:169
  263.0 13.1 %collective-permute-start.74 = (bf16[320,384]{1,0:T(8,128)(2,1)S(1)}, bf16[320,384]{1,0:T(8,128)(2,1)S(1)}, u32[]{:S(2)}, u32[]{:S(2)}) collective-permute-start(bf16[320,384]{1,0:T(8,128)(2,1)S(1)} %collective-permute-done.71), channel_id=1, source_target_pairs={{8,16},{12,20},{16,8},{20,12},{9,17},{13,21},{17,9},{21,13},{10,18... | collective-permute-start | bytes 737288 | tf_op jit(solution)/shard_map/ppermute | solution.py:169
  264.0 12.2 %collective-permute-start.73 = (bf16[320,384]{1,0:T(8,128)(2,1)S(1)}, bf16[320,384]{1,0:T(8,128)(2,1)S(1)}, u32[]{:S(2)}, u32[]{:S(2)}) collective-permute-start(bf16[320,384]{1,0:T(8,128)(2,1)S(1)} %pad_select_fusion), channel_id=1, source_target_pairs={{0,8},{4,12},{8,0},{12,4},{16,24},{20,28},{24,16},{28,20},{1,9},{5... | collective-permute-start | bytes 737288 | tf_op jit(solution)/shard_map/ppermute | solution.py:169
  271.8 18.1 %collective-permute-start.79 = (bf16[768,384]{1,0:T(8,128)(2,1)S(1)}, bf16[768,384]{1,0:T(8,128)(2,1)S(1)}, u32[]{:S(2)}, u32[]{:S(2)}) collective-permute-start(bf16[768,384]{1,0:T(8,128)(2,1)S(1)} %add_convert_fusion.2), channel_id=1, source_target_pairs={{0,4},{4,0},{8,12},{12,8},{16,20},{20,16},{24,28},{28,24},{1,5},{5... | collective-permute-start | bytes 1769480 | tf_op jit(solution)/shard_map/ppermute | solution.py:183
  280.7 19.7 %collective-permute-start.78 = (bf16[768,384]{1,0:T(8,128)(2,1)S(1)}, bf16[768,384]{1,0:T(8,128)(2,1)S(1)}, u32[]{:S(2)}, u32[]{:S(2)}) collective-permute-start(bf16[768,384]{1,0:T(8,128)(2,1)S(1)} %add_convert_fusion.3), channel_id=1, source_target_pairs={{0,4},{4,0},{8,12},{12,8},{16,20},{20,16},{24,28},{28,24},{1,5},{5... | collective-permute-start | bytes 1769480 | tf_op jit(solution)/shard_map/ppermute | solution.py:183
  283.8 22.9 %collective-permute-start.77 = (bf16[768,384]{1,0:T(8,128)(2,1)S(1)}, bf16[768,384]{1,0:T(8,128)(2,1)S(1)}, u32[]{:S(2)}, u32[]{:S(2)}) collective-permute-start(bf16[768,384]{1,0:T(8,128)(2,1)S(1)} %add_convert_fusion.4), channel_id=1, source_target_pairs={{0,4},{4,0},{8,12},{12,8},{16,20},{20,16},{24,28},{28,24},{1,5},{5... | collective-permute-start | bytes 1769480 | tf_op jit(solution)/shard_map/ppermute | solution.py:183
  (61 other events, 456.7 us)

commit v5 on v4

--- a/solution.py
+++ b/solution.py
@@ -317,8 +317,9 @@
         (0, 0): [(0, 1, 0), "scales", "features"],
         (0, late): [(1, 0, 0), (1, 1, 0), "own"],
         (1, late): [(0, 0, 1)],
-        (2, 0): [(0, 1, 1)],
-        (2, late): [(1, 0, 1), (1, 1, 1)],
+(3, 0): [(0, 1, 1)],
+        (4, 0): [(1, 0, 1)],
+        (5, 0): [(1, 1, 1)],
     }
     for tick, part in [(t, p) for t in range(2 * units + line) for p in range(streams)]:
         back_tick = tick - units

time: 314 us -> 309 us (0.984)
  starting transfers between devices: 154 us -> 146 us
    ppermute x69, starting transfers between devices: 135 us -> 128 us  [swap(): return lax.ppermute(value, 'dp', pairs)]
    unnamed x52 -> x48, local copies, waits for them, and re-layouts: 7.07 us -> 6.73 us
where the time goes in v5:
time: 309 us; the launch traced here: 305 us
  starting transfers between devices  146 us (47%)
  matrix products  55 us (18%)
  waiting for transfers between devices  50 us (16%)
  local copies, waits for them, and re-layouts  16.4 us (5%)
  other arithmetic  14.9 us (5%)
  Pallas kernels  11.7 us (4%)
  blocking collectives  7.72 us (2%)
  between operations  3.36 us (1%)
    ppermute x69, starting transfers between devices, swap(): return lax.ppermute(value, 'dp', pairs)  128 us
    dot_general x22, matrix products, dot32(): return jnp.dot(left, right, preferred_element_type=jnp.float32)  30.4 us
    ppermute x69, waiting for transfers between devices, swap(): return lax.ppermute(value, 'dp', pairs)  21.2 us
    dot_general x12, matrix products, gradient_term(): lax.dot_general(features[unit // pieces][:, rows], jnp.concatenate(arrive...  18.7 us
    ppermute x6, waiting for transfers between devices, turn(): return lax.ppermute(value, 'dp', pairs)  11.8 us
    pallas_call x4, Pallas kernels, adam_piece(): pl.pallas_call(adam_kernel, grid=(3,), in_specs=[piece, piece, column, co...  11.7 us
    ppermute x6, waiting for transfers between devices, mp_sum(): lax.ppermute(value, 'mp', [(m, m ^ step) for m in range(model_count)])  9.24 us
    all_to_all x1, waiting for transfers between devices, route(): lax.all_to_all(outgoing.reshape(devices_all, line * lot, patch_width), ('...  7.78 us
  transfers between devices with their start and end apart: 82, of which 22 were waited for; matrix products, arithmetic and copies ran while one was open for 25% of the time, Pallas kernels for 3%

profile of v5, /device:TPU:0, one launch (start us, length us, event | category | flops | bytes accessed | tf_op | source)
XLA Modules:
  0.0 305.0 jit_solution(934084027076495212)
XLA Ops:
  1.4 2.6 convert.14
  8.9 7.3 %all-to-all-start = ((bf16[32,64,128]{2,1,0:T(8,128)(2,1)}), bf16[32,64,128]{2,1,0:T(8,128)(2,1)S(1)}, u32[]{:S(2)}, u32[]{:S(2)}) async-start(bf16[32,64,128]{2,1,0:T(8,128)(2,1)} %bitcast.4), calls=%async_computation | async-start | bytes 1048576 | tf_op jit(solution)/shard_map/all_to_all | solution.py:74
  21.6 2.4 constant_dynamic-update-slice_fusion.1
  24.0 7.8 %all-to-all-done = bf16[32,64,128]{2,1,0:T(8,128)(2,1)S(1)} async-done(((bf16[32,64,128]{2,1,0:T(8,128)(2,1)}), bf16[32,64,128]{2,1,0:T(8,128)(2,1)S(1)}, u32[]{:S(2)}, u32[]{:S(2)}) %all-to-all-start) | async-done | bytes 524320 | tf_op jit(solution)/shard_map/all_to_all | solution.py:74
  33.1 7.7 %all_gather.3 = bf16[4,640,128]{2,1,0:T(8,128)(2,1)S(1)} all-gather(bf16[4,160,128]{2,1,0:T(8,128)(2,1)S(1)} %bitcast.75), channel_id=1, replica_groups=mesh['dp'=8,'mp'=4] {'mp'}, dimensions={1}, use_global_device_ids=true | all-gather | bytes 819200 | tf_op jit(solution)/shard_map/all_gather | solution.py:216
  40.9 3.5 %fusion.3 = f32[320]{0:T(512)S(1)} fusion(bf16[128,6144]{1,0:T(8,128)(2,1)S(1)} %copy-done.9, bf16[160,128]{1,0:T(8,128)(2,1)S(1)} %get-tuple-element.349, bf16[160,128]{1,0:T(8,128)(2,1)S(1)} %get-tuple-element.350), kind=kOutput, calls=%fused_computation.6 | convolution fusion | flops 521174720 | bytes 1656064 | tf_op jit(solution)/shard_map/dot_general | solution.py:37
  44.4 2.9 fusion.5
  47.3 2.9 fusion.1
  51.6 3.1 %constant_dynamic-update-slice_fusion.3 = bf16[1536,768]{1,0:T(8,128)(2,1)} fusion(bf16[768,768]{1,0:T(8,128)(2,1)} %get-tuple-element.153), kind=kLoop, calls=%fused_computation.367 | loop fusion | bytes 2359296
  70.4 2.6 collective-permute-done.4
  79.8 2.5 fusion.135
  84.3 7.6 %collective-permute-start.6 = (bf16[320,384]{1,0:T(8,128)(2,1)S(1)}, bf16[320,384]{1,0:T(8,128)(2,1)S(1)}, u32[]{:S(2)}, u32[]{:S(2)}) collective-permute-start(bf16[320,384]{1,0:T(8,128)(2,1)S(1)} %fusion.175), channel_id=1, source_target_pairs={{0,8},{4,12},{8,0},{12,4},{16,24},{20,28},{24,16},{28,20},{1,9},{5... | collective-permute-start | bytes 737288 | tf_op jit(solution)/shard_map/ppermute | solution.py:169
  98.0 4.7 %collective-permute-start.14 = (bf16[320,384]{1,0:T(8,128)(2,1)S(1)}, bf16[320,384]{1,0:T(8,128)(2,1)S(1)}, u32[]{:S(2)}, u32[]{:S(2)}) collective-permute-start(bf16[320,384]{1,0:T(8,128)(2,1)S(1)} %fusion.177), channel_id=1, source_target_pairs={{0,8},{4,12},{8,0},{12,4},{16,24},{20,28},{24,16},{28,20},{1,9},{5... | collective-permute-start | bytes 737288 | tf_op jit(solution)/shard_map/ppermute | solution.py:169
  105.3 3.3 %collective-permute-start.16 = (bf16[320,384]{1,0:T(8,128)(2,1)S(1)}, bf16[320,384]{1,0:T(8,128)(2,1)S(1)}, u32[]{:S(2)}, u32[]{:S(2)}) collective-permute-start(bf16[320,384]{1,0:T(8,128)(2,1)S(1)} %fusion.178), channel_id=1, source_target_pairs={{0,8},{4,12},{8,0},{12,4},{16,24},{20,28},{24,16},{28,20},{1,9},{5... | collective-permute-start | bytes 737288 | tf_op jit(solution)/shard_map/ppermute | solution.py:169
  109.6 4.3 %collective-permute-start.18 = (bf16[320,384]{1,0:T(8,128)(2,1)S(1)}, bf16[320,384]{1,0:T(8,128)(2,1)S(1)}, u32[]{:S(2)}, u32[]{:S(2)}) collective-permute-start(bf16[320,384]{1,0:T(8,128)(2,1)S(1)} %fusion.179), channel_id=1, source_target_pairs={{0,8},{4,12},{8,0},{12,4},{16,24},{20,28},{24,16},{28,20},{1,9},{5... | collective-permute-start | bytes 737288 | tf_op jit(solution)/shard_map/ppermute | solution.py:169
  120.5 4.2 %collective-permute-start.22 = (bf16[320,384]{1,0:T(8,128)(2,1)S(1)}, bf16[320,384]{1,0:T(8,128)(2,1)S(1)}, u32[]{:S(2)}, u32[]{:S(2)}) collective-permute-start(bf16[320,384]{1,0:T(8,128)(2,1)S(1)} %fusion.181), channel_id=1, source_target_pairs={{0,8},{4,12},{8,0},{12,4},{16,24},{20,28},{24,16},{28,20},{1,9},{5... | collective-permute-start | bytes 737288 | tf_op jit(solution)/shard_map/ppermute | solution.py:169
  127.3 3.2 %collective-permute-start.24 = (bf16[320,384]{1,0:T(8,128)(2,1)S(1)}, bf16[320,384]{1,0:T(8,128)(2,1)S(1)}, u32[]{:S(2)}, u32[]{:S(2)}) collective-permute-start(bf16[320,384]{1,0:T(8,128)(2,1)S(1)} %fusion.182), channel_id=1, source_target_pairs={{0,8},{4,12},{8,0},{12,4},{16,24},{20,28},{24,16},{28,20},{1,9},{5... | collective-permute-start | bytes 737288 | tf_op jit(solution)/shard_map/ppermute | solution.py:169
  131.4 4.4 %collective-permute-start.28 = (bf16[320,384]{1,0:T(8,128)(2,1)S(1)}, bf16[320,384]{1,0:T(8,128)(2,1)S(1)}, u32[]{:S(2)}, u32[]{:S(2)}) collective-permute-start(bf16[320,384]{1,0:T(8,128)(2,1)S(1)} %fusion.183), channel_id=1, source_target_pairs={{0,8},{4,12},{8,0},{12,4},{16,24},{20,28},{24,16},{28,20},{1,9},{5... | collective-permute-start | bytes 737288 | tf_op jit(solution)/shard_map/ppermute | solution.py:169
  143.2 4.0 %collective-permute-done.27 = bf16[640,128]{1,0:T(8,128)(2,1)S(1)} collective-permute-done((bf16[640,128]{1,0:T(8,128)(2,1)S(1)}, bf16[640,128]{1,0:T(8,128)(2,1)S(1)}, u32[]{:S(2)}, u32[]{:S(2)}) %collective-permute-start.27) | collective-permute-done | bytes 163872 | tf_op jit(solution)/shard_map/ppermute | solution.py:189
  147.2 3.1 %collective-permute-start.32 = (bf16[320,384]{1,0:T(8,128)(2,1)S(1)}, bf16[320,384]{1,0:T(8,128)(2,1)S(1)}, u32[]{:S(2)}, u32[]{:S(2)}) collective-permute-start(bf16[320,384]{1,0:T(8,128)(2,1)S(1)} %fusion.185), channel_id=1, source_target_pairs={{0,8},{4,12},{8,0},{12,4},{16,24},{20,28},{24,16},{28,20},{1,9},{5... | collective-permute-start | bytes 737288 | tf_op jit(solution)/shard_map/ppermute | solution.py:169
  152.6 2.6 collective-permute-start.34
  157.6 4.1 %collective-permute-start.36 = (bf16[320,384]{1,0:T(8,128)(2,1)S(1)}, bf16[320,384]{1,0:T(8,128)(2,1)S(1)}, u32[]{:S(2)}, u32[]{:S(2)}) collective-permute-start(bf16[320,384]{1,0:T(8,128)(2,1)S(1)} %fusion.187), channel_id=1, source_target_pairs={{0,8},{4,12},{8,0},{12,4},{16,24},{20,28},{24,16},{28,20},{1,9},{5... | collective-permute-start | bytes 737288 | tf_op jit(solution)/shard_map/ppermute | solution.py:169
  164.4 4.1 %collective-permute-done.36 = bf16[320,384]{1,0:T(8,128)(2,1)S(1)} collective-permute-done((bf16[320,384]{1,0:T(8,128)(2,1)S(1)}, bf16[320,384]{1,0:T(8,128)(2,1)S(1)}, u32[]{:S(2)}, u32[]{:S(2)}) %collective-permute-start.36) | collective-permute-done | bytes 245792 | tf_op jit(solution)/shard_map/ppermute | solution.py:169
  169.4 4.1 %collective-permute-start.40 = (bf16[320,384]{1,0:T(8,128)(2,1)S(1)}, bf16[320,384]{1,0:T(8,128)(2,1)S(1)}, u32[]{:S(2)}, u32[]{:S(2)}) collective-permute-start(bf16[320,384]{1,0:T(8,128)(2,1)S(1)} %fusion.189), channel_id=1, source_target_pairs={{0,8},{4,12},{8,0},{12,4},{16,24},{20,28},{24,16},{28,20},{1,9},{5... | collective-permute-start | bytes 737288 | tf_op jit(solution)/shard_map/ppermute | solution.py:169
  174.7 3.7 %collective-permute-start.42 = (bf16[320,384]{1,0:T(8,128)(2,1)S(1)}, bf16[320,384]{1,0:T(8,128)(2,1)S(1)}, u32[]{:S(2)}, u32[]{:S(2)}) collective-permute-start(bf16[320,384]{1,0:T(8,128)(2,1)S(1)} %fusion.190), channel_id=1, source_target_pairs={{0,8},{4,12},{8,0},{12,4},{16,24},{20,28},{24,16},{28,20},{1,9},{5... | collective-permute-start | bytes 737288 | tf_op jit(solution)/shard_map/ppermute | solution.py:169
  180.2 3.9 %collective-permute-start.49 = (bf16[320,384]{1,0:T(8,128)(2,1)S(1)}, bf16[320,384]{1,0:T(8,128)(2,1)S(1)}, u32[]{:S(2)}, u32[]{:S(2)}) collective-permute-start(bf16[320,384]{1,0:T(8,128)(2,1)S(1)} %broadcast_select_fusion.43), channel_id=1, source_target_pairs={{0,8},{4,12},{8,0},{12,4},{16,24},{20,28},{24,16},{28,20},{1,9},{5... | collective-permute-start | bytes 737288 | tf_op jit(solution)/shard_map/ppermute | solution.py:169
  186.5 3.8 %collective-permute-start.46 = (bf16[320,384]{1,0:T(8,128)(2,1)S(1)}, bf16[320,384]{1,0:T(8,128)(2,1)S(1)}, u32[]{:S(2)}, u32[]{:S(2)}) collective-permute-start(bf16[320,384]{1,0:T(8,128)(2,1)S(1)} %broadcast_select_fusion.42), channel_id=1, source_target_pairs={{0,8},{4,12},{8,0},{12,4},{16,24},{20,28},{24,16},{28,20},{1,9},{5... | collective-permute-start | bytes 737288 | tf_op jit(solution)/shard_map/ppermute | solution.py:169
  196.8 3.6 %collective-permute-done.45 = bf16[640,128]{1,0:T(8,128)(2,1)S(1)} collective-permute-done((bf16[640,128]{1,0:T(8,128)(2,1)S(1)}, bf16[640,128]{1,0:T(8,128)(2,1)S(1)}, u32[]{:S(2)}, u32[]{:S(2)}) %collective-permute-start.45) | collective-permute-done | bytes 163872 | tf_op jit(solution)/shard_map/ppermute | solution.py:189
  202.6 4.0 %collective-permute-start.55 = (bf16[320,384]{1,0:T(8,128)(2,1)S(1)}, bf16[320,384]{1,0:T(8,128)(2,1)S(1)}, u32[]{:S(2)}, u32[]{:S(2)}) collective-permute-start(bf16[320,384]{1,0:T(8,128)(2,1)S(1)} %broadcast_select_fusion.36), channel_id=1, source_target_pairs={{0,8},{4,12},{8,0},{12,4},{16,24},{20,28},{24,16},{28,20},{1,9},{5... | collective-permute-start | bytes 737288 | tf_op jit(solution)/shard_map/ppermute | solution.py:169
  206.6 2.2 fusion.103
  210.0 2.3 collective-permute-start.53
  213.7 3.1 %collective-permute-start.57 = (bf16[320,384]{1,0:T(8,128)(2,1)S(1)}, bf16[320,384]{1,0:T(8,128)(2,1)S(1)}, u32[]{:S(2)}, u32[]{:S(2)}) collective-permute-start(bf16[320,384]{1,0:T(8,128)(2,1)S(1)} %broadcast_select_fusion.30), channel_id=1, source_target_pairs={{0,8},{4,12},{8,0},{12,4},{16,24},{20,28},{24,16},{28,20},{1,9},{5... | collective-permute-start | bytes 737288 | tf_op jit(solution)/shard_map/ppermute | solution.py:169
  216.9 2.2 fusion.111
  220.3 3.5 %collective-permute-start.61 = (bf16[320,384]{1,0:T(8,128)(2,1)S(1)}, bf16[320,384]{1,0:T(8,128)(2,1)S(1)}, u32[]{:S(2)}, u32[]{:S(2)}) collective-permute-start(bf16[320,384]{1,0:T(8,128)(2,1)S(1)} %broadcast_select_fusion.29), channel_id=1, source_target_pairs={{0,8},{4,12},{8,0},{12,4},{16,24},{20,28},{24,16},{28,20},{1,9},{5... | collective-permute-start | bytes 737288 | tf_op jit(solution)/shard_map/ppermute | solution.py:169
  224.9 4.2 %collective-permute-start.59 = (bf16[320,384]{1,0:T(8,128)(2,1)S(1)}, bf16[320,384]{1,0:T(8,128)(2,1)S(1)}, u32[]{:S(2)}, u32[]{:S(2)}) collective-permute-start(bf16[320,384]{1,0:T(8,128)(2,1)S(1)} %broadcast_select_fusion.28), channel_id=1, source_target_pairs={{0,8},{4,12},{8,0},{12,4},{16,24},{20,28},{24,16},{28,20},{1,9},{5... | collective-permute-start | bytes 737288 | tf_op jit(solution)/shard_map/ppermute | solution.py:169
  229.1 2.2 fusion.119
  232.5 2.4 collective-permute-start.63
  236.1 3.4 %collective-permute-start.67 = (bf16[320,384]{1,0:T(8,128)(2,1)S(1)}, bf16[320,384]{1,0:T(8,128)(2,1)S(1)}, u32[]{:S(2)}, u32[]{:S(2)}) collective-permute-start(bf16[320,384]{1,0:T(8,128)(2,1)S(1)} %broadcast_select_fusion.18), channel_id=1, source_target_pairs={{0,8},{4,12},{8,0},{12,4},{16,24},{20,28},{24,16},{28,20},{1,9},{5... | collective-permute-start | bytes 737288 | tf_op jit(solution)/shard_map/ppermute | solution.py:169
  239.5 2.2 fusion.127
  247.2 4.5 %collective-permute-start.71 = (bf16[320,384]{1,0:T(8,128)(2,1)S(1)}, bf16[320,384]{1,0:T(8,128)(2,1)S(1)}, u32[]{:S(2)}, u32[]{:S(2)}) collective-permute-start(bf16[320,384]{1,0:T(8,128)(2,1)S(1)} %broadcast_select_fusion.16), channel_id=1, source_target_pairs={{0,8},{4,12},{8,0},{12,4},{16,24},{20,28},{24,16},{28,20},{1,9},{5... | collective-permute-start | bytes 737288 | tf_op jit(solution)/shard_map/ppermute | solution.py:169
  258.8 5.8 %collective-permute-start.73 = (bf16[320,384]{1,0:T(8,128)(2,1)S(1)}, bf16[320,384]{1,0:T(8,128)(2,1)S(1)}, u32[]{:S(2)}, u32[]{:S(2)}) collective-permute-start(bf16[320,384]{1,0:T(8,128)(2,1)S(1)} %pad_select_fusion), channel_id=1, source_target_pairs={{0,8},{4,12},{8,0},{12,4},{16,24},{20,28},{24,16},{28,20},{1,9},{5... | collective-permute-start | bytes 737288 | tf_op jit(solution)/shard_map/ppermute | solution.py:169
  267.4 4.1 %collective-permute-done.73 = bf16[320,384]{1,0:T(8,128)(2,1)S(1)} collective-permute-done((bf16[320,384]{1,0:T(8,128)(2,1)S(1)}, bf16[320,384]{1,0:T(8,128)(2,1)S(1)}, u32[]{:S(2)}, u32[]{:S(2)}) %collective-permute-start.73) | collective-permute-done | bytes 245792 | tf_op jit(solution)/shard_map/ppermute | solution.py:169
  280.9 2.9 adam_piece.4
  285.0 2.9 adam_piece.5
  288.0 7.5 %collective-permute-done.78.came_ref = bf16[768,384]{1,0:T(8,128)(2,1)S(1)} collective-permute-done((bf16[768,384]{1,0:T(8,128)(2,1)S(1)}, bf16[768,384]{1,0:T(8,128)(2,1)S(1)}, u32[]{:S(2)}, u32[]{:S(2)}) %collective-permute-start.78) | collective-permute-done | bytes 589856 | tf_op jit(solution)/shard_map/ppermute | solution.py:183
  295.5 2.9 adam_piece.6
  298.4 3.4 %collective-permute-done.77.came_ref = bf16[768,384]{1,0:T(8,128)(2,1)S(1)} collective-permute-done((bf16[768,384]{1,0:T(8,128)(2,1)S(1)}, bf16[768,384]{1,0:T(8,128)(2,1)S(1)}, u32[]{:S(2)}, u32[]{:S(2)}) %collective-permute-start.77) | collective-permute-done | bytes 589856 | tf_op jit(solution)/shard_map/ppermute | solution.py:183
  301.8 2.9 adam_piece.7
  (345 shorter events, 118.6 us)
Async XLA Ops:
  8.9 22.9 %all-to-all-start = ((bf16[32,64,128]{2,1,0:T(8,128)(2,1)}), bf16[32,64,128]{2,1,0:T(8,128)(2,1)S(1)}, u32[]{:S(2)}, u32[]{:S(2)}) async-start(bf16[32,64,128]{2,1,0:T(8,128)(2,1)} %bitcast.4), calls=%async_computation | async-start | bytes 1048576 | tf_op jit(solution)/shard_map/all_to_all | solution.py:74
  16.2 179.7 %collective-permute-start.48 = (bf16[640,128]{1,0:T(8,128)(2,1)}, bf16[640,128]{1,0:T(8,128)(2,1)}, u32[]{:S(2)}, u32[]{:S(2)}) collective-permute-start(bf16[640,128]{1,0:T(8,128)(2,1)} %param.18), channel_id=1, source_target_pairs={{0,8},{4,12},{8,0},{12,4},{16,24},{20,28},{24,16},{28,20},{1,9},{5... | collective-permute-start | bytes 491528 | tf_op jit(solution)/shard_map/ppermute | solution.py:169
  18.0 32.4 %collective-permute-start = (bf16[768,768]{1,0:T(8,128)(2,1)}, bf16[768,768]{1,0:T(8,128)(2,1)}, u32[]{:S(2)}, u32[]{:S(2)}) collective-permute-start(bf16[768,768]{1,0:T(8,128)(2,1)} %get-tuple-element.145), channel_id=1, source_target_pairs={{0,4},{4,0},{8,12},{12,8},{16,20},{20,16},{24,28},{28,24},{1,5},{5... | collective-permute-start | bytes 3538952 | tf_op jit(solution)/shard_map/ppermute | solution.py:183
  50.4 28.4 %collective-permute-start.5 = (bf16[768,768]{1,0:T(8,128)(2,1)}, bf16[768,768]{1,0:T(8,128)(2,1)}, u32[]{:S(2)}, u32[]{:S(2)}) collective-permute-start(bf16[768,768]{1,0:T(8,128)(2,1)} %get-tuple-element.153), channel_id=1, source_target_pairs={{0,4},{4,0},{8,12},{12,8},{16,20},{20,16},{24,28},{28,24},{1,5},{5... | collective-permute-start | bytes 3538952 | tf_op jit(solution)/shard_map/ppermute | solution.py:183
  59.6 13.4 %collective-permute-start.4 = (bf16[320,384]{1,0:T(8,128)(2,1)}, bf16[320,384]{1,0:T(8,128)(2,1)}, u32[]{:S(2)}, u32[]{:S(2)}) collective-permute-start(bf16[320,384]{1,0:T(8,128)(2,1)} %get-tuple-element.302), channel_id=1, source_target_pairs={{0,8},{4,12},{8,0},{12,4},{16,24},{20,28},{24,16},{28,20},{1,9},{5... | collective-permute-start | bytes 737288 | tf_op jit(solution)/shard_map/ppermute | solution.py:169
  66.4 25.5 %collective-permute-start.8 = (bf16[320,384]{1,0:T(8,128)(2,1)}, bf16[320,384]{1,0:T(8,128)(2,1)S(1)}, u32[]{:S(2)}, u32[]{:S(2)}) collective-permute-start(bf16[320,384]{1,0:T(8,128)(2,1)} %get-tuple-element.300), channel_id=1, source_target_pairs={{0,8},{4,12},{8,0},{12,4},{16,24},{20,28},{24,16},{28,20},{1,9},{5... | collective-permute-start | bytes 737288 | tf_op jit(solution)/shard_map/ppermute | solution.py:169
  78.9 13.1 %collective-permute-start.9 = (bf16[320,384]{1,0:T(8,128)(2,1)S(1)}, bf16[320,384]{1,0:T(8,128)(2,1)S(1)}, u32[]{:S(2)}, u32[]{:S(2)}) collective-permute-start(bf16[320,384]{1,0:T(8,128)(2,1)S(1)} %add_convert_fusion.35), channel_id=1, source_target_pairs={{8,16},{12,20},{16,8},{20,12},{9,17},{13,21},{17,9},{21,13},{10,18... | collective-permute-start | bytes 737288 | tf_op jit(solution)/shard_map/ppermute | solution.py:169
  83.6 11.4 %collective-permute-start.7 = (bf16[320,384]{1,0:T(8,128)(2,1)S(1)}, bf16[320,384]{1,0:T(8,128)(2,1)S(1)}, u32[]{:S(2)}, u32[]{:S(2)}) collective-permute-start(bf16[320,384]{1,0:T(8,128)(2,1)S(1)} %add_convert_fusion.33), channel_id=1, source_target_pairs={{8,16},{12,20},{16,8},{20,12},{9,17},{13,21},{17,9},{21,13},{10,18... | collective-permute-start | bytes 737288 | tf_op jit(solution)/shard_map/ppermute | solution.py:169
  84.3 12.7 %collective-permute-start.6 = (bf16[320,384]{1,0:T(8,128)(2,1)S(1)}, bf16[320,384]{1,0:T(8,128)(2,1)S(1)}, u32[]{:S(2)}, u32[]{:S(2)}) collective-permute-start(bf16[320,384]{1,0:T(8,128)(2,1)S(1)} %fusion.175), channel_id=1, source_target_pairs={{0,8},{4,12},{8,0},{12,4},{16,24},{20,28},{24,16},{28,20},{1,9},{5... | collective-permute-start | bytes 737288 | tf_op jit(solution)/shard_map/ppermute | solution.py:169
  92.1 12.3 %collective-permute-start.10 = (bf16[320,384]{1,0:T(8,128)(2,1)S(1)}, bf16[320,384]{1,0:T(8,128)(2,1)S(1)}, u32[]{:S(2)}, u32[]{:S(2)}) collective-permute-start(bf16[320,384]{1,0:T(8,128)(2,1)S(1)} %fusion.176), channel_id=1, source_target_pairs={{0,8},{4,12},{8,0},{12,4},{16,24},{20,28},{24,16},{28,20},{1,9},{5... | collective-permute-start | bytes 737288 | tf_op jit(solution)/shard_map/ppermute | solution.py:169
  92.8 11.6 %collective-permute-start.11 = (bf16[320,384]{1,0:T(8,128)(2,1)S(1)}, bf16[320,384]{1,0:T(8,128)(2,1)S(1)}, u32[]{:S(2)}, u32[]{:S(2)}) collective-permute-start(bf16[320,384]{1,0:T(8,128)(2,1)S(1)} %add_convert_fusion.31), channel_id=1, source_target_pairs={{8,16},{12,20},{16,8},{20,12},{9,17},{13,21},{17,9},{21,13},{10,18... | collective-permute-start | bytes 737288 | tf_op jit(solution)/shard_map/ppermute | solution.py:169
  97.3 11.3 %collective-permute-start.15 = (bf16[320,384]{1,0:T(8,128)(2,1)S(1)}, bf16[320,384]{1,0:T(8,128)(2,1)S(1)}, u32[]{:S(2)}, u32[]{:S(2)}) collective-permute-start(bf16[320,384]{1,0:T(8,128)(2,1)S(1)} %add_convert_fusion.29), channel_id=1, source_target_pairs={{8,16},{12,20},{16,8},{20,12},{9,17},{13,21},{17,9},{21,13},{10,18... | collective-permute-start | bytes 737288 | tf_op jit(solution)/shard_map/ppermute | solution.py:169
  98.0 10.7 %collective-permute-start.14 = (bf16[320,384]{1,0:T(8,128)(2,1)S(1)}, bf16[320,384]{1,0:T(8,128)(2,1)S(1)}, u32[]{:S(2)}, u32[]{:S(2)}) collective-permute-start(bf16[320,384]{1,0:T(8,128)(2,1)S(1)} %fusion.177), channel_id=1, source_target_pairs={{0,8},{4,12},{8,0},{12,4},{16,24},{20,28},{24,16},{28,20},{1,9},{5... | collective-permute-start | bytes 737288 | tf_op jit(solution)/shard_map/ppermute | solution.py:169
  104.5 11.1 %collective-permute-start.17 = (bf16[320,384]{1,0:T(8,128)(2,1)S(1)}, bf16[320,384]{1,0:T(8,128)(2,1)S(1)}, u32[]{:S(2)}, u32[]{:S(2)}) collective-permute-start(bf16[320,384]{1,0:T(8,128)(2,1)S(1)} %add_convert_fusion.27), channel_id=1, source_target_pairs={{8,16},{12,20},{16,8},{20,12},{9,17},{13,21},{17,9},{21,13},{10,18... | collective-permute-start | bytes 737288 | tf_op jit(solution)/shard_map/ppermute | solution.py:169
  115.7 10.7 %collective-permute-start.20 = (bf16[320,384]{1,0:T(8,128)(2,1)S(1)}, bf16[320,384]{1,0:T(8,128)(2,1)S(1)}, u32[]{:S(2)}, u32[]{:S(2)}) collective-permute-start(bf16[320,384]{1,0:T(8,128)(2,1)S(1)} %fusion.180), channel_id=1, source_target_pairs={{0,8},{4,12},{8,0},{12,4},{16,24},{20,28},{24,16},{28,20},{1,9},{5... | collective-permute-start | bytes 737288 | tf_op jit(solution)/shard_map/ppermute | solution.py:169
  119.8 10.7 %collective-permute-start.23 = (bf16[320,384]{1,0:T(8,128)(2,1)S(1)}, bf16[320,384]{1,0:T(8,128)(2,1)S(1)}, u32[]{:S(2)}, u32[]{:S(2)}) collective-permute-start(bf16[320,384]{1,0:T(8,128)(2,1)S(1)} %add_convert_fusion.21), channel_id=1, source_target_pairs={{8,16},{12,20},{16,8},{20,12},{9,17},{13,21},{17,9},{21,13},{10,18... | collective-permute-start | bytes 737288 | tf_op jit(solution)/shard_map/ppermute | solution.py:169
  131.4 11.0 %collective-permute-start.28 = (bf16[320,384]{1,0:T(8,128)(2,1)S(1)}, bf16[320,384]{1,0:T(8,128)(2,1)S(1)}, u32[]{:S(2)}, u32[]{:S(2)}) collective-permute-start(bf16[320,384]{1,0:T(8,128)(2,1)S(1)} %fusion.183), channel_id=1, source_target_pairs={{0,8},{4,12},{8,0},{12,4},{16,24},{20,28},{24,16},{28,20},{1,9},{5... | collective-permute-start | bytes 737288 | tf_op jit(solution)/shard_map/ppermute | solution.py:169
  138.7 13.0 %collective-permute-start.30 = (bf16[320,384]{1,0:T(8,128)(2,1)S(1)}, bf16[320,384]{1,0:T(8,128)(2,1)S(1)}, u32[]{:S(2)}, u32[]{:S(2)}) collective-permute-start(bf16[320,384]{1,0:T(8,128)(2,1)S(1)} %fusion.184), channel_id=1, source_target_pairs={{0,8},{4,12},{8,0},{12,4},{16,24},{20,28},{24,16},{28,20},{1,9},{5... | collective-permute-start | bytes 737288 | tf_op jit(solution)/shard_map/ppermute | solution.py:169
  140.1 11.6 %collective-permute-start.31 = (bf16[320,384]{1,0:T(8,128)(2,1)S(1)}, bf16[320,384]{1,0:T(8,128)(2,1)S(1)}, u32[]{:S(2)}, u32[]{:S(2)}) collective-permute-start(bf16[320,384]{1,0:T(8,128)(2,1)S(1)} %add_convert_fusion.15), channel_id=1, source_target_pairs={{8,16},{12,20},{16,8},{20,12},{9,17},{13,21},{17,9},{21,13},{10,18... | collective-permute-start | bytes 737288 | tf_op jit(solution)/shard_map/ppermute | solution.py:169
  142.4 13.1 %collective-permute-start.33 = (bf16[320,384]{1,0:T(8,128)(2,1)S(1)}, bf16[320,384]{1,0:T(8,128)(2,1)S(1)}, u32[]{:S(2)}, u32[]{:S(2)}) collective-permute-start(bf16[320,384]{1,0:T(8,128)(2,1)S(1)} %add_convert_fusion.13), channel_id=1, source_target_pairs={{8,16},{12,20},{16,8},{20,12},{9,17},{13,21},{17,9},{21,13},{10,18... | collective-permute-start | bytes 737288 | tf_op jit(solution)/shard_map/ppermute | solution.py:169
  157.6 11.0 %collective-permute-start.36 = (bf16[320,384]{1,0:T(8,128)(2,1)S(1)}, bf16[320,384]{1,0:T(8,128)(2,1)S(1)}, u32[]{:S(2)}, u32[]{:S(2)}) collective-permute-start(bf16[320,384]{1,0:T(8,128)(2,1)S(1)} %fusion.187), channel_id=1, source_target_pairs={{0,8},{4,12},{8,0},{12,4},{16,24},{20,28},{24,16},{28,20},{1,9},{5... | collective-permute-start | bytes 737288 | tf_op jit(solution)/shard_map/ppermute | solution.py:169
  162.2 11.6 %collective-permute-start.38 = (bf16[320,384]{1,0:T(8,128)(2,1)S(1)}, bf16[320,384]{1,0:T(8,128)(2,1)S(1)}, u32[]{:S(2)}, u32[]{:S(2)}) collective-permute-start(bf16[320,384]{1,0:T(8,128)(2,1)S(1)} %fusion.188), channel_id=1, source_target_pairs={{0,8},{4,12},{8,0},{12,4},{16,24},{20,28},{24,16},{28,20},{1,9},{5... | collective-permute-start | bytes 737288 | tf_op jit(solution)/shard_map/ppermute | solution.py:169
  168.6 10.8 %collective-permute-start.41 = (bf16[320,384]{1,0:T(8,128)(2,1)S(1)}, bf16[320,384]{1,0:T(8,128)(2,1)S(1)}, u32[]{:S(2)}, u32[]{:S(2)}) collective-permute-start(bf16[320,384]{1,0:T(8,128)(2,1)S(1)} %collective-permute-done.36), channel_id=1, source_target_pairs={{8,16},{12,20},{16,8},{20,12},{9,17},{13,21},{17,9},{21,13},{10,18... | collective-permute-start | bytes 737288 | tf_op jit(solution)/shard_map/ppermute | solution.py:169
  173.9 11.3 %collective-permute-start.43 = (bf16[320,384]{1,0:T(8,128)(2,1)S(1)}, bf16[320,384]{1,0:T(8,128)(2,1)S(1)}, u32[]{:S(2)}, u32[]{:S(2)}) collective-permute-start(bf16[320,384]{1,0:T(8,128)(2,1)S(1)} %collective-permute-done.38), channel_id=1, source_target_pairs={{8,16},{12,20},{16,8},{20,12},{9,17},{13,21},{17,9},{21,13},{10,18... | collective-permute-start | bytes 737288 | tf_op jit(solution)/shard_map/ppermute | solution.py:169
  179.4 13.0 %collective-permute-start.50 = (bf16[320,384]{1,0:T(8,128)(2,1)S(1)}, bf16[320,384]{1,0:T(8,128)(2,1)S(1)}, u32[]{:S(2)}, u32[]{:S(2)}) collective-permute-start(bf16[320,384]{1,0:T(8,128)(2,1)S(1)} %collective-permute-done.40), channel_id=1, source_target_pairs={{8,16},{12,20},{16,8},{20,12},{9,17},{13,21},{17,9},{21,13},{10,18... | collective-permute-start | bytes 737288 | tf_op jit(solution)/shard_map/ppermute | solution.py:169
  180.2 12.2 %collective-permute-start.49 = (bf16[320,384]{1,0:T(8,128)(2,1)S(1)}, bf16[320,384]{1,0:T(8,128)(2,1)S(1)}, u32[]{:S(2)}, u32[]{:S(2)}) collective-permute-start(bf16[320,384]{1,0:T(8,128)(2,1)S(1)} %broadcast_select_fusion.43), channel_id=1, source_target_pairs={{0,8},{4,12},{8,0},{12,4},{16,24},{20,28},{24,16},{28,20},{1,9},{5... | collective-permute-start | bytes 737288 | tf_op jit(solution)/shard_map/ppermute | solution.py:169
  185.2 16.6 %collective-permute-start.47 = (bf16[320,384]{1,0:T(8,128)(2,1)S(1)}, bf16[320,384]{1,0:T(8,128)(2,1)S(1)}, u32[]{:S(2)}, u32[]{:S(2)}) collective-permute-start(bf16[320,384]{1,0:T(8,128)(2,1)S(1)} %collective-permute-done.42), channel_id=1, source_target_pairs={{8,16},{12,20},{16,8},{20,12},{9,17},{13,21},{17,9},{21,13},{10,18... | collective-permute-start | bytes 737288 | tf_op jit(solution)/shard_map/ppermute | solution.py:169
  186.5 15.3 %collective-permute-start.46 = (bf16[320,384]{1,0:T(8,128)(2,1)S(1)}, bf16[320,384]{1,0:T(8,128)(2,1)S(1)}, u32[]{:S(2)}, u32[]{:S(2)}) collective-permute-start(bf16[320,384]{1,0:T(8,128)(2,1)S(1)} %broadcast_select_fusion.42), channel_id=1, source_target_pairs={{0,8},{4,12},{8,0},{12,4},{16,24},{20,28},{24,16},{28,20},{1,9},{5... | collective-permute-start | bytes 737288 | tf_op jit(solution)/shard_map/ppermute | solution.py:169
  192.4 16.8 %collective-permute-start.52 = (bf16[320,384]{1,0:T(8,128)(2,1)S(1)}, bf16[320,384]{1,0:T(8,128)(2,1)S(1)}, u32[]{:S(2)}, u32[]{:S(2)}) collective-permute-start(bf16[320,384]{1,0:T(8,128)(2,1)S(1)} %collective-permute-done.49), channel_id=1, source_target_pairs={{8,16},{12,20},{16,8},{20,12},{9,17},{13,21},{17,9},{21,13},{10,18... | collective-permute-start | bytes 737288 | tf_op jit(solution)/shard_map/ppermute | solution.py:169
  195.9 13.3 %collective-permute-start.51 = (bf16[320,384]{1,0:T(8,128)(2,1)S(1)}, bf16[320,384]{1,0:T(8,128)(2,1)S(1)}, u32[]{:S(2)}, u32[]{:S(2)}) collective-permute-start(bf16[320,384]{1,0:T(8,128)(2,1)S(1)} %broadcast_select_fusion.41), channel_id=1, source_target_pairs={{0,8},{4,12},{8,0},{12,4},{16,24},{20,28},{24,16},{28,20},{1,9},{5... | collective-permute-start | bytes 737288 | tf_op jit(solution)/shard_map/ppermute | solution.py:169
  201.9 10.9 %collective-permute-start.56 = (bf16[320,384]{1,0:T(8,128)(2,1)S(1)}, bf16[320,384]{1,0:T(8,128)(2,1)S(1)}, u32[]{:S(2)}, u32[]{:S(2)}) collective-permute-start(bf16[320,384]{1,0:T(8,128)(2,1)S(1)} %collective-permute-done.46), channel_id=1, source_target_pairs={{8,16},{12,20},{16,8},{20,12},{9,17},{13,21},{17,9},{21,13},{10,18... | collective-permute-start | bytes 737288 | tf_op jit(solution)/shard_map/ppermute | solution.py:169
  212.8 11.3 %collective-permute-start.58 = (bf16[320,384]{1,0:T(8,128)(2,1)S(1)}, bf16[320,384]{1,0:T(8,128)(2,1)S(1)}, u32[]{:S(2)}, u32[]{:S(2)}) collective-permute-start(bf16[320,384]{1,0:T(8,128)(2,1)S(1)} %collective-permute-done.55), channel_id=1, source_target_pairs={{8,16},{12,20},{16,8},{20,12},{9,17},{13,21},{17,9},{21,13},{10,18... | collective-permute-start | bytes 737288 | tf_op jit(solution)/shard_map/ppermute | solution.py:169
  219.6 12.2 %collective-permute-start.62 = (bf16[320,384]{1,0:T(8,128)(2,1)S(1)}, bf16[320,384]{1,0:T(8,128)(2,1)S(1)}, u32[]{:S(2)}, u32[]{:S(2)}) collective-permute-start(bf16[320,384]{1,0:T(8,128)(2,1)S(1)} %collective-permute-done.53), channel_id=1, source_target_pairs={{8,16},{12,20},{16,8},{20,12},{9,17},{13,21},{17,9},{21,13},{10,18... | collective-permute-start | bytes 737288 | tf_op jit(solution)/shard_map/ppermute | solution.py:169
  220.3 11.4 %collective-permute-start.61 = (bf16[320,384]{1,0:T(8,128)(2,1)S(1)}, bf16[320,384]{1,0:T(8,128)(2,1)S(1)}, u32[]{:S(2)}, u32[]{:S(2)}) collective-permute-start(bf16[320,384]{1,0:T(8,128)(2,1)S(1)} %broadcast_select_fusion.29), channel_id=1, source_target_pairs={{0,8},{4,12},{8,0},{12,4},{16,24},{20,28},{24,16},{28,20},{1,9},{5... | collective-permute-start | bytes 737288 | tf_op jit(solution)/shard_map/ppermute | solution.py:169
  224.2 11.1 %collective-permute-start.60 = (bf16[320,384]{1,0:T(8,128)(2,1)S(1)}, bf16[320,384]{1,0:T(8,128)(2,1)S(1)}, u32[]{:S(2)}, u32[]{:S(2)}) collective-permute-start(bf16[320,384]{1,0:T(8,128)(2,1)S(1)} %collective-permute-done.57), channel_id=1, source_target_pairs={{8,16},{12,20},{16,8},{20,12},{9,17},{13,21},{17,9},{21,13},{10,18... | collective-permute-start | bytes 737288 | tf_op jit(solution)/shard_map/ppermute | solution.py:169
  235.4 11.1 %collective-permute-start.68 = (bf16[320,384]{1,0:T(8,128)(2,1)S(1)}, bf16[320,384]{1,0:T(8,128)(2,1)S(1)}, u32[]{:S(2)}, u32[]{:S(2)}) collective-permute-start(bf16[320,384]{1,0:T(8,128)(2,1)S(1)} %collective-permute-done.59), channel_id=1, source_target_pairs={{8,16},{12,20},{16,8},{20,12},{9,17},{13,21},{17,9},{21,13},{10,18... | collective-permute-start | bytes 737288 | tf_op jit(solution)/shard_map/ppermute | solution.py:169
  242.2 13.9 %collective-permute-start.65 = (bf16[320,384]{1,0:T(8,128)(2,1)S(1)}, bf16[320,384]{1,0:T(8,128)(2,1)S(1)}, u32[]{:S(2)}, u32[]{:S(2)}) collective-permute-start(bf16[320,384]{1,0:T(8,128)(2,1)S(1)} %broadcast_select_fusion.17), channel_id=1, source_target_pairs={{0,8},{4,12},{8,0},{12,4},{16,24},{20,28},{24,16},{28,20},{1,9},{5... | collective-permute-start | bytes 737288 | tf_op jit(solution)/shard_map/ppermute | solution.py:169
  243.5 12.6 %collective-permute-start.66 = (bf16[320,384]{1,0:T(8,128)(2,1)S(1)}, bf16[320,384]{1,0:T(8,128)(2,1)S(1)}, u32[]{:S(2)}, u32[]{:S(2)}) collective-permute-start(bf16[320,384]{1,0:T(8,128)(2,1)S(1)} %collective-permute-done.63), channel_id=1, source_target_pairs={{8,16},{12,20},{16,8},{20,12},{9,17},{13,21},{17,9},{21,13},{10,18... | collective-permute-start | bytes 737288 | tf_op jit(solution)/shard_map/ppermute | solution.py:169
  246.5 11.3 %collective-permute-start.72 = (bf16[320,384]{1,0:T(8,128)(2,1)S(1)}, bf16[320,384]{1,0:T(8,128)(2,1)S(1)}, u32[]{:S(2)}, u32[]{:S(2)}) collective-permute-start(bf16[320,384]{1,0:T(8,128)(2,1)S(1)} %collective-permute-done.67), channel_id=1, source_target_pairs={{8,16},{12,20},{16,8},{20,12},{9,17},{13,21},{17,9},{21,13},{10,18... | collective-permute-start | bytes 737288 | tf_op jit(solution)/shard_map/ppermute | solution.py:169
  247.2 10.6 %collective-permute-start.71 = (bf16[320,384]{1,0:T(8,128)(2,1)S(1)}, bf16[320,384]{1,0:T(8,128)(2,1)S(1)}, u32[]{:S(2)}, u32[]{:S(2)}) collective-permute-start(bf16[320,384]{1,0:T(8,128)(2,1)S(1)} %broadcast_select_fusion.16), channel_id=1, source_target_pairs={{0,8},{4,12},{8,0},{12,4},{16,24},{20,28},{24,16},{28,20},{1,9},{5... | collective-permute-start | bytes 737288 | tf_op jit(solution)/shard_map/ppermute | solution.py:169
  253.0 27.8 %collective-permute-start.80 = (bf16[768,384]{1,0:T(8,128)(2,1)S(1)}, bf16[768,384]{1,0:T(8,128)(2,1)S(1)}, u32[]{:S(2)}, u32[]{:S(2)}) collective-permute-start(bf16[768,384]{1,0:T(8,128)(2,1)S(1)} %add_convert_fusion.1), channel_id=1, source_target_pairs={{0,4},{4,0},{8,12},{12,8},{16,20},{20,16},{24,28},{28,24},{1,5},{5... | collective-permute-start | bytes 1769480 | tf_op jit(solution)/shard_map/ppermute | solution.py:183
  256.2 10.9 %collective-permute-start.69 = (bf16[320,384]{1,0:T(8,128)(2,1)S(1)}, bf16[320,384]{1,0:T(8,128)(2,1)S(1)}, u32[]{:S(2)}, u32[]{:S(2)}) collective-permute-start(bf16[320,384]{1,0:T(8,128)(2,1)S(1)} %pad_select_fusion.1), channel_id=1, source_target_pairs={{0,8},{4,12},{8,0},{12,4},{16,24},{20,28},{24,16},{28,20},{1,9},{5... | collective-permute-start | bytes 737288 | tf_op jit(solution)/shard_map/ppermute | solution.py:169
  256.3 11.1 %collective-permute-start.70 = (bf16[320,384]{1,0:T(8,128)(2,1)S(1)}, bf16[320,384]{1,0:T(8,128)(2,1)S(1)}, u32[]{:S(2)}, u32[]{:S(2)}) collective-permute-start(bf16[320,384]{1,0:T(8,128)(2,1)S(1)} %collective-permute-done.65), channel_id=1, source_target_pairs={{8,16},{12,20},{16,8},{20,12},{9,17},{13,21},{17,9},{21,13},{10,18... | collective-permute-start | bytes 737288 | tf_op jit(solution)/shard_map/ppermute | solution.py:169
  257.9 13.6 %collective-permute-start.74 = (bf16[320,384]{1,0:T(8,128)(2,1)S(1)}, bf16[320,384]{1,0:T(8,128)(2,1)S(1)}, u32[]{:S(2)}, u32[]{:S(2)}) collective-permute-start(bf16[320,384]{1,0:T(8,128)(2,1)S(1)} %collective-permute-done.71), channel_id=1, source_target_pairs={{8,16},{12,20},{16,8},{20,12},{9,17},{13,21},{17,9},{21,13},{10,18... | collective-permute-start | bytes 737288 | tf_op jit(solution)/shard_map/ppermute | solution.py:169
  258.8 12.7 %collective-permute-start.73 = (bf16[320,384]{1,0:T(8,128)(2,1)S(1)}, bf16[320,384]{1,0:T(8,128)(2,1)S(1)}, u32[]{:S(2)}, u32[]{:S(2)}) collective-permute-start(bf16[320,384]{1,0:T(8,128)(2,1)S(1)} %pad_select_fusion), channel_id=1, source_target_pairs={{0,8},{4,12},{8,0},{12,4},{16,24},{20,28},{24,16},{28,20},{1,9},{5... | collective-permute-start | bytes 737288 | tf_op jit(solution)/shard_map/ppermute | solution.py:169
  267.1 17.9 %collective-permute-start.79 = (bf16[768,384]{1,0:T(8,128)(2,1)S(1)}, bf16[768,384]{1,0:T(8,128)(2,1)S(1)}, u32[]{:S(2)}, u32[]{:S(2)}) collective-permute-start(bf16[768,384]{1,0:T(8,128)(2,1)S(1)} %add_convert_fusion.2), channel_id=1, source_target_pairs={{0,4},{4,0},{8,12},{12,8},{16,20},{20,16},{24,28},{28,24},{1,5},{5... | collective-permute-start | bytes 1769480 | tf_op jit(solution)/shard_map/ppermute | solution.py:183
  275.8 19.7 %collective-permute-start.78 = (bf16[768,384]{1,0:T(8,128)(2,1)S(1)}, bf16[768,384]{1,0:T(8,128)(2,1)S(1)}, u32[]{:S(2)}, u32[]{:S(2)}) collective-permute-start(bf16[768,384]{1,0:T(8,128)(2,1)S(1)} %add_convert_fusion.3), channel_id=1, source_target_pairs={{0,4},{4,0},{8,12},{12,8},{16,20},{20,16},{24,28},{28,24},{1,5},{5... | collective-permute-start | bytes 1769480 | tf_op jit(solution)/shard_map/ppermute | solution.py:183
  279.1 22.7 %collective-permute-start.77 = (bf16[768,384]{1,0:T(8,128)(2,1)S(1)}, bf16[768,384]{1,0:T(8,128)(2,1)S(1)}, u32[]{:S(2)}, u32[]{:S(2)}) collective-permute-start(bf16[768,384]{1,0:T(8,128)(2,1)S(1)} %add_convert_fusion.4), channel_id=1, source_target_pairs={{0,4},{4,0},{8,12},{12,8},{16,20},{20,16},{24,28},{28,24},{1,5},{5... | collective-permute-start | bytes 1769480 | tf_op jit(solution)/shard_map/ppermute | solution.py:183
  (59 other events, 444.1 us)

commit v6 on v5

--- a/solution.py
+++ b/solution.py
@@ -368,7 +368,7 @@
         elif 1 <= back_tick < units + 1:
             middles[part, tick] = swap_middle(was_end)
 
-        if payload is not None and tick < 99:
+        if payload is not None:
             pending["sent", "last"] = payload
         for work in side_work.get((tick, part), ()):
             if work == "scales":
@@ -397,7 +397,11 @@
 
         unit = back_tick + 1
         if 0 <= unit < units:
-            pending["delta", (part, unit)] = new_delta(part, unit, was_end)
+            these = [part]
+            if unit == (groups - 1) * pieces:
+                these = range(streams) if part == late else []
+            for other in these:
+                pending["delta", (other, unit)] = new_delta(other, unit, was_end)
 
         unit = back_tick - line + 1
         if 0 <= unit < units and part == streams - 1:

time: 309 us -> 306 us (level)
    ppermute x6, waiting for transfers between devices: 9.24 us -> 5.64 us  [mp_sum(): lax.ppermute(value, 'mp', [(m, m ^ step) for m in range(model_count)])]
  transfers between devices with their start and end apart: 82 -> 82, of which waited for: 22 -> 22; matrix products, arithmetic and copies ran while one was open for 25% -> 26% of each run, Pallas kernels for 3% -> 3%
where the time goes in v6:
time: 306 us; the launch traced here: 301 us
  starting transfers between devices  146 us (48%)
  matrix products  55 us (18%)
  waiting for transfers between devices  47.1 us (15%)
  local copies, waits for them, and re-layouts  15.8 us (5%)
  other arithmetic  14.9 us (5%)
  Pallas kernels  11.7 us (4%)
  blocking collectives  7.72 us (3%)
  between operations  3.34 us (1%)
    ppermute x69, starting transfers between devices, swap(): return lax.ppermute(value, 'dp', pairs)  127 us
    dot_general x22, matrix products, dot32(): return jnp.dot(left, right, preferred_element_type=jnp.float32)  30.4 us
    ppermute x69, waiting for transfers between devices, swap(): return lax.ppermute(value, 'dp', pairs)  21.6 us
    dot_general x12, matrix products, gradient_term(): lax.dot_general(features[unit // pieces][:, rows], jnp.concatenate(arrive...  18.7 us
    ppermute x6, waiting for transfers between devices, turn(): return lax.ppermute(value, 'dp', pairs)  12.1 us
    pallas_call x4, Pallas kernels, adam_piece(): pl.pallas_call(adam_kernel, grid=(3,), in_specs=[piece, piece, column, co...  11.7 us
    all_to_all x1, waiting for transfers between devices, route(): lax.all_to_all(outgoing.reshape(devices_all, line * lot, patch_width), ('...  7.78 us
    all_gather x1, blocking collectives, shards(): lax.all_gather(blocks.reshape(line, block_rows, -1), 'mp', axis=1, tiled=...  7.72 us
  transfers between devices with their start and end apart: 82, of which 22 were waited for; matrix products, arithmetic and copies ran while one was open for 26% of the time, Pallas kernels for 3%

profile of v6, /device:TPU:0, one launch (start us, length us, event | category | flops | bytes accessed | tf_op | source)
XLA Modules:
  0.0 301.1 jit_solution(682182596412777969)
XLA Ops:
  1.4 2.6 convert.14
  8.9 7.3 %all-to-all-start = ((bf16[32,64,128]{2,1,0:T(8,128)(2,1)}), bf16[32,64,128]{2,1,0:T(8,128)(2,1)S(1)}, u32[]{:S(2)}, u32[]{:S(2)}) async-start(bf16[32,64,128]{2,1,0:T(8,128)(2,1)} %bitcast.4), calls=%async_computation | async-start | bytes 1048576 | tf_op jit(solution)/shard_map/all_to_all | solution.py:74
  21.6 2.4 constant_dynamic-update-slice_fusion.1
  24.0 7.8 %all-to-all-done = bf16[32,64,128]{2,1,0:T(8,128)(2,1)S(1)} async-done(((bf16[32,64,128]{2,1,0:T(8,128)(2,1)}), bf16[32,64,128]{2,1,0:T(8,128)(2,1)S(1)}, u32[]{:S(2)}, u32[]{:S(2)}) %all-to-all-start) | async-done | bytes 524320 | tf_op jit(solution)/shard_map/all_to_all | solution.py:74
  33.1 7.7 %all_gather.3 = bf16[4,640,128]{2,1,0:T(8,128)(2,1)S(1)} all-gather(bf16[4,160,128]{2,1,0:T(8,128)(2,1)S(1)} %bitcast.75), channel_id=1, replica_groups=mesh['dp'=8,'mp'=4] {'mp'}, dimensions={1}, use_global_device_ids=true | all-gather | bytes 819200 | tf_op jit(solution)/shard_map/all_gather | solution.py:216
  40.9 3.5 %fusion.3 = f32[320]{0:T(512)S(1)} fusion(bf16[128,6144]{1,0:T(8,128)(2,1)S(1)} %copy-done.9, bf16[160,128]{1,0:T(8,128)(2,1)S(1)} %get-tuple-element.349, bf16[160,128]{1,0:T(8,128)(2,1)S(1)} %get-tuple-element.350), kind=kOutput, calls=%fused_computation.6 | convolution fusion | flops 521174720 | bytes 1656064 | tf_op jit(solution)/shard_map/dot_general | solution.py:37
  44.4 2.9 fusion.5
  47.3 2.9 fusion.1
  51.6 3.1 %constant_dynamic-update-slice_fusion.3 = bf16[1536,768]{1,0:T(8,128)(2,1)} fusion(bf16[768,768]{1,0:T(8,128)(2,1)} %get-tuple-element.153), kind=kLoop, calls=%fused_computation.367 | loop fusion | bytes 2359296
  70.4 2.6 collective-permute-done.4
  79.8 2.5 fusion.135
  84.3 7.6 %collective-permute-start.6 = (bf16[320,384]{1,0:T(8,128)(2,1)S(1)}, bf16[320,384]{1,0:T(8,128)(2,1)S(1)}, u32[]{:S(2)}, u32[]{:S(2)}) collective-permute-start(bf16[320,384]{1,0:T(8,128)(2,1)S(1)} %fusion.175), channel_id=1, source_target_pairs={{0,8},{4,12},{8,0},{12,4},{16,24},{20,28},{24,16},{28,20},{1,9},{5... | collective-permute-start | bytes 737288 | tf_op jit(solution)/shard_map/ppermute | solution.py:169
  98.0 4.7 %collective-permute-start.14 = (bf16[320,384]{1,0:T(8,128)(2,1)S(1)}, bf16[320,384]{1,0:T(8,128)(2,1)S(1)}, u32[]{:S(2)}, u32[]{:S(2)}) collective-permute-start(bf16[320,384]{1,0:T(8,128)(2,1)S(1)} %fusion.177), channel_id=1, source_target_pairs={{0,8},{4,12},{8,0},{12,4},{16,24},{20,28},{24,16},{28,20},{1,9},{5... | collective-permute-start | bytes 737288 | tf_op jit(solution)/shard_map/ppermute | solution.py:169
  105.3 3.3 %collective-permute-start.16 = (bf16[320,384]{1,0:T(8,128)(2,1)S(1)}, bf16[320,384]{1,0:T(8,128)(2,1)S(1)}, u32[]{:S(2)}, u32[]{:S(2)}) collective-permute-start(bf16[320,384]{1,0:T(8,128)(2,1)S(1)} %fusion.178), channel_id=1, source_target_pairs={{0,8},{4,12},{8,0},{12,4},{16,24},{20,28},{24,16},{28,20},{1,9},{5... | collective-permute-start | bytes 737288 | tf_op jit(solution)/shard_map/ppermute | solution.py:169
  109.6 4.3 %collective-permute-start.18 = (bf16[320,384]{1,0:T(8,128)(2,1)S(1)}, bf16[320,384]{1,0:T(8,128)(2,1)S(1)}, u32[]{:S(2)}, u32[]{:S(2)}) collective-permute-start(bf16[320,384]{1,0:T(8,128)(2,1)S(1)} %fusion.179), channel_id=1, source_target_pairs={{0,8},{4,12},{8,0},{12,4},{16,24},{20,28},{24,16},{28,20},{1,9},{5... | collective-permute-start | bytes 737288 | tf_op jit(solution)/shard_map/ppermute | solution.py:169
  120.5 4.2 %collective-permute-start.22 = (bf16[320,384]{1,0:T(8,128)(2,1)S(1)}, bf16[320,384]{1,0:T(8,128)(2,1)S(1)}, u32[]{:S(2)}, u32[]{:S(2)}) collective-permute-start(bf16[320,384]{1,0:T(8,128)(2,1)S(1)} %fusion.181), channel_id=1, source_target_pairs={{0,8},{4,12},{8,0},{12,4},{16,24},{20,28},{24,16},{28,20},{1,9},{5... | collective-permute-start | bytes 737288 | tf_op jit(solution)/shard_map/ppermute | solution.py:169
  127.3 3.2 %collective-permute-start.24 = (bf16[320,384]{1,0:T(8,128)(2,1)S(1)}, bf16[320,384]{1,0:T(8,128)(2,1)S(1)}, u32[]{:S(2)}, u32[]{:S(2)}) collective-permute-start(bf16[320,384]{1,0:T(8,128)(2,1)S(1)} %fusion.182), channel_id=1, source_target_pairs={{0,8},{4,12},{8,0},{12,4},{16,24},{20,28},{24,16},{28,20},{1,9},{5... | collective-permute-start | bytes 737288 | tf_op jit(solution)/shard_map/ppermute | solution.py:169
  131.4 4.4 %collective-permute-start.28 = (bf16[320,384]{1,0:T(8,128)(2,1)S(1)}, bf16[320,384]{1,0:T(8,128)(2,1)S(1)}, u32[]{:S(2)}, u32[]{:S(2)}) collective-permute-start(bf16[320,384]{1,0:T(8,128)(2,1)S(1)} %fusion.183), channel_id=1, source_target_pairs={{0,8},{4,12},{8,0},{12,4},{16,24},{20,28},{24,16},{28,20},{1,9},{5... | collective-permute-start | bytes 737288 | tf_op jit(solution)/shard_map/ppermute | solution.py:169
  143.2 4.0 %collective-permute-done.27 = bf16[640,128]{1,0:T(8,128)(2,1)S(1)} collective-permute-done((bf16[640,128]{1,0:T(8,128)(2,1)S(1)}, bf16[640,128]{1,0:T(8,128)(2,1)S(1)}, u32[]{:S(2)}, u32[]{:S(2)}) %collective-permute-start.27) | collective-permute-done | bytes 163872 | tf_op jit(solution)/shard_map/ppermute | solution.py:189
  147.2 3.1 %collective-permute-start.32 = (bf16[320,384]{1,0:T(8,128)(2,1)S(1)}, bf16[320,384]{1,0:T(8,128)(2,1)S(1)}, u32[]{:S(2)}, u32[]{:S(2)}) collective-permute-start(bf16[320,384]{1,0:T(8,128)(2,1)S(1)} %fusion.185), channel_id=1, source_target_pairs={{0,8},{4,12},{8,0},{12,4},{16,24},{20,28},{24,16},{28,20},{1,9},{5... | collective-permute-start | bytes 737288 | tf_op jit(solution)/shard_map/ppermute | solution.py:169
  152.6 2.6 collective-permute-start.34
  157.6 4.1 %collective-permute-start.36 = (bf16[320,384]{1,0:T(8,128)(2,1)S(1)}, bf16[320,384]{1,0:T(8,128)(2,1)S(1)}, u32[]{:S(2)}, u32[]{:S(2)}) collective-permute-start(bf16[320,384]{1,0:T(8,128)(2,1)S(1)} %fusion.187), channel_id=1, source_target_pairs={{0,8},{4,12},{8,0},{12,4},{16,24},{20,28},{24,16},{28,20},{1,9},{5... | collective-permute-start | bytes 737288 | tf_op jit(solution)/shard_map/ppermute | solution.py:169
  164.4 4.1 %collective-permute-done.36 = bf16[320,384]{1,0:T(8,128)(2,1)S(1)} collective-permute-done((bf16[320,384]{1,0:T(8,128)(2,1)S(1)}, bf16[320,384]{1,0:T(8,128)(2,1)S(1)}, u32[]{:S(2)}, u32[]{:S(2)}) %collective-permute-start.36) | collective-permute-done | bytes 245792 | tf_op jit(solution)/shard_map/ppermute | solution.py:169
  169.4 4.1 %collective-permute-start.40 = (bf16[320,384]{1,0:T(8,128)(2,1)S(1)}, bf16[320,384]{1,0:T(8,128)(2,1)S(1)}, u32[]{:S(2)}, u32[]{:S(2)}) collective-permute-start(bf16[320,384]{1,0:T(8,128)(2,1)S(1)} %fusion.189), channel_id=1, source_target_pairs={{0,8},{4,12},{8,0},{12,4},{16,24},{20,28},{24,16},{28,20},{1,9},{5... | collective-permute-start | bytes 737288 | tf_op jit(solution)/shard_map/ppermute | solution.py:169
  174.7 3.7 %collective-permute-start.42 = (bf16[320,384]{1,0:T(8,128)(2,1)S(1)}, bf16[320,384]{1,0:T(8,128)(2,1)S(1)}, u32[]{:S(2)}, u32[]{:S(2)}) collective-permute-start(bf16[320,384]{1,0:T(8,128)(2,1)S(1)} %fusion.190), channel_id=1, source_target_pairs={{0,8},{4,12},{8,0},{12,4},{16,24},{20,28},{24,16},{28,20},{1,9},{5... | collective-permute-start | bytes 737288 | tf_op jit(solution)/shard_map/ppermute | solution.py:169
  180.2 3.9 %collective-permute-start.46 = (bf16[320,384]{1,0:T(8,128)(2,1)S(1)}, bf16[320,384]{1,0:T(8,128)(2,1)S(1)}, u32[]{:S(2)}, u32[]{:S(2)}) collective-permute-start(bf16[320,384]{1,0:T(8,128)(2,1)S(1)} %broadcast_select_fusion.43), channel_id=1, source_target_pairs={{0,8},{4,12},{8,0},{12,4},{16,24},{20,28},{24,16},{28,20},{1,9},{5... | collective-permute-start | bytes 737288 | tf_op jit(solution)/shard_map/ppermute | solution.py:169
  186.5 3.8 %collective-permute-start.51 = (bf16[320,384]{1,0:T(8,128)(2,1)S(1)}, bf16[320,384]{1,0:T(8,128)(2,1)S(1)}, u32[]{:S(2)}, u32[]{:S(2)}) collective-permute-start(bf16[320,384]{1,0:T(8,128)(2,1)S(1)} %broadcast_select_fusion.42), channel_id=1, source_target_pairs={{0,8},{4,12},{8,0},{12,4},{16,24},{20,28},{24,16},{28,20},{1,9},{5... | collective-permute-start | bytes 737288 | tf_op jit(solution)/shard_map/ppermute | solution.py:169
  197.6 2.2 fusion.103
  199.9 3.1 %collective-permute-start.55 = (bf16[320,384]{1,0:T(8,128)(2,1)S(1)}, bf16[320,384]{1,0:T(8,128)(2,1)S(1)}, u32[]{:S(2)}, u32[]{:S(2)}) collective-permute-start(bf16[320,384]{1,0:T(8,128)(2,1)S(1)} %broadcast_select_fusion.36), channel_id=1, source_target_pairs={{0,8},{4,12},{8,0},{12,4},{16,24},{20,28},{24,16},{28,20},{1,9},{5... | collective-permute-start | bytes 737288 | tf_op jit(solution)/shard_map/ppermute | solution.py:169
  205.6 3.1 %collective-permute-start.53 = (bf16[320,384]{1,0:T(8,128)(2,1)S(1)}, bf16[320,384]{1,0:T(8,128)(2,1)S(1)}, u32[]{:S(2)}, u32[]{:S(2)}) collective-permute-start(bf16[320,384]{1,0:T(8,128)(2,1)S(1)} %broadcast_select_fusion.35), channel_id=1, source_target_pairs={{0,8},{4,12},{8,0},{12,4},{16,24},{20,28},{24,16},{28,20},{1,9},{5... | collective-permute-start | bytes 737288 | tf_op jit(solution)/shard_map/ppermute | solution.py:169
  210.4 3.8 %collective-permute-start.57 = (bf16[320,384]{1,0:T(8,128)(2,1)S(1)}, bf16[320,384]{1,0:T(8,128)(2,1)S(1)}, u32[]{:S(2)}, u32[]{:S(2)}) collective-permute-start(bf16[320,384]{1,0:T(8,128)(2,1)S(1)} %broadcast_select_fusion.30), channel_id=1, source_target_pairs={{0,8},{4,12},{8,0},{12,4},{16,24},{20,28},{24,16},{28,20},{1,9},{5... | collective-permute-start | bytes 737288 | tf_op jit(solution)/shard_map/ppermute | solution.py:169
  214.2 2.2 fusion.111
  217.6 2.6 collective-permute-start.61
  221.4 4.0 %collective-permute-start.59 = (bf16[320,384]{1,0:T(8,128)(2,1)S(1)}, bf16[320,384]{1,0:T(8,128)(2,1)S(1)}, u32[]{:S(2)}, u32[]{:S(2)}) collective-permute-start(bf16[320,384]{1,0:T(8,128)(2,1)S(1)} %broadcast_select_fusion.28), channel_id=1, source_target_pairs={{0,8},{4,12},{8,0},{12,4},{16,24},{20,28},{24,16},{28,20},{1,9},{5... | collective-permute-start | bytes 737288 | tf_op jit(solution)/shard_map/ppermute | solution.py:169
  225.4 2.2 fusion.119
  228.8 3.2 %collective-permute-start.63 = (bf16[320,384]{1,0:T(8,128)(2,1)S(1)}, bf16[320,384]{1,0:T(8,128)(2,1)S(1)}, u32[]{:S(2)}, u32[]{:S(2)}) collective-permute-start(bf16[320,384]{1,0:T(8,128)(2,1)S(1)} %broadcast_select_fusion.23), channel_id=1, source_target_pairs={{0,8},{4,12},{8,0},{12,4},{16,24},{20,28},{24,16},{28,20},{1,9},{5... | collective-permute-start | bytes 737288 | tf_op jit(solution)/shard_map/ppermute | solution.py:169
  233.1 4.1 %collective-permute-start.67 = (bf16[320,384]{1,0:T(8,128)(2,1)S(1)}, bf16[320,384]{1,0:T(8,128)(2,1)S(1)}, u32[]{:S(2)}, u32[]{:S(2)}) collective-permute-start(bf16[320,384]{1,0:T(8,128)(2,1)S(1)} %broadcast_select_fusion.18), channel_id=1, source_target_pairs={{0,8},{4,12},{8,0},{12,4},{16,24},{20,28},{24,16},{28,20},{1,9},{5... | collective-permute-start | bytes 737288 | tf_op jit(solution)/shard_map/ppermute | solution.py:169
  237.2 2.2 fusion.127
  241.6 2.4 collective-permute-done.67
  244.8 3.4 %collective-permute-start.71 = (bf16[320,384]{1,0:T(8,128)(2,1)S(1)}, bf16[320,384]{1,0:T(8,128)(2,1)S(1)}, u32[]{:S(2)}, u32[]{:S(2)}) collective-permute-start(bf16[320,384]{1,0:T(8,128)(2,1)S(1)} %broadcast_select_fusion.16), channel_id=1, source_target_pairs={{0,8},{4,12},{8,0},{12,4},{16,24},{20,28},{24,16},{28,20},{1,9},{5... | collective-permute-start | bytes 737288 | tf_op jit(solution)/shard_map/ppermute | solution.py:169
  255.9 4.4 %collective-permute-start.73 = (bf16[320,384]{1,0:T(8,128)(2,1)S(1)}, bf16[320,384]{1,0:T(8,128)(2,1)S(1)}, u32[]{:S(2)}, u32[]{:S(2)}) collective-permute-start(bf16[320,384]{1,0:T(8,128)(2,1)S(1)} %pad_select_fusion), channel_id=1, source_target_pairs={{0,8},{4,12},{8,0},{12,4},{16,24},{20,28},{24,16},{28,20},{1,9},{5... | collective-permute-start | bytes 737288 | tf_op jit(solution)/shard_map/ppermute | solution.py:169
  263.9 3.3 %collective-permute-done.73 = bf16[320,384]{1,0:T(8,128)(2,1)S(1)} collective-permute-done((bf16[320,384]{1,0:T(8,128)(2,1)S(1)}, bf16[320,384]{1,0:T(8,128)(2,1)S(1)}, u32[]{:S(2)}, u32[]{:S(2)}) %collective-permute-start.73) | collective-permute-done | bytes 245792 | tf_op jit(solution)/shard_map/ppermute | solution.py:169
  276.7 2.9 adam_piece.4
  280.8 2.9 adam_piece.5
  283.8 7.8 %collective-permute-done.78.came_ref = bf16[768,384]{1,0:T(8,128)(2,1)S(1)} collective-permute-done((bf16[768,384]{1,0:T(8,128)(2,1)S(1)}, bf16[768,384]{1,0:T(8,128)(2,1)S(1)}, u32[]{:S(2)}, u32[]{:S(2)}) %collective-permute-start.78) | collective-permute-done | bytes 589856 | tf_op jit(solution)/shard_map/ppermute | solution.py:183
  291.6 2.9 adam_piece.6
  294.5 3.4 %collective-permute-done.77.came_ref = bf16[768,384]{1,0:T(8,128)(2,1)S(1)} collective-permute-done((bf16[768,384]{1,0:T(8,128)(2,1)S(1)}, bf16[768,384]{1,0:T(8,128)(2,1)S(1)}, u32[]{:S(2)}, u32[]{:S(2)}) %collective-permute-start.77) | collective-permute-done | bytes 589856 | tf_op jit(solution)/shard_map/ppermute | solution.py:183
  298.0 2.9 adam_piece.7
  (345 shorter events, 118.0 us)
Async XLA Ops:
  8.9 22.9 %all-to-all-start = ((bf16[32,64,128]{2,1,0:T(8,128)(2,1)}), bf16[32,64,128]{2,1,0:T(8,128)(2,1)S(1)}, u32[]{:S(2)}, u32[]{:S(2)}) async-start(bf16[32,64,128]{2,1,0:T(8,128)(2,1)} %bitcast.4), calls=%async_computation | async-start | bytes 1048576 | tf_op jit(solution)/shard_map/all_to_all | solution.py:74
  16.2 183.7 %collective-permute-start.50 = (bf16[640,128]{1,0:T(8,128)(2,1)}, bf16[640,128]{1,0:T(8,128)(2,1)}, u32[]{:S(2)}, u32[]{:S(2)}) collective-permute-start(bf16[640,128]{1,0:T(8,128)(2,1)} %param.18), channel_id=1, source_target_pairs={{0,8},{4,12},{8,0},{12,4},{16,24},{20,28},{24,16},{28,20},{1,9},{5... | collective-permute-start | bytes 491528 | tf_op jit(solution)/shard_map/ppermute | solution.py:169
  18.0 32.4 %collective-permute-start = (bf16[768,768]{1,0:T(8,128)(2,1)}, bf16[768,768]{1,0:T(8,128)(2,1)}, u32[]{:S(2)}, u32[]{:S(2)}) collective-permute-start(bf16[768,768]{1,0:T(8,128)(2,1)} %get-tuple-element.145), channel_id=1, source_target_pairs={{0,4},{4,0},{8,12},{12,8},{16,20},{20,16},{24,28},{28,24},{1,5},{5... | collective-permute-start | bytes 3538952 | tf_op jit(solution)/shard_map/ppermute | solution.py:183
  50.4 28.4 %collective-permute-start.5 = (bf16[768,768]{1,0:T(8,128)(2,1)}, bf16[768,768]{1,0:T(8,128)(2,1)}, u32[]{:S(2)}, u32[]{:S(2)}) collective-permute-start(bf16[768,768]{1,0:T(8,128)(2,1)} %get-tuple-element.153), channel_id=1, source_target_pairs={{0,4},{4,0},{8,12},{12,8},{16,20},{20,16},{24,28},{28,24},{1,5},{5... | collective-permute-start | bytes 3538952 | tf_op jit(solution)/shard_map/ppermute | solution.py:183
  59.6 13.4 %collective-permute-start.4 = (bf16[320,384]{1,0:T(8,128)(2,1)}, bf16[320,384]{1,0:T(8,128)(2,1)}, u32[]{:S(2)}, u32[]{:S(2)}) collective-permute-start(bf16[320,384]{1,0:T(8,128)(2,1)} %get-tuple-element.302), channel_id=1, source_target_pairs={{0,8},{4,12},{8,0},{12,4},{16,24},{20,28},{24,16},{28,20},{1,9},{5... | collective-permute-start | bytes 737288 | tf_op jit(solution)/shard_map/ppermute | solution.py:169
  66.4 25.5 %collective-permute-start.8 = (bf16[320,384]{1,0:T(8,128)(2,1)}, bf16[320,384]{1,0:T(8,128)(2,1)S(1)}, u32[]{:S(2)}, u32[]{:S(2)}) collective-permute-start(bf16[320,384]{1,0:T(8,128)(2,1)} %get-tuple-element.300), channel_id=1, source_target_pairs={{0,8},{4,12},{8,0},{12,4},{16,24},{20,28},{24,16},{28,20},{1,9},{5... | collective-permute-start | bytes 737288 | tf_op jit(solution)/shard_map/ppermute | solution.py:169
  78.9 13.1 %collective-permute-start.9 = (bf16[320,384]{1,0:T(8,128)(2,1)S(1)}, bf16[320,384]{1,0:T(8,128)(2,1)S(1)}, u32[]{:S(2)}, u32[]{:S(2)}) collective-permute-start(bf16[320,384]{1,0:T(8,128)(2,1)S(1)} %add_convert_fusion.35), channel_id=1, source_target_pairs={{8,16},{12,20},{16,8},{20,12},{9,17},{13,21},{17,9},{21,13},{10,18... | collective-permute-start | bytes 737288 | tf_op jit(solution)/shard_map/ppermute | solution.py:169
  83.6 11.4 %collective-permute-start.7 = (bf16[320,384]{1,0:T(8,128)(2,1)S(1)}, bf16[320,384]{1,0:T(8,128)(2,1)S(1)}, u32[]{:S(2)}, u32[]{:S(2)}) collective-permute-start(bf16[320,384]{1,0:T(8,128)(2,1)S(1)} %add_convert_fusion.33), channel_id=1, source_target_pairs={{8,16},{12,20},{16,8},{20,12},{9,17},{13,21},{17,9},{21,13},{10,18... | collective-permute-start | bytes 737288 | tf_op jit(solution)/shard_map/ppermute | solution.py:169
  84.3 12.7 %collective-permute-start.6 = (bf16[320,384]{1,0:T(8,128)(2,1)S(1)}, bf16[320,384]{1,0:T(8,128)(2,1)S(1)}, u32[]{:S(2)}, u32[]{:S(2)}) collective-permute-start(bf16[320,384]{1,0:T(8,128)(2,1)S(1)} %fusion.175), channel_id=1, source_target_pairs={{0,8},{4,12},{8,0},{12,4},{16,24},{20,28},{24,16},{28,20},{1,9},{5... | collective-permute-start | bytes 737288 | tf_op jit(solution)/shard_map/ppermute | solution.py:169
  92.1 12.3 %collective-permute-start.10 = (bf16[320,384]{1,0:T(8,128)(2,1)S(1)}, bf16[320,384]{1,0:T(8,128)(2,1)S(1)}, u32[]{:S(2)}, u32[]{:S(2)}) collective-permute-start(bf16[320,384]{1,0:T(8,128)(2,1)S(1)} %fusion.176), channel_id=1, source_target_pairs={{0,8},{4,12},{8,0},{12,4},{16,24},{20,28},{24,16},{28,20},{1,9},{5... | collective-permute-start | bytes 737288 | tf_op jit(solution)/shard_map/ppermute | solution.py:169
  92.8 11.6 %collective-permute-start.11 = (bf16[320,384]{1,0:T(8,128)(2,1)S(1)}, bf16[320,384]{1,0:T(8,128)(2,1)S(1)}, u32[]{:S(2)}, u32[]{:S(2)}) collective-permute-start(bf16[320,384]{1,0:T(8,128)(2,1)S(1)} %add_convert_fusion.31), channel_id=1, source_target_pairs={{8,16},{12,20},{16,8},{20,12},{9,17},{13,21},{17,9},{21,13},{10,18... | collective-permute-start | bytes 737288 | tf_op jit(solution)/shard_map/ppermute | solution.py:169
  97.3 11.3 %collective-permute-start.15 = (bf16[320,384]{1,0:T(8,128)(2,1)S(1)}, bf16[320,384]{1,0:T(8,128)(2,1)S(1)}, u32[]{:S(2)}, u32[]{:S(2)}) collective-permute-start(bf16[320,384]{1,0:T(8,128)(2,1)S(1)} %add_convert_fusion.29), channel_id=1, source_target_pairs={{8,16},{12,20},{16,8},{20,12},{9,17},{13,21},{17,9},{21,13},{10,18... | collective-permute-start | bytes 737288 | tf_op jit(solution)/shard_map/ppermute | solution.py:169
  104.5 11.1 %collective-permute-start.17 = (bf16[320,384]{1,0:T(8,128)(2,1)S(1)}, bf16[320,384]{1,0:T(8,128)(2,1)S(1)}, u32[]{:S(2)}, u32[]{:S(2)}) collective-permute-start(bf16[320,384]{1,0:T(8,128)(2,1)S(1)} %add_convert_fusion.27), channel_id=1, source_target_pairs={{8,16},{12,20},{16,8},{20,12},{9,17},{13,21},{17,9},{21,13},{10,18... | collective-permute-start | bytes 737288 | tf_op jit(solution)/shard_map/ppermute | solution.py:169
  131.4 11.0 %collective-permute-start.28 = (bf16[320,384]{1,0:T(8,128)(2,1)S(1)}, bf16[320,384]{1,0:T(8,128)(2,1)S(1)}, u32[]{:S(2)}, u32[]{:S(2)}) collective-permute-start(bf16[320,384]{1,0:T(8,128)(2,1)S(1)} %fusion.183), channel_id=1, source_target_pairs={{0,8},{4,12},{8,0},{12,4},{16,24},{20,28},{24,16},{28,20},{1,9},{5... | collective-permute-start | bytes 737288 | tf_op jit(solution)/shard_map/ppermute | solution.py:169
  138.7 13.0 %collective-permute-start.30 = (bf16[320,384]{1,0:T(8,128)(2,1)S(1)}, bf16[320,384]{1,0:T(8,128)(2,1)S(1)}, u32[]{:S(2)}, u32[]{:S(2)}) collective-permute-start(bf16[320,384]{1,0:T(8,128)(2,1)S(1)} %fusion.184), channel_id=1, source_target_pairs={{0,8},{4,12},{8,0},{12,4},{16,24},{20,28},{24,16},{28,20},{1,9},{5... | collective-permute-start | bytes 737288 | tf_op jit(solution)/shard_map/ppermute | solution.py:169
  140.1 11.6 %collective-permute-start.31 = (bf16[320,384]{1,0:T(8,128)(2,1)S(1)}, bf16[320,384]{1,0:T(8,128)(2,1)S(1)}, u32[]{:S(2)}, u32[]{:S(2)}) collective-permute-start(bf16[320,384]{1,0:T(8,128)(2,1)S(1)} %add_convert_fusion.15), channel_id=1, source_target_pairs={{8,16},{12,20},{16,8},{20,12},{9,17},{13,21},{17,9},{21,13},{10,18... | collective-permute-start | bytes 737288 | tf_op jit(solution)/shard_map/ppermute | solution.py:169
  142.4 13.1 %collective-permute-start.33 = (bf16[320,384]{1,0:T(8,128)(2,1)S(1)}, bf16[320,384]{1,0:T(8,128)(2,1)S(1)}, u32[]{:S(2)}, u32[]{:S(2)}) collective-permute-start(bf16[320,384]{1,0:T(8,128)(2,1)S(1)} %add_convert_fusion.13), channel_id=1, source_target_pairs={{8,16},{12,20},{16,8},{20,12},{9,17},{13,21},{17,9},{21,13},{10,18... | collective-permute-start | bytes 737288 | tf_op jit(solution)/shard_map/ppermute | solution.py:169
  157.6 11.0 %collective-permute-start.36 = (bf16[320,384]{1,0:T(8,128)(2,1)S(1)}, bf16[320,384]{1,0:T(8,128)(2,1)S(1)}, u32[]{:S(2)}, u32[]{:S(2)}) collective-permute-start(bf16[320,384]{1,0:T(8,128)(2,1)S(1)} %fusion.187), channel_id=1, source_target_pairs={{0,8},{4,12},{8,0},{12,4},{16,24},{20,28},{24,16},{28,20},{1,9},{5... | collective-permute-start | bytes 737288 | tf_op jit(solution)/shard_map/ppermute | solution.py:169
  162.2 11.6 %collective-permute-start.38 = (bf16[320,384]{1,0:T(8,128)(2,1)S(1)}, bf16[320,384]{1,0:T(8,128)(2,1)S(1)}, u32[]{:S(2)}, u32[]{:S(2)}) collective-permute-start(bf16[320,384]{1,0:T(8,128)(2,1)S(1)} %fusion.188), channel_id=1, source_target_pairs={{0,8},{4,12},{8,0},{12,4},{16,24},{20,28},{24,16},{28,20},{1,9},{5... | collective-permute-start | bytes 737288 | tf_op jit(solution)/shard_map/ppermute | solution.py:169
  168.6 10.8 %collective-permute-start.41 = (bf16[320,384]{1,0:T(8,128)(2,1)S(1)}, bf16[320,384]{1,0:T(8,128)(2,1)S(1)}, u32[]{:S(2)}, u32[]{:S(2)}) collective-permute-start(bf16[320,384]{1,0:T(8,128)(2,1)S(1)} %collective-permute-done.36), channel_id=1, source_target_pairs={{8,16},{12,20},{16,8},{20,12},{9,17},{13,21},{17,9},{21,13},{10,18... | collective-permute-start | bytes 737288 | tf_op jit(solution)/shard_map/ppermute | solution.py:169
  173.9 11.3 %collective-permute-start.43 = (bf16[320,384]{1,0:T(8,128)(2,1)S(1)}, bf16[320,384]{1,0:T(8,128)(2,1)S(1)}, u32[]{:S(2)}, u32[]{:S(2)}) collective-permute-start(bf16[320,384]{1,0:T(8,128)(2,1)S(1)} %collective-permute-done.38), channel_id=1, source_target_pairs={{8,16},{12,20},{16,8},{20,12},{9,17},{13,21},{17,9},{21,13},{10,18... | collective-permute-start | bytes 737288 | tf_op jit(solution)/shard_map/ppermute | solution.py:169
  179.4 13.0 %collective-permute-start.47 = (bf16[320,384]{1,0:T(8,128)(2,1)S(1)}, bf16[320,384]{1,0:T(8,128)(2,1)S(1)}, u32[]{:S(2)}, u32[]{:S(2)}) collective-permute-start(bf16[320,384]{1,0:T(8,128)(2,1)S(1)} %collective-permute-done.40), channel_id=1, source_target_pairs={{8,16},{12,20},{16,8},{20,12},{9,17},{13,21},{17,9},{21,13},{10,18... | collective-permute-start | bytes 737288 | tf_op jit(solution)/shard_map/ppermute | solution.py:169
  180.2 12.2 %collective-permute-start.46 = (bf16[320,384]{1,0:T(8,128)(2,1)S(1)}, bf16[320,384]{1,0:T(8,128)(2,1)S(1)}, u32[]{:S(2)}, u32[]{:S(2)}) collective-permute-start(bf16[320,384]{1,0:T(8,128)(2,1)S(1)} %broadcast_select_fusion.43), channel_id=1, source_target_pairs={{0,8},{4,12},{8,0},{12,4},{16,24},{20,28},{24,16},{28,20},{1,9},{5... | collective-permute-start | bytes 737288 | tf_op jit(solution)/shard_map/ppermute | solution.py:169
  185.2 11.6 %collective-permute-start.52 = (bf16[320,384]{1,0:T(8,128)(2,1)S(1)}, bf16[320,384]{1,0:T(8,128)(2,1)S(1)}, u32[]{:S(2)}, u32[]{:S(2)}) collective-permute-start(bf16[320,384]{1,0:T(8,128)(2,1)S(1)} %collective-permute-done.42), channel_id=1, source_target_pairs={{8,16},{12,20},{16,8},{20,12},{9,17},{13,21},{17,9},{21,13},{10,18... | collective-permute-start | bytes 737288 | tf_op jit(solution)/shard_map/ppermute | solution.py:169
  192.5 12.3 %collective-permute-start.49 = (bf16[320,384]{1,0:T(8,128)(2,1)S(1)}, bf16[320,384]{1,0:T(8,128)(2,1)S(1)}, u32[]{:S(2)}, u32[]{:S(2)}) collective-permute-start(bf16[320,384]{1,0:T(8,128)(2,1)S(1)} %collective-permute-done.46), channel_id=1, source_target_pairs={{8,16},{12,20},{16,8},{20,12},{9,17},{13,21},{17,9},{21,13},{10,18... | collective-permute-start | bytes 737288 | tf_op jit(solution)/shard_map/ppermute | solution.py:169
  193.8 11.0 %collective-permute-start.48 = (bf16[320,384]{1,0:T(8,128)(2,1)S(1)}, bf16[320,384]{1,0:T(8,128)(2,1)S(1)}, u32[]{:S(2)}, u32[]{:S(2)}) collective-permute-start(bf16[320,384]{1,0:T(8,128)(2,1)S(1)} %broadcast_select_fusion.41), channel_id=1, source_target_pairs={{0,8},{4,12},{8,0},{12,4},{16,24},{20,28},{24,16},{28,20},{1,9},{5... | collective-permute-start | bytes 737288 | tf_op jit(solution)/shard_map/ppermute | solution.py:169
  196.9 12.5 %collective-permute-start.56 = (bf16[320,384]{1,0:T(8,128)(2,1)S(1)}, bf16[320,384]{1,0:T(8,128)(2,1)S(1)}, u32[]{:S(2)}, u32[]{:S(2)}) collective-permute-start(bf16[320,384]{1,0:T(8,128)(2,1)S(1)} %collective-permute-done.51), channel_id=1, source_target_pairs={{8,16},{12,20},{16,8},{20,12},{9,17},{13,21},{17,9},{21,13},{10,18... | collective-permute-start | bytes 737288 | tf_op jit(solution)/shard_map/ppermute | solution.py:169
  204.9 11.9 %collective-permute-start.54 = (bf16[320,384]{1,0:T(8,128)(2,1)S(1)}, bf16[320,384]{1,0:T(8,128)(2,1)S(1)}, u32[]{:S(2)}, u32[]{:S(2)}) collective-permute-start(bf16[320,384]{1,0:T(8,128)(2,1)S(1)} %collective-permute-done.48), channel_id=1, source_target_pairs={{8,16},{12,20},{16,8},{20,12},{9,17},{13,21},{17,9},{21,13},{10,18... | collective-permute-start | bytes 737288 | tf_op jit(solution)/shard_map/ppermute | solution.py:169
  205.6 11.2 %collective-permute-start.53 = (bf16[320,384]{1,0:T(8,128)(2,1)S(1)}, bf16[320,384]{1,0:T(8,128)(2,1)S(1)}, u32[]{:S(2)}, u32[]{:S(2)}) collective-permute-start(bf16[320,384]{1,0:T(8,128)(2,1)S(1)} %broadcast_select_fusion.35), channel_id=1, source_target_pairs={{0,8},{4,12},{8,0},{12,4},{16,24},{20,28},{24,16},{28,20},{1,9},{5... | collective-permute-start | bytes 737288 | tf_op jit(solution)/shard_map/ppermute | solution.py:169
  209.5 11.1 %collective-permute-start.58 = (bf16[320,384]{1,0:T(8,128)(2,1)S(1)}, bf16[320,384]{1,0:T(8,128)(2,1)S(1)}, u32[]{:S(2)}, u32[]{:S(2)}) collective-permute-start(bf16[320,384]{1,0:T(8,128)(2,1)S(1)} %collective-permute-done.55), channel_id=1, source_target_pairs={{8,16},{12,20},{16,8},{20,12},{9,17},{13,21},{17,9},{21,13},{10,18... | collective-permute-start | bytes 737288 | tf_op jit(solution)/shard_map/ppermute | solution.py:169
  216.9 11.1 %collective-permute-start.62 = (bf16[320,384]{1,0:T(8,128)(2,1)S(1)}, bf16[320,384]{1,0:T(8,128)(2,1)S(1)}, u32[]{:S(2)}, u32[]{:S(2)}) collective-permute-start(bf16[320,384]{1,0:T(8,128)(2,1)S(1)} %collective-permute-done.53), channel_id=1, source_target_pairs={{8,16},{12,20},{16,8},{20,12},{9,17},{13,21},{17,9},{21,13},{10,18... | collective-permute-start | bytes 737288 | tf_op jit(solution)/shard_map/ppermute | solution.py:169
  220.6 11.7 %collective-permute-start.60 = (bf16[320,384]{1,0:T(8,128)(2,1)S(1)}, bf16[320,384]{1,0:T(8,128)(2,1)S(1)}, u32[]{:S(2)}, u32[]{:S(2)}) collective-permute-start(bf16[320,384]{1,0:T(8,128)(2,1)S(1)} %collective-permute-done.57), channel_id=1, source_target_pairs={{8,16},{12,20},{16,8},{20,12},{9,17},{13,21},{17,9},{21,13},{10,18... | collective-permute-start | bytes 737288 | tf_op jit(solution)/shard_map/ppermute | solution.py:169
  221.4 11.0 %collective-permute-start.59 = (bf16[320,384]{1,0:T(8,128)(2,1)S(1)}, bf16[320,384]{1,0:T(8,128)(2,1)S(1)}, u32[]{:S(2)}, u32[]{:S(2)}) collective-permute-start(bf16[320,384]{1,0:T(8,128)(2,1)S(1)} %broadcast_select_fusion.28), channel_id=1, source_target_pairs={{0,8},{4,12},{8,0},{12,4},{16,24},{20,28},{24,16},{28,20},{1,9},{5... | collective-permute-start | bytes 737288 | tf_op jit(solution)/shard_map/ppermute | solution.py:169
  228.1 11.8 %collective-permute-start.64 = (bf16[320,384]{1,0:T(8,128)(2,1)S(1)}, bf16[320,384]{1,0:T(8,128)(2,1)S(1)}, u32[]{:S(2)}, u32[]{:S(2)}) collective-permute-start(bf16[320,384]{1,0:T(8,128)(2,1)S(1)} %collective-permute-done.61), channel_id=1, source_target_pairs={{8,16},{12,20},{16,8},{20,12},{9,17},{13,21},{17,9},{21,13},{10,18... | collective-permute-start | bytes 737288 | tf_op jit(solution)/shard_map/ppermute | solution.py:169
  228.8 11.0 %collective-permute-start.63 = (bf16[320,384]{1,0:T(8,128)(2,1)S(1)}, bf16[320,384]{1,0:T(8,128)(2,1)S(1)}, u32[]{:S(2)}, u32[]{:S(2)}) collective-permute-start(bf16[320,384]{1,0:T(8,128)(2,1)S(1)} %broadcast_select_fusion.23), channel_id=1, source_target_pairs={{0,8},{4,12},{8,0},{12,4},{16,24},{20,28},{24,16},{28,20},{1,9},{5... | collective-permute-start | bytes 737288 | tf_op jit(solution)/shard_map/ppermute | solution.py:169
  232.4 11.6 %collective-permute-start.68 = (bf16[320,384]{1,0:T(8,128)(2,1)S(1)}, bf16[320,384]{1,0:T(8,128)(2,1)S(1)}, u32[]{:S(2)}, u32[]{:S(2)}) collective-permute-start(bf16[320,384]{1,0:T(8,128)(2,1)S(1)} %collective-permute-done.59), channel_id=1, source_target_pairs={{8,16},{12,20},{16,8},{20,12},{9,17},{13,21},{17,9},{21,13},{10,18... | collective-permute-start | bytes 737288 | tf_op jit(solution)/shard_map/ppermute | solution.py:169
  233.1 10.9 %collective-permute-start.67 = (bf16[320,384]{1,0:T(8,128)(2,1)S(1)}, bf16[320,384]{1,0:T(8,128)(2,1)S(1)}, u32[]{:S(2)}, u32[]{:S(2)}) collective-permute-start(bf16[320,384]{1,0:T(8,128)(2,1)S(1)} %broadcast_select_fusion.18), channel_id=1, source_target_pairs={{0,8},{4,12},{8,0},{12,4},{16,24},{20,28},{24,16},{28,20},{1,9},{5... | collective-permute-start | bytes 737288 | tf_op jit(solution)/shard_map/ppermute | solution.py:169
  239.9 11.8 %collective-permute-start.65 = (bf16[320,384]{1,0:T(8,128)(2,1)S(1)}, bf16[320,384]{1,0:T(8,128)(2,1)S(1)}, u32[]{:S(2)}, u32[]{:S(2)}) collective-permute-start(bf16[320,384]{1,0:T(8,128)(2,1)S(1)} %broadcast_select_fusion.17), channel_id=1, source_target_pairs={{0,8},{4,12},{8,0},{12,4},{16,24},{20,28},{24,16},{28,20},{1,9},{5... | collective-permute-start | bytes 737288 | tf_op jit(solution)/shard_map/ppermute | solution.py:169
  240.9 10.9 %collective-permute-start.66 = (bf16[320,384]{1,0:T(8,128)(2,1)S(1)}, bf16[320,384]{1,0:T(8,128)(2,1)S(1)}, u32[]{:S(2)}, u32[]{:S(2)}) collective-permute-start(bf16[320,384]{1,0:T(8,128)(2,1)S(1)} %collective-permute-done.63), channel_id=1, source_target_pairs={{8,16},{12,20},{16,8},{20,12},{9,17},{13,21},{17,9},{21,13},{10,18... | collective-permute-start | bytes 737288 | tf_op jit(solution)/shard_map/ppermute | solution.py:169
  244.1 10.8 %collective-permute-start.72 = (bf16[320,384]{1,0:T(8,128)(2,1)S(1)}, bf16[320,384]{1,0:T(8,128)(2,1)S(1)}, u32[]{:S(2)}, u32[]{:S(2)}) collective-permute-start(bf16[320,384]{1,0:T(8,128)(2,1)S(1)} %collective-permute-done.67), channel_id=1, source_target_pairs={{8,16},{12,20},{16,8},{20,12},{9,17},{13,21},{17,9},{21,13},{10,18... | collective-permute-start | bytes 737288 | tf_op jit(solution)/shard_map/ppermute | solution.py:169
  249.4 27.2 %collective-permute-start.80 = (bf16[768,384]{1,0:T(8,128)(2,1)S(1)}, bf16[768,384]{1,0:T(8,128)(2,1)S(1)}, u32[]{:S(2)}, u32[]{:S(2)}) collective-permute-start(bf16[768,384]{1,0:T(8,128)(2,1)S(1)} %add_convert_fusion.1), channel_id=1, source_target_pairs={{0,4},{4,0},{8,12},{12,8},{16,20},{20,16},{24,28},{28,24},{1,5},{5... | collective-permute-start | bytes 1769480 | tf_op jit(solution)/shard_map/ppermute | solution.py:183
  251.8 10.9 %collective-permute-start.69 = (bf16[320,384]{1,0:T(8,128)(2,1)S(1)}, bf16[320,384]{1,0:T(8,128)(2,1)S(1)}, u32[]{:S(2)}, u32[]{:S(2)}) collective-permute-start(bf16[320,384]{1,0:T(8,128)(2,1)S(1)} %pad_select_fusion.1), channel_id=1, source_target_pairs={{0,8},{4,12},{8,0},{12,4},{16,24},{20,28},{24,16},{28,20},{1,9},{5... | collective-permute-start | bytes 737288 | tf_op jit(solution)/shard_map/ppermute | solution.py:169
  251.9 11.9 %collective-permute-start.70 = (bf16[320,384]{1,0:T(8,128)(2,1)S(1)}, bf16[320,384]{1,0:T(8,128)(2,1)S(1)}, u32[]{:S(2)}, u32[]{:S(2)}) collective-permute-start(bf16[320,384]{1,0:T(8,128)(2,1)S(1)} %collective-permute-done.65), channel_id=1, source_target_pairs={{8,16},{12,20},{16,8},{20,12},{9,17},{13,21},{17,9},{21,13},{10,18... | collective-permute-start | bytes 737288 | tf_op jit(solution)/shard_map/ppermute | solution.py:169
  254.9 12.2 %collective-permute-start.74 = (bf16[320,384]{1,0:T(8,128)(2,1)S(1)}, bf16[320,384]{1,0:T(8,128)(2,1)S(1)}, u32[]{:S(2)}, u32[]{:S(2)}) collective-permute-start(bf16[320,384]{1,0:T(8,128)(2,1)S(1)} %collective-permute-done.71), channel_id=1, source_target_pairs={{8,16},{12,20},{16,8},{20,12},{9,17},{13,21},{17,9},{21,13},{10,18... | collective-permute-start | bytes 737288 | tf_op jit(solution)/shard_map/ppermute | solution.py:169
  255.9 11.2 %collective-permute-start.73 = (bf16[320,384]{1,0:T(8,128)(2,1)S(1)}, bf16[320,384]{1,0:T(8,128)(2,1)S(1)}, u32[]{:S(2)}, u32[]{:S(2)}) collective-permute-start(bf16[320,384]{1,0:T(8,128)(2,1)S(1)} %pad_select_fusion), channel_id=1, source_target_pairs={{0,8},{4,12},{8,0},{12,4},{16,24},{20,28},{24,16},{28,20},{1,9},{5... | collective-permute-start | bytes 737288 | tf_op jit(solution)/shard_map/ppermute | solution.py:169
  262.7 18.1 %collective-permute-start.79 = (bf16[768,384]{1,0:T(8,128)(2,1)S(1)}, bf16[768,384]{1,0:T(8,128)(2,1)S(1)}, u32[]{:S(2)}, u32[]{:S(2)}) collective-permute-start(bf16[768,384]{1,0:T(8,128)(2,1)S(1)} %add_convert_fusion.2), channel_id=1, source_target_pairs={{0,4},{4,0},{8,12},{12,8},{16,20},{20,16},{24,28},{28,24},{1,5},{5... | collective-permute-start | bytes 1769480 | tf_op jit(solution)/shard_map/ppermute | solution.py:183
  271.8 19.8 %collective-permute-start.78 = (bf16[768,384]{1,0:T(8,128)(2,1)S(1)}, bf16[768,384]{1,0:T(8,128)(2,1)S(1)}, u32[]{:S(2)}, u32[]{:S(2)}) collective-permute-start(bf16[768,384]{1,0:T(8,128)(2,1)S(1)} %add_convert_fusion.3), channel_id=1, source_target_pairs={{0,4},{4,0},{8,12},{12,8},{16,20},{20,16},{24,28},{28,24},{1,5},{5... | collective-permute-start | bytes 1769480 | tf_op jit(solution)/shard_map/ppermute | solution.py:183
  274.8 23.2 %collective-permute-start.77 = (bf16[768,384]{1,0:T(8,128)(2,1)S(1)}, bf16[768,384]{1,0:T(8,128)(2,1)S(1)}, u32[]{:S(2)}, u32[]{:S(2)}) collective-permute-start(bf16[768,384]{1,0:T(8,128)(2,1)S(1)} %add_convert_fusion.4), channel_id=1, source_target_pairs={{0,4},{4,0},{8,12},{12,8},{16,20},{20,16},{24,28},{28,24},{1,5},{5... | collective-permute-start | bytes 1769480 | tf_op jit(solution)/shard_map/ppermute | solution.py:183
  (59 other events, 446.3 us)
